TPU v7x, 32 devices: a whole 2x2x4 slice. The times are simulated.
32 devices in a mesh: groups: 2 (over y), gz: 4 (over z), dev: 2 (over x), xy: 2 (over core).
Axes of the slice: x: 2, y: 2, z: 4, core: 2. Of those that a mesh axis runs over, the one named last changes fastest.
Arguments:
- fields: float32 [12, 8, 64, 256], P('groups', 'dev', 'gz', 'xy'), parts along dimension 0, may hold values from -6 to 6
- spectra: float32 [24, 8, 64, 256], P('groups', 'dev', 'gz', 'xy'), parts along dimension 0, may hold values from -6 to 6
- permittivity: float32 [16, 64, 256], P(('groups', 'dev'), 'gz', 'xy'), parts along dimension 0, may hold values from 1 to 12
- phase_start: float32 [2], P('groups'), parts along dimension 0, may hold values from -3.140625 to 3.140625
- wall_owner: int32 [4, 4], P('gz'), may hold values from 0 to 3, as said below
- cap_owner: int32 [2, 32], replicated, may hold values from 0 to 3, as said below
- dir_index: int32 [2048], replicated, may hold values from 0 to 4095
- target: float32 [4096], P('groups'), parts along dimension 0, may hold values from 1 to 12
- aim_mask: int32 [4096], P('groups'), parts along dimension 0, may hold values 0 or 1
Outputs:
- fields_out: float32 [12, 8, 64, 256], P('groups', 'dev', 'gz', 'xy'), parts along dimension 0
- spectra_out: float32 [24, 8, 64, 256], P('groups', 'dev', 'gz', 'xy'), parts along dimension 0
- owned_currents: float32 [8, 2, 2, 20, 128], P(('groups', 'gz'), 'dev', 'xy'), parts along dimension 0
- intensity: float32 [4096], P(('groups', 'gz', 'dev', 'xy')), parts along dimension 0
- adjoint_currents: float32 [8, 2, 2, 36, 128], P(('groups', 'gz'), 'dev', 'xy'), parts along dimension 0
There are 2 independent parts, one for each index of `groups`. A program takes and returns all parts, laid end to end along the dimension named above; an argument that names none is the same for every part. Nothing has to cross between parts.
Inputs may be any that keep to these rules, and one draw needn't show every extreme that they name: `wall_owner`: entry [s, j] names the index of gz that owns wall patch j of slab s; every index owns exactly 4 wall patches of a column, and a slab gives one index at most 1 of them. `cap_owner`: row 0 names the owner on gz of each patch of the lower cap, row 1 of the upper cap; each index owns exactly 8 patches of each cap, so that every index owns exactly 20 patches of a column.
All inputs are finite; a program needn't handle non-finite values.
Results may differ from a plain program's by a relative error of at most 0.0003.
Values sent between devices are 32-bit elements; how exact they have to be, the bound alone decides.
No kernel may reach another device: no remote copies, remote signals or barrier semaphores. Data moves between devices by JAX's collectives and lax.ppermute only.
A program may use at most 64 MiB of HBM per device.

v0:
```python
import math

import jax
import jax.numpy as jnp
from jax import lax
from jax.sharding import PartitionSpec as P

PATCH = 16
XB = 8
ZB = 4
STEPS = 3
THETAS = 64


COURANT = 0.5
ANGULAR_STEP = 0.3
WAVE_NUMBER = 0.6
HIGHEST = lax.Precision.HIGHEST
CURRENT_SIGNS = (-1.0, 1.0, 1.0, -1.0)
X_PICKS = (5, 4, 2, 1)
Z_PICKS = (4, 3, 1, 0)


def padded_2(shard, sides, width):
    for axis, dim in sides:
        peers, length = (lax.axis_size(axis), shard.shape[dim])
        up = [(i, (i + 1) % peers) for i in range(peers - 1)]
        down = [(j, i) for i, j in up]
        last = lax.slice_in_dim(shard, length - width, length, axis=dim)
        first = lax.slice_in_dim(shard, 0, width, axis=dim)
        before = lax.ppermute(last, axis, up)
        after = lax.ppermute(first, axis, down)
        shard = jnp.concatenate([before, shard, after], axis=dim)
    return shard


def broadcast(block, axis, holder):
    block = jnp.where(lax.axis_index(axis) == holder, block, jnp.zeros_like(block))
    return lax.psum(block, axis)


def spectral_update(spectra_now, electric, magnetic, phase_start, step_number):
    angle_half = phase_start[0] + ANGULAR_STEP * (step_number + 0.5)
    angle_full = phase_start[0] + ANGULAR_STEP * (step_number + 1.0)
    return jnp.concatenate(
        [
            spectra_now[0:3] + electric * jnp.cos(angle_full),
            spectra_now[3:6] + magnetic * jnp.cos(angle_half),
            spectra_now[6:9] - electric * jnp.sin(angle_full),
            spectra_now[9:12] - magnetic * jnp.sin(angle_half),
        ]
    )


def face_values(spectral_plane, facing, chosen):
    real_part = [
        CURRENT_SIGNS[number] * facing * spectral_plane[chosen[number]] for number in range(4)
    ]
    imag_part = [
        CURRENT_SIGNS[number] * facing * spectral_plane[6 + chosen[number]] for number in range(4)
    ]
    return jnp.stack(real_part + imag_part)


def to_vectors(record_values, x_flag):
    z_flag = 1.0 - x_flag
    stacked_rows = []
    for offset in (0, 4):
        tangent_one = record_values[offset]
        tangent_two = record_values[offset + 1]
        moment_one = record_values[offset + 2]
        moment_two = record_values[offset + 3]
        stacked_rows += [
            z_flag * tangent_one,
            x_flag * tangent_one + z_flag * tangent_two,
            x_flag * tangent_two,
            z_flag * moment_one,
            x_flag * moment_one + z_flag * moment_two,
            x_flag * moment_two,
        ]
    return jnp.stack(stacked_rows)


def to_record(gradient, x_flag):
    z_flag = 1.0 - x_flag
    stacked_rows = []
    for offset in (0, 6):
        stacked_rows += [
            x_flag * gradient[offset + 1] + z_flag * gradient[offset],
            x_flag * gradient[offset + 2] + z_flag * gradient[offset + 1],
            x_flag * gradient[offset + 4] + z_flag * gradient[offset + 3],
            x_flag * gradient[offset + 5] + z_flag * gradient[offset + 4],
        ]
    return jnp.stack(stacked_rows)


def direction_frames(dir_index):
    polar_row = (dir_index // THETAS).astype(jnp.float32)
    azimuth_col = (dir_index % THETAS).astype(jnp.float32)
    polar_angle = jnp.pi * (polar_row + 0.5) / THETAS
    azimuth = 2.0 * jnp.pi * azimuth_col / THETAS
    sin_polar = jnp.sin(polar_angle)
    cos_polar = jnp.cos(polar_angle)
    sin_azim = jnp.sin(azimuth)
    cos_azim = jnp.cos(azimuth)
    unit_vectors = jnp.stack([sin_polar * cos_azim, sin_polar * sin_azim, cos_polar], axis=1)
    theta_hat = jnp.stack([cos_polar * cos_azim, cos_polar * sin_azim, -sin_polar], axis=1)
    phi_hat = jnp.stack([-sin_azim, cos_azim, jnp.zeros_like(sin_azim)], axis=1)
    return (unit_vectors, theta_hat, phi_hat)


def steering(unit_block, positions):
    angle_table = WAVE_NUMBER * (
        positions[0][:, None] * unit_block[None, :, 0]
        + positions[1][:, None] * unit_block[None, :, 1]
        + positions[2][:, None] * unit_block[None, :, 2]
    )
    return (jnp.cos(angle_table), jnp.sin(angle_table))


def far_block(unit_block, currents, positions):
    cosine_table, sine_table = steering(unit_block, positions)
    real_part = jnp.dot(currents[:6], cosine_table, precision=HIGHEST) - jnp.dot(
        currents[6:], sine_table, precision=HIGHEST
    )
    imag_part = jnp.dot(currents[:6], sine_table, precision=HIGHEST) + jnp.dot(
        currents[6:], cosine_table, precision=HIGHEST
    )
    return jnp.concatenate([real_part, imag_part], axis=0)


def adjoint_block(unit_block, slope_block, positions):
    cosine_table, sine_table = steering(unit_block, positions)
    real_part = jnp.dot(slope_block[:6], cosine_table.T, precision=HIGHEST) + jnp.dot(
        slope_block[6:], sine_table.T, precision=HIGHEST
    )
    imag_part = jnp.dot(slope_block[6:], cosine_table.T, precision=HIGHEST) - jnp.dot(
        slope_block[:6], sine_table.T, precision=HIGHEST
    )
    return jnp.concatenate([real_part, imag_part], axis=0)


def intensity_and_slope(far_total, theta_hat, phi_hat, target, aim_mask):
    theta_rows = theta_hat.T
    phi_rows = phi_hat.T

    def project(vectors, frame_rows):
        return jnp.sum(vectors * frame_rows, axis=0)

    e_theta_re = -(project(far_total[3:6], phi_rows) + project(far_total[0:3], theta_rows))
    e_phi_re = project(far_total[3:6], theta_rows) - project(far_total[0:3], phi_rows)
    e_theta_im = -(project(far_total[9:12], phi_rows) + project(far_total[6:9], theta_rows))
    e_phi_im = project(far_total[9:12], theta_rows) - project(far_total[6:9], phi_rows)
    intensity = (
        e_theta_re * e_theta_re
        + e_theta_im * e_theta_im
        + e_phi_re * e_phi_re
        + e_phi_im * e_phi_im
    )
    residual = aim_mask.astype(jnp.float32) * (intensity - target)
    slope_theta_re = 2.0 * residual * e_theta_re
    slope_phi_re = 2.0 * residual * e_phi_re
    slope_theta_im = 2.0 * residual * e_theta_im
    slope_phi_im = 2.0 * residual * e_phi_im
    n_re = -slope_theta_re * theta_rows - slope_phi_re * phi_rows
    l_re = -slope_theta_re * phi_rows + slope_phi_re * theta_rows
    n_im = -slope_theta_im * theta_rows - slope_phi_im * phi_rows
    l_im = -slope_theta_im * phi_rows + slope_phi_im * theta_rows
    return (intensity, jnp.concatenate([n_re, l_re, n_im, l_im], axis=0))


def rim_keep_mask(length, device_index):
    indices = jnp.arange(length)
    return jnp.where((indices == 0) & (device_index == 0), 0.0, 1.0).astype(jnp.float32)


def yee_step(field_state, step_rate, rim_keep):
    padded = padded_2(field_state, (("gz", 2), ("dev", 1), ("xy", 3)), 1)
    size_y, size_z, size_x = (field_state.shape[1], field_state.shape[2], field_state.shape[3])

    def region(component, shift_y, shift_z, shift_x):
        return padded[
            component,
            shift_y : shift_y + size_y + 1,
            shift_z : shift_z + size_z + 1,
            shift_x : shift_x + size_x + 1,
        ]

    def ahead_diff(component, axis_number):
        shifts = [0, 0, 0]
        shifts[axis_number] = 1
        return region(component, shifts[0], shifts[1], shifts[2]) - region(component, 0, 0, 0)

    magn_x = (region(3, 0, 0, 0) - COURANT * (ahead_diff(2, 0) - ahead_diff(1, 1))) * rim_keep
    magn_y = (region(4, 0, 0, 0) - COURANT * (ahead_diff(0, 1) - ahead_diff(2, 2))) * rim_keep
    magn_z = (region(5, 0, 0, 0) - COURANT * (ahead_diff(1, 2) - ahead_diff(0, 0))) * rim_keep

    def behind(magnetic, axis_number):
        center = magnetic[1:, 1:, 1:]
        if axis_number == 0:
            earlier = magnetic[:-1, 1:, 1:]
        elif axis_number == 1:
            earlier = magnetic[1:, :-1, 1:]
        else:
            earlier = magnetic[1:, 1:, :-1]
        return center - earlier

    elec_x = padded[0, 1:-1, 1:-1, 1:-1] + step_rate * (behind(magn_z, 0) - behind(magn_y, 1))
    elec_y = padded[1, 1:-1, 1:-1, 1:-1] + step_rate * (behind(magn_x, 1) - behind(magn_z, 2))
    elec_z = padded[2, 1:-1, 1:-1, 1:-1] + step_rate * (behind(magn_y, 2) - behind(magn_x, 0))
    electric = jnp.stack([elec_x, elec_y, elec_z])
    magnetic = jnp.stack([magn_x[1:, 1:, 1:], magn_y[1:, 1:, 1:], magn_z[1:, 1:, 1:]])
    return (electric, magnetic)


def point_layout(home_records, home_meta, centers, norm_scale):
    record_total = home_records.shape[0]
    record_values = (
        home_records.reshape(record_total, 8, PATCH)
        .transpose(1, 0, 2)
        .reshape(8, record_total * PATCH)
    )
    x_flag = jnp.repeat(jnp.where(home_meta[:, 3] < 2.5, 1.0, 0.0).astype(jnp.float32), PATCH)
    offsets = jnp.tile(jnp.arange(PATCH, dtype=jnp.float32), record_total)
    positions = jnp.stack(
        [
            jnp.repeat(home_meta[:, 0], PATCH) + offsets * (1.0 - x_flag) - centers[0],
            jnp.repeat(home_meta[:, 1], PATCH) - centers[1],
            jnp.repeat(home_meta[:, 2], PATCH) + offsets * x_flag - centers[2],
        ]
    )
    return (to_vectors(record_values, x_flag) * norm_scale, positions, x_flag)


def cap_layout(cap_count, size_x, size_y, xy_index, dev_index, z_global, flag_value):
    cap_flat = jnp.arange(cap_count, dtype=jnp.int32) * PATCH
    cap_ones = jnp.ones((cap_count,), jnp.float32)
    return jnp.stack(
        [
            (xy_index * size_x + cap_flat % size_x).astype(jnp.float32),
            (dev_index * size_y + cap_flat // size_x).astype(jnp.float32),
            cap_ones * z_global,
            cap_ones * flag_value,
        ],
        axis=1,
    )


def mine_selector(owner_row, gz_index, share):
    mine = owner_row == gz_index
    rank = jnp.cumsum(mine.astype(jnp.int32)) - 1
    return jnp.where(
        (jnp.arange(share, dtype=jnp.int32)[:, None] == rank[None, :]) & mine[None, :], 1.0, 0.0
    ).astype(jnp.float32)


def local(
    fields, spectra, permittivity, phase_start, wall_owner, cap_owner, dir_index, target, aim_mask
):
    slab_count = lax.axis_size("gz")
    dev_count = lax.axis_size("dev")
    xy_count = lax.axis_size("xy")
    gz_index = lax.axis_index("gz")
    dev_index = lax.axis_index("dev")
    xy_index = lax.axis_index("xy")
    size_y, size_z, size_x = permittivity.shape
    keep_y = rim_keep_mask(size_y + 1, dev_index)
    keep_z = rim_keep_mask(size_z + 1, gz_index)
    keep_x = rim_keep_mask(size_x + 1, xy_index)
    rim_keep = keep_y[:, None, None] * keep_z[None, :, None] * keep_x[None, None, :]
    step_rate = COURANT / permittivity
    field_state = fields
    spectra_now = spectra
    for step_number in range(STEPS):
        electric, magnetic = yee_step(field_state, step_rate, rim_keep)
        field_state = jnp.concatenate([electric, magnetic])
        spectra_now = spectral_update(spectra_now, electric, magnetic, phase_start, step_number)
    grid_x = size_x * xy_count
    grid_y = size_y * dev_count
    grid_z = size_z * slab_count
    x_local = jnp.where(xy_index == 0, XB, size_x - 1 - XB).astype(jnp.int32)
    facing_x = jnp.where(xy_index == 0, -1.0, 1.0)
    wall_plane = lax.dynamic_slice_in_dim(spectra_now, x_local, 1, axis=3)[:, :, :, 0]
    wall_count = size_y * size_z // PATCH
    wall_records = (
        face_values(wall_plane, facing_x, X_PICKS).transpose(1, 0, 2).reshape(wall_count, 8 * PATCH)
    )
    z_local = jnp.where(gz_index == 0, ZB, size_z - 1 - ZB).astype(jnp.int32)
    facing_z = jnp.where(gz_index == 0, -1.0, 1.0)
    cap_plane = lax.dynamic_slice_in_dim(spectra_now, z_local, 1, axis=2)[:, :, 0, :]
    cap_count = size_y * size_x // PATCH
    cap_records = (
        face_values(cap_plane, facing_z, Z_PICKS)
        .reshape(8, cap_count, PATCH)
        .transpose(1, 0, 2)
        .reshape(cap_count, 8 * PATCH)
    )
    is_end = jnp.logical_or(gz_index == 0, gz_index == slab_count - 1)
    end_weight = jnp.where(is_end, 1.0, 0.0)
    wall_flat = jnp.arange(wall_count, dtype=jnp.int32) * PATCH
    wall_ones = jnp.ones((wall_count,), jnp.float32)
    wall_meta = jnp.stack(
        [
            wall_ones * (xy_index * size_x + x_local).astype(jnp.float32),
            (dev_index * size_y + wall_flat // size_z).astype(jnp.float32),
            (gz_index * size_z + wall_flat % size_z).astype(jnp.float32),
            wall_ones * jnp.where(xy_index == 0, 1.0, 2.0),
        ],
        axis=1,
    )
    owners = wall_owner[0]
    record_order = jnp.arange(wall_count, dtype=jnp.int32)
    earlier_same = (owners[:, None] == owners[None, :]) & (
        record_order[None, :] < record_order[:, None]
    )
    slot_rank = jnp.sum(earlier_same.astype(jnp.int32), axis=1)
    cap_share = cap_count // slab_count
    wall_most = (wall_count + slab_count - 1) // slab_count
    slot_index = owners * wall_most + slot_rank
    slot_range = jnp.arange(slab_count * wall_most, dtype=jnp.int32)
    send_onehot = jnp.where(slot_range[:, None] == slot_index[None, :], 1.0, 0.0).astype(
        jnp.float32
    )
    send_records = jnp.dot(send_onehot, wall_records, precision=HIGHEST).reshape(
        slab_count, wall_most, 8 * PATCH
    )
    send_meta = jnp.dot(send_onehot, wall_meta, precision=HIGHEST).reshape(slab_count, wall_most, 4)
    got_records, got_meta = (
        lax.all_to_all(send_records, "gz", split_axis=0, concat_axis=0, tiled=True),
        lax.all_to_all(send_meta, "gz", split_axis=0, concat_axis=0, tiled=True),
    )
    flat_records = got_records.reshape(slab_count * wall_most, 8 * PATCH)
    flat_meta = got_meta.reshape(slab_count * wall_most, 4)
    alive_slots = flat_meta[:, 3] > 0.5
    position = jnp.cumsum(alive_slots.astype(jnp.int32)) - 1
    own_onehot = jnp.where(
        (jnp.arange(wall_count, dtype=jnp.int32)[:, None] == position[None, :])
        & alive_slots[None, :],
        1.0,
        0.0,
    ).astype(jnp.float32)
    owned_walls = jnp.dot(own_onehot, flat_records, precision=HIGHEST)
    owned_wall_meta = jnp.dot(own_onehot, flat_meta, precision=HIGHEST)
    lower_got = broadcast(cap_records, "gz", 0)
    upper_got = broadcast(cap_records, "gz", slab_count - 1)
    lower_onehot = mine_selector(cap_owner[0], gz_index, cap_share)
    upper_onehot = mine_selector(cap_owner[1], gz_index, cap_share)
    lower_meta = cap_layout(cap_count, size_x, size_y, xy_index, dev_index, float(ZB), 3.0)
    upper_meta = cap_layout(
        cap_count, size_x, size_y, xy_index, dev_index, float(grid_z - 1 - ZB), 4.0
    )
    owned_rows = jnp.concatenate(
        [
            owned_walls,
            jnp.dot(lower_onehot, lower_got, precision=HIGHEST),
            jnp.dot(upper_onehot, upper_got, precision=HIGHEST),
        ]
    )
    owned_meta = jnp.concatenate(
        [
            owned_wall_meta,
            jnp.dot(lower_onehot, lower_meta, precision=HIGHEST),
            jnp.dot(upper_onehot, upper_meta, precision=HIGHEST),
        ]
    )
    unit_vectors, theta_hat, phi_hat = direction_frames(dir_index)
    centers = ((grid_x - 1) / 2.0, (grid_y - 1) / 2.0, (grid_z - 1) / 2.0)
    surface_count = 2 * grid_y * grid_z + 2 * grid_y * grid_x
    norm_scale = 1.0 / math.sqrt(2.0 * surface_count)
    currents, positions, x_flag = point_layout(owned_rows, owned_meta, centers, norm_scale)
    direction_count = unit_vectors.shape[0]
    block_size = min(512, direction_count)
    partial_far = jnp.concatenate(
        [
            far_block(unit_vectors[block_start : block_start + block_size], currents, positions)
            for block_start in range(0, direction_count, block_size)
        ],
        axis=1,
    )
    joined_index = (gz_index * dev_count + dev_index) * xy_count + xy_index
    share_count = direction_count // (slab_count * dev_count * xy_count)
    first_dir = joined_index * share_count
    far_total = lax.psum(partial_far, ("gz", "dev", "xy"))
    intensity_all, slope_total = intensity_and_slope(
        far_total, theta_hat, phi_hat, target, aim_mask
    )
    intensity = lax.dynamic_slice_in_dim(intensity_all, first_dir, share_count, 0)
    gradient = adjoint_block(unit_vectors[0:block_size], slope_total[:, 0:block_size], positions)
    for block_start in range(block_size, direction_count, block_size):
        gradient = gradient + adjoint_block(
            unit_vectors[block_start : block_start + block_size],
            slope_total[:, block_start : block_start + block_size],
            positions,
        )
    point_count = gradient.shape[1] // PATCH
    adjoint_records = (
        to_record(gradient * norm_scale, x_flag)
        .reshape(8, point_count, PATCH)
        .transpose(1, 0, 2)
        .reshape(point_count, 8 * PATCH)
    )
    spread_back = jnp.dot(own_onehot.T, adjoint_records[:wall_count], precision=HIGHEST).reshape(
        slab_count, wall_most, 8 * PATCH
    )
    returned = lax.all_to_all(spread_back, "gz", split_axis=0, concat_axis=0, tiled=True)
    wall_adjoint = jnp.dot(
        send_onehot.T, returned.reshape(slab_count * wall_most, 8 * PATCH), precision=HIGHEST
    )
    lower_part = adjoint_records[wall_count : wall_count + cap_share]
    upper_part = adjoint_records[wall_count + cap_share :]
    cap_sheet = jnp.stack(
        [
            jnp.dot(lower_onehot.T, lower_part, precision=HIGHEST),
            jnp.dot(upper_onehot.T, upper_part, precision=HIGHEST),
        ]
    )
    cap_sum = lax.psum(cap_sheet, "gz")
    cap_adjoint = jnp.where(gz_index == 0, cap_sum[0], cap_sum[1]) * end_weight
    adjoint_local = jnp.concatenate([wall_adjoint, cap_adjoint])
    return (
        field_state,
        spectra_now,
        owned_rows[None, None, None],
        intensity,
        adjoint_local[None, None, None],
    )


def solution(mesh):
    placed = (
        P("groups", "dev", "gz", "xy"),
        P("groups", "dev", "gz", "xy"),
        P(("groups", "dev"), "gz", "xy"),
        P("groups"),
        P("gz", None),
        P(),
        P(),
        P("groups"),
        P("groups"),
    )
    return jax.shard_map(
        local,
        mesh=mesh,
        in_specs=placed,
        out_specs=(
            P("groups", "dev", "gz", "xy"),
            P("groups", "dev", "gz", "xy"),
            P(("groups", "gz"), "dev", "xy", None, None),
            P(("groups", "gz", "dev", "xy")),
            P(("groups", "gz"), "dev", "xy", None, None),
        ),
        check_vma=False,
    )
```

profile of v0, /device:TPU:0, one launch (start us, length us, event | category | flops | bytes accessed | tf_op | source)
XLA Modules:
  0.0 338.1 jit_solution(17645889408166721853)
XLA Ops:
  8.9 6.3 %all-to-all-start = ((f32[4,1,4]{2,1,0:T(1,128)}), f32[4,1,4]{2,1,0:T(1,128)S(1)}, u32[]{:S(2)}, u32[]{:S(2)}) async-start(f32[4,1,4]{2,1,0:T(1,128)} %bitcast.46), calls=%async_computation | async-start | bytes 4096 | tf_op jit(solution)/shard_map/all_to_all | solution.py:330
  16.2 3.9 %collective-permute-start = (f32[6,4,1,128]{3,2,1,0:T(1,128)S(1)}, f32[6,4,1,128]{3,2,1,0:T(1,128)S(1)}, u32[]{:S(2)}, u32[]{:S(2)}) collective-permute-start(f32[6,4,1,128]{3,2,1,0:T(1,128)S(1)} %get-tuple-element.119), channel_id=1, source_target_pairs={{0,4},{4,8},{8,12},{1,5},{5,9},{9,13},{2,6},{6,10},{10,14},{3,7},{... | collective-permute-start | bytes 36872 | tf_op jit(solution)/shard_map/ppermute | solution.py:31
  25.9 3.4 %collective-permute-start.2 = (f32[6,1,18,128]{3,2,1,0:T(8,128)S(1)}, f32[6,1,18,128]{3,2,1,0:T(8,128)S(1)}, u32[]{:S(2)}, u32[]{:S(2)}) collective-permute-start(f32[6,1,18,128]{3,2,1,0:T(8,128)S(1)} %get-tuple-element.113), channel_id=1, source_target_pairs={{0,2},{1,3},{4,6},{5,7},{8,10},{9,11},{12,14},{13,15},{16,18},{17,... | collective-permute-start | bytes 165896 | tf_op jit(solution)/shard_map/ppermute | solution.py:31
  31.3 4.3 %collective-permute-done.3 = f32[6,1,18,128]{3,2,1,0:T(8,128)S(1)} collective-permute-done((f32[6,1,18,128]{3,2,1,0:T(8,128)S(1)}, f32[6,1,18,128]{3,2,1,0:T(8,128)S(1)}, u32[]{:S(2)}, u32[]{:S(2)}) %collective-permute-start.3) | collective-permute-done | bytes 55328 | tf_op jit(solution)/shard_map/ppermute | solution.py:32
  38.9 2.0 collective-permute-done.5
  42.3 4.5 %collective-permute-start.6 = (f32[6,4,1,128]{3,2,1,0:T(1,128)S(1)}, f32[6,4,1,128]{3,2,1,0:T(1,128)S(1)}, u32[]{:S(2)}, u32[]{:S(2)}) collective-permute-start(f32[6,4,1,128]{3,2,1,0:T(1,128)S(1)} %get-tuple-element.117), channel_id=1, source_target_pairs={{0,4},{4,8},{8,12},{1,5},{5,9},{9,13},{2,6},{6,10},{10,14},{3,7},{... | collective-permute-start | bytes 36872 | tf_op jit(solution)/shard_map/ppermute | solution.py:31
  48.6 3.8 %collective-permute-done.7 = f32[6,4,1,128]{3,2,1,0:T(1,128)S(1)} collective-permute-done((f32[6,4,1,128]{3,2,1,0:T(1,128)S(1)}, f32[6,4,1,128]{3,2,1,0:T(1,128)S(1)}, u32[]{:S(2)}, u32[]{:S(2)}) %collective-permute-start.7) | collective-permute-done | bytes 12320 | tf_op jit(solution)/shard_map/ppermute | solution.py:32
  56.0 4.3 %collective-permute-done.9 = f32[6,1,18,128]{3,2,1,0:T(8,128)S(1)} collective-permute-done((f32[6,1,18,128]{3,2,1,0:T(8,128)S(1)}, f32[6,1,18,128]{3,2,1,0:T(8,128)S(1)}, u32[]{:S(2)}, u32[]{:S(2)}) %collective-permute-start.9) | collective-permute-done | bytes 55328 | tf_op jit(solution)/shard_map/ppermute | solution.py:32
  66.4 3.4 collective-permute-start.12
  71.2 4.2 %collective-permute-done.13 = f32[6,4,1,128]{3,2,1,0:T(1,128)S(1)} collective-permute-done((f32[6,4,1,128]{3,2,1,0:T(1,128)S(1)}, f32[6,4,1,128]{3,2,1,0:T(1,128)S(1)}, u32[]{:S(2)}, u32[]{:S(2)}) %collective-permute-start.13) | collective-permute-done | bytes 12320 | tf_op jit(solution)/shard_map/ppermute | solution.py:32
  78.9 4.3 %collective-permute-done.15 = f32[6,1,18,128]{3,2,1,0:T(8,128)S(1)} collective-permute-done((f32[6,1,18,128]{3,2,1,0:T(8,128)S(1)}, f32[6,1,18,128]{3,2,1,0:T(8,128)S(1)}, u32[]{:S(2)}, u32[]{:S(2)}) %collective-permute-start.15) | collective-permute-done | bytes 55328 | tf_op jit(solution)/shard_map/ppermute | solution.py:32
  92.0 3.2 all-to-all-start.1
  95.6 21.6 %all-reduce = (f32[32,128]{0,1:T(8,128)S(1)}, f32[32,128]{0,1:T(8,128)S(1)}) all-reduce(f32[32,128]{0,1:T(8,128)S(1)} %bitcast.259, f32[32,128]{0,1:T(8,128)S(1)} %bitcast.258), channel_id=1, replica_groups=mesh['groups'=2,'gz'=4,'dev'=2,'xy'=2] {'gz'}, use_global_device_ids=true, to_apply=%region_5.6 | all-reduce | flops 8192 | bytes 65536 | tf_op jit(solution)/shard_map/psum | solution.py:39
  119.0 2.8 fusion.40
  121.8 2.8 fusion.32
  124.6 2.8 fusion.26
  127.4 2.8 fusion.18
  130.3 3.2 fusion.12
  133.5 2.8 fusion.4
  136.3 2.8 fusion.46
  139.1 2.8 fusion.54
  141.9 3.0 convolution_add_fusion.3
  144.9 2.8 convolution_subtract_fusion.2
  147.7 2.8 convolution_add_fusion.2
  150.5 2.8 convolution_subtract_fusion.1
  153.3 3.0 convolution_add_fusion.1
  156.3 2.8 convolution_subtract_fusion
  159.1 2.8 convolution_add_fusion
  162.0 2.8 convolution_subtract_fusion.3
  166.2 83.9 %all-reduce.3.cloned.1.call-done = f32[12,2048]{1,0:T(8,128)} async-done(((f32[12,2048]{1,0:T(8,128)}), f32[12,2048]{1,0:T(8,128)}) %all-reduce.3.cloned.1.call-update) | async-done | bytes 98320 | tf_op jit(solution)/shard_map/psum | solution.py:383
  252.2 3.3 fusion.21
  255.6 3.0 fusion.49
  258.5 3.0 fusion.35
  261.7 2.9 fusion.51
  264.6 3.0 fusion.37
  267.6 3.2 fusion.23
  270.8 3.0 convolution_subtract_fusion.5
  273.8 3.0 convolution_subtract_fusion.7
  276.8 3.0 convolution_subtract_fusion.6
  279.8 3.2 convolution_add_fusion.7
  283.0 3.0 convolution_add_fusion.6
  286.1 3.0 convolution_add_fusion.5
  289.1 3.0 fusion.7
  292.1 3.2 fusion.9
  295.3 3.0 convolution_subtract_fusion.4
  298.3 3.0 convolution_add_fusion.4
  303.2 6.2 %all-to-all-start.2 = ((f32[4,1,128]{2,1,0:T(1,128)}), f32[4,1,128]{2,1,0:T(1,128)S(1)}, u32[]{:S(2)}, u32[]{:S(2)}) async-start(f32[4,1,128]{2,1,0:T(1,128)} %bitcast.77), calls=%async_computation.2 | async-start | bytes 4096 | tf_op jit(solution)/shard_map/all_to_all | solution.py:405
  309.9 19.5 %psum.31 = f32[2,32,128]{2,1,0:T(8,128)S(1)} all-reduce(f32[2,32,128]{2,1,0:T(8,128)S(1)} %pad_maximum_fusion.34), channel_id=1, replica_groups=mesh['groups'=2,'gz'=4,'dev'=2,'xy'=2] {'gz'}, use_global_device_ids=true, to_apply=%region_15.16 | all-reduce | flops 8192 | bytes 65536 | tf_op jit(solution)/shard_map/psum | solution.py:417
  (245 shorter events, 47.8 us)
Async XLA Ops:
  7.3 0.7 copy-start.9
  8.9 16.5 %all-to-all-start = ((f32[4,1,4]{2,1,0:T(1,128)}), f32[4,1,4]{2,1,0:T(1,128)S(1)}, u32[]{:S(2)}, u32[]{:S(2)}) async-start(f32[4,1,4]{2,1,0:T(1,128)} %bitcast.46), calls=%async_computation | async-start | bytes 4096 | tf_op jit(solution)/shard_map/all_to_all | solution.py:330
  16.2 9.6 %collective-permute-start = (f32[6,4,1,128]{3,2,1,0:T(1,128)S(1)}, f32[6,4,1,128]{3,2,1,0:T(1,128)S(1)}, u32[]{:S(2)}, u32[]{:S(2)}) collective-permute-start(f32[6,4,1,128]{3,2,1,0:T(1,128)S(1)} %get-tuple-element.119), channel_id=1, source_target_pairs={{0,4},{4,8},{8,12},{1,5},{5,9},{9,13},{2,6},{6,10},{10,14},{3,7},{... | collective-permute-start | bytes 36872 | tf_op jit(solution)/shard_map/ppermute | solution.py:31
  20.1 5.7 %collective-permute-start.1 = (f32[6,4,1,128]{3,2,1,0:T(1,128)S(1)}, f32[6,4,1,128]{3,2,1,0:T(1,128)S(1)}, u32[]{:S(2)}, u32[]{:S(2)}) collective-permute-start(f32[6,4,1,128]{3,2,1,0:T(1,128)S(1)} %get-tuple-element.120), channel_id=1, source_target_pairs={{4,0},{8,4},{12,8},{5,1},{9,5},{13,9},{6,2},{10,6},{14,10},{7,3},{... | collective-permute-start | bytes 36872 | tf_op jit(solution)/shard_map/ppermute | solution.py:32
  23.3 0.7 copy-start.8
  24.2 0.7 copy-start.4
  24.3 1.6 copy-start
  25.9 5.4 %collective-permute-start.2 = (f32[6,1,18,128]{3,2,1,0:T(8,128)S(1)}, f32[6,1,18,128]{3,2,1,0:T(8,128)S(1)}, u32[]{:S(2)}, u32[]{:S(2)}) collective-permute-start(f32[6,1,18,128]{3,2,1,0:T(8,128)S(1)} %get-tuple-element.113), channel_id=1, source_target_pairs={{0,2},{1,3},{4,6},{5,7},{8,10},{9,11},{12,14},{13,15},{16,18},{17,... | collective-permute-start | bytes 165896 | tf_op jit(solution)/shard_map/ppermute | solution.py:31
  29.3 6.2 %collective-permute-start.3 = (f32[6,1,18,128]{3,2,1,0:T(8,128)S(1)}, f32[6,1,18,128]{3,2,1,0:T(8,128)S(1)}, u32[]{:S(2)}, u32[]{:S(2)}) collective-permute-start(f32[6,1,18,128]{3,2,1,0:T(8,128)S(1)} %get-tuple-element.114), channel_id=1, source_target_pairs={{2,0},{3,1},{6,4},{7,5},{10,8},{11,9},{14,12},{15,13},{18,16},{19,... | collective-permute-start | bytes 165896 | tf_op jit(solution)/shard_map/ppermute | solution.py:32
  35.8 2.7 collective-permute-start.4
  37.2 3.7 %collective-permute-start.5 = (f32[6,6,18,1]{3,2,1,0:T(8,128)S(1)}, f32[6,6,18,1]{3,2,1,0:T(8,128)S(1)}, u32[]{:S(2)}, u32[]{:S(2)}) collective-permute-start(f32[6,6,18,1]{3,2,1,0:T(8,128)S(1)} %get-tuple-element.108), channel_id=1, source_target_pairs={{1,0},{3,2},{5,4},{7,6},{9,8},{11,10},{13,12},{15,14},{17,16},{19,... | collective-permute-start | bytes 7784 | tf_op jit(solution)/shard_map/ppermute | solution.py:32
  41.0 0.8 copy-start.1
  42.3 6.3 %collective-permute-start.6 = (f32[6,4,1,128]{3,2,1,0:T(1,128)S(1)}, f32[6,4,1,128]{3,2,1,0:T(1,128)S(1)}, u32[]{:S(2)}, u32[]{:S(2)}) collective-permute-start(f32[6,4,1,128]{3,2,1,0:T(1,128)S(1)} %get-tuple-element.117), channel_id=1, source_target_pairs={{0,4},{4,8},{8,12},{1,5},{5,9},{9,13},{2,6},{6,10},{10,14},{3,7},{... | collective-permute-start | bytes 36872 | tf_op jit(solution)/shard_map/ppermute | solution.py:31
  46.8 5.6 %collective-permute-start.7 = (f32[6,4,1,128]{3,2,1,0:T(1,128)S(1)}, f32[6,4,1,128]{3,2,1,0:T(1,128)S(1)}, u32[]{:S(2)}, u32[]{:S(2)}) collective-permute-start(f32[6,4,1,128]{3,2,1,0:T(1,128)S(1)} %get-tuple-element.118), channel_id=1, source_target_pairs={{4,0},{8,4},{12,8},{5,1},{9,5},{13,9},{6,2},{10,6},{14,10},{7,3},{... | collective-permute-start | bytes 36872 | tf_op jit(solution)/shard_map/ppermute | solution.py:32
  52.5 3.5 %collective-permute-start.8 = (f32[6,1,18,128]{3,2,1,0:T(8,128)S(1)}, f32[6,1,18,128]{3,2,1,0:T(8,128)S(1)}, u32[]{:S(2)}, u32[]{:S(2)}) collective-permute-start(f32[6,1,18,128]{3,2,1,0:T(8,128)S(1)} %get-tuple-element.111), channel_id=1, source_target_pairs={{0,2},{1,3},{4,6},{5,7},{8,10},{9,11},{12,14},{13,15},{16,18},{17,... | collective-permute-start | bytes 165896 | tf_op jit(solution)/shard_map/ppermute | solution.py:31
  54.0 6.2 %collective-permute-start.9 = (f32[6,1,18,128]{3,2,1,0:T(8,128)S(1)}, f32[6,1,18,128]{3,2,1,0:T(8,128)S(1)}, u32[]{:S(2)}, u32[]{:S(2)}) collective-permute-start(f32[6,1,18,128]{3,2,1,0:T(8,128)S(1)} %get-tuple-element.112), channel_id=1, source_target_pairs={{2,0},{3,1},{6,4},{7,5},{10,8},{11,9},{14,12},{15,13},{18,16},{19,... | collective-permute-start | bytes 165896 | tf_op jit(solution)/shard_map/ppermute | solution.py:32
  60.5 2.7 collective-permute-start.10
  61.9 3.7 %collective-permute-start.11 = (f32[6,6,18,1]{3,2,1,0:T(8,128)S(1)}, f32[6,6,18,1]{3,2,1,0:T(8,128)S(1)}, u32[]{:S(2)}, u32[]{:S(2)}) collective-permute-start(f32[6,6,18,1]{3,2,1,0:T(8,128)S(1)} %get-tuple-element.106), channel_id=1, source_target_pairs={{1,0},{3,2},{5,4},{7,6},{9,8},{11,10},{13,12},{15,14},{17,16},{19,... | collective-permute-start | bytes 7784 | tf_op jit(solution)/shard_map/ppermute | solution.py:32
  66.4 4.8 %collective-permute-start.12 = (f32[6,4,1,128]{3,2,1,0:T(1,128)S(1)}, f32[6,4,1,128]{3,2,1,0:T(1,128)S(1)}, u32[]{:S(2)}, u32[]{:S(2)}) collective-permute-start(f32[6,4,1,128]{3,2,1,0:T(1,128)S(1)} %get-tuple-element.115), channel_id=1, source_target_pairs={{0,4},{4,8},{8,12},{1,5},{5,9},{9,13},{2,6},{6,10},{10,14},{3,7},{... | collective-permute-start | bytes 36872 | tf_op jit(solution)/shard_map/ppermute | solution.py:31
  69.8 5.6 %collective-permute-start.13 = (f32[6,4,1,128]{3,2,1,0:T(1,128)S(1)}, f32[6,4,1,128]{3,2,1,0:T(1,128)S(1)}, u32[]{:S(2)}, u32[]{:S(2)}) collective-permute-start(f32[6,4,1,128]{3,2,1,0:T(1,128)S(1)} %get-tuple-element.116), channel_id=1, source_target_pairs={{4,0},{8,4},{12,8},{5,1},{9,5},{13,9},{6,2},{10,6},{14,10},{7,3},{... | collective-permute-start | bytes 36872 | tf_op jit(solution)/shard_map/ppermute | solution.py:32
  75.4 3.5 %collective-permute-start.14 = (f32[6,1,18,128]{3,2,1,0:T(8,128)S(1)}, f32[6,1,18,128]{3,2,1,0:T(8,128)S(1)}, u32[]{:S(2)}, u32[]{:S(2)}) collective-permute-start(f32[6,1,18,128]{3,2,1,0:T(8,128)S(1)} %get-tuple-element.109), channel_id=1, source_target_pairs={{0,2},{1,3},{4,6},{5,7},{8,10},{9,11},{12,14},{13,15},{16,18},{17,... | collective-permute-start | bytes 165896 | tf_op jit(solution)/shard_map/ppermute | solution.py:31
  77.0 6.2 %collective-permute-start.15 = (f32[6,1,18,128]{3,2,1,0:T(8,128)S(1)}, f32[6,1,18,128]{3,2,1,0:T(8,128)S(1)}, u32[]{:S(2)}, u32[]{:S(2)}) collective-permute-start(f32[6,1,18,128]{3,2,1,0:T(8,128)S(1)} %get-tuple-element.110), channel_id=1, source_target_pairs={{2,0},{3,1},{6,4},{7,5},{10,8},{11,9},{14,12},{15,13},{18,16},{19,... | collective-permute-start | bytes 165896 | tf_op jit(solution)/shard_map/ppermute | solution.py:32
  83.5 2.7 collective-permute-start.16
  84.9 3.7 %collective-permute-start.17 = (f32[6,6,18,1]{3,2,1,0:T(8,128)S(1)}, f32[6,6,18,1]{3,2,1,0:T(8,128)S(1)}, u32[]{:S(2)}, u32[]{:S(2)}) collective-permute-start(f32[6,6,18,1]{3,2,1,0:T(8,128)S(1)} %get-tuple-element.104), channel_id=1, source_target_pairs={{1,0},{3,2},{5,4},{7,6},{9,8},{11,10},{13,12},{15,14},{17,16},{19,... | collective-permute-start | bytes 7784 | tf_op jit(solution)/shard_map/ppermute | solution.py:32
  88.9 1.0 copy-start.3
  90.1 5.3 %copy-start.2 = (f32[12,4,16,128]{3,2,1,0:T(8,128)}, f32[12,4,16,128]{3,2,1,0:T(8,128)S(1)}, u32[]{:S(2)}) copy-start(f32[12,4,16,128]{3,2,1,0:T(8,128)S(1)} %pad_maximum_fusion.3) | copy-start | bytes 1179652
  92.0 25.7 %all-to-all-start.1 = ((f32[4,1,128]{2,1,0:T(1,128)}), f32[4,1,128]{2,1,0:T(1,128)S(1)}, u32[]{:S(2)}, u32[]{:S(2)}) async-start(f32[4,1,128]{2,1,0:T(1,128)} %bitcast.50), calls=%async_computation.1 | async-start | bytes 4096 | tf_op jit(solution)/shard_map/all_to_all | solution.py:329
  95.3 154.8 %all-reduce.3.cloned.1.call-start = ((), (), s32[]{:S(2)}) async-start(), calls=%async_computation.3 | async-start | bytes 262144 | tf_op jit(solution)/shard_map/psum | solution.py:383
  165.6 86.5 %copy-start.7 = (f32[6,4,16,128]{3,2,1,0:T(8,128)}, f32[6,4,16,128]{3,2,1,0:T(8,128)S(1)}, u32[]{:S(2)}) copy-start(f32[6,4,16,128]{3,2,1,0:T(8,128)S(1)} %constant_dynamic-update-slice_fusion.12) | copy-start | bytes 589828
  250.1 1.3 copy-start.6
  251.4 0.7 copy-start.5
  303.2 26.9 %all-to-all-start.2 = ((f32[4,1,128]{2,1,0:T(1,128)}), f32[4,1,128]{2,1,0:T(1,128)S(1)}, u32[]{:S(2)}, u32[]{:S(2)}) async-start(f32[4,1,128]{2,1,0:T(1,128)} %bitcast.77), calls=%async_computation.2 | async-start | bytes 4096 | tf_op jit(solution)/shard_map/all_to_all | solution.py:405
Sparse Core Ops, SparseCore 0:
  165.6 84.4 all-reduce.2
where the time goes:
time: 345 us; the launch traced here: 338 us
  waiting for transfers between devices  112 us (32%)
  matrix products  98.6 us (29%)
  starting transfers between devices  49.7 us (14%)
  blocking collectives  41.1 us (12%)
  between operations  17 us (5%)
  local copies, waits for them, and re-layouts  12.6 us (4%)
  other arithmetic  6.95 us (2%)
    psum x1, waiting for transfers between devices, local(): far_total = lax.psum(partial_far, ('gz', 'dev', 'xy'))  83.9 us
    ppermute x9, waiting for transfers between devices, padded_2(): after = lax.ppermute(first, axis, down)  26.8 us
    ppermute x9, starting transfers between devices, padded_2(): before = lax.ppermute(last, axis, up)  22.3 us
    psum x1, blocking collectives, broadcast(): return lax.psum(block, axis)  21.6 us
    psum x1, blocking collectives, local(): cap_sum = lax.psum(cap_sheet, 'gz')  19.5 us
    dot_general x4, matrix products, adjoint_block(): jnp.dot(slope_block[:6], cosine_table.T, precision=HIGHEST)  12.3 us
    dot_general x4, matrix products, adjoint_block(): jnp.dot(slope_block[6:], cosine_table.T, precision=HIGHEST)  12.3 us
    dot_general x4, matrix products, adjoint_block(): jnp.dot(slope_block[6:], sine_table.T, precision=HIGHEST)  12.3 us
  transfers between devices with their start and end apart: 22, of which 12 were waited for; matrix products, arithmetic and copies ran while one was open for 2% of the time, Pallas kernels for 0%

commit v1 on v0

v1 whole, which is shorter than its diff:
```python
import functools
import math

import jax
import jax.numpy as jnp
from jax import lax
from jax.experimental import pallas as pl
from jax.experimental.pallas import tpu as pltpu
from jax.sharding import PartitionSpec as P

PATCH = 16
XB = 8
ZB = 4
STEPS = 3
THETAS = 64
COURANT = 0.5
ANGULAR_STEP = 0.3
WAVE_NUMBER = 0.6
CURRENT_SIGNS = (-1.0, 1.0, 1.0, -1.0)
X_PICKS = (5, 4, 2, 1)
Z_PICKS = (4, 3, 1, 0)
LANES = 128
HALO = STEPS
F32 = jnp.float32
BF16 = jnp.bfloat16
VMEM = pl.BlockSpec(memory_space=pltpu.VMEM)
SMEM = pl.BlockSpec(memory_space=pltpu.SMEM)


def up8(rows):
    return -(-rows // 8) * 8


def sincos(angle):
    turns = jnp.floor(angle * (2.0 / math.pi) + 0.5)
    r = angle - turns * 1.5703125
    r = r - turns * 4.837512969970703125e-4
    r = r - turns * 7.54978995489188e-8
    r2 = r * r
    s = r + r * r2 * (-1.6666654611e-1 + r2 * (8.3321608736e-3 + r2 * -1.9515295891e-4))
    c = 1.0 - 0.5 * r2 + r2 * r2 * (
        4.166664568298827e-2 + r2 * (-1.388731625493765e-3 + r2 * 2.443315711809948e-5)
    )
    quarter = turns.astype(jnp.int32)
    odd = (quarter & 1) == 1
    sine = jnp.where(odd, c, s)
    cosine = jnp.where(odd, s, c)
    sine = jnp.where((quarter & 2) == 2, -sine, sine)
    cosine = jnp.where(((quarter + 1) & 2) == 2, -cosine, cosine)
    return sine, cosine


def split(values):
    high = values.astype(BF16)
    return high, (values - high.astype(F32)).astype(BF16)


def rows_iota(shape):
    return lax.broadcasted_iota(jnp.int32, shape, 0)


def lanes_iota(shape):
    return lax.broadcasted_iota(jnp.int32, shape, len(shape) - 1)


class Sizes:
    def __init__(self, block, directions, caps):
        self.gz, self.dev, self.xy = (lax.axis_size(a) for a in ("gz", "dev", "xy"))
        self.y, self.z, self.x = block
        self.both_y = self.dev > 2
        self.rows = self.y + HALO * (2 if self.both_y else 1)
        self.nx, self.ny, self.nz = self.x * self.xy, self.y * self.dev, self.z * self.gz
        self.dirs = directions
        self.tiles = directions // LANES
        self.walls = self.y * self.z // PATCH
        self.caps = caps
        self.share = caps // self.gz
        self.chunk = up8(2 + self.share)
        self.far_rows = 4 * self.tiles
        self.norm = 1.0 / math.sqrt(2.0 * (2 * self.ny * self.nz + 2 * self.ny * self.nx))
        self.y_rows = 7 * HALO * self.z
        self.z_rows = up8(7 * self.y * HALO)
        self.e_rows = up8(7 * HALO * HALO)
        y_kinds = 2 if self.both_y else 1
        sizes = [self.y_rows] * y_kinds + [self.z_rows] * 2 + [self.e_rows] * (2 * y_kinds)
        self.starts = [sum(sizes[:i]) for i in range(len(sizes))]
        self.halo_rows = sum(sizes)
        self.y_kinds = y_kinds


def pack_kernel(n, f_ref, eps_ref, *outs):
    own, y_outs, z_outs, e_outs = (
        outs[0],
        outs[1 : 1 + n.y_kinds],
        outs[1 + n.y_kinds : 3 + n.y_kinds],
        outs[3 + n.y_kinds :],
    )
    gz_even = lax.axis_index("gz") % 2 == 0
    dev_even = lax.axis_index("dev") % 2 == 0
    for c in range(7):
        for y in range(n.y):
            value = f_ref[c, y] if c < 6 else COURANT / eps_ref[y]
            own[pl.ds((c * n.y + y) * n.z, n.z), :] = value
    for c in range(7):
        at = lambda y: own[pl.ds((c * n.y + y) * n.z, n.z), :]
        for kind in range(n.y_kinds):
            top = dev_even if kind == 0 else jnp.logical_not(dev_even)
            for r in range(HALO):
                value = jnp.where(top, at(n.y - HALO + r), at(r))
                y_outs[kind][pl.ds((c * HALO + r) * n.z, n.z), :] = value
                for z_kind in range(2):
                    z_top = gz_even if z_kind == 0 else jnp.logical_not(gz_even)
                    edge = jnp.where(z_top, value[n.z - HALO :], value[:HALO])
                    e_outs[kind * 2 + z_kind][pl.ds((c * HALO + r) * HALO, HALO), :] = edge
        for z_kind in range(2):
            z_top = gz_even if z_kind == 0 else jnp.logical_not(gz_even)
            for y in range(n.y):
                value = at(y)
                edge = jnp.where(z_top, value[n.z - HALO :], value[:HALO])
                z_outs[z_kind][pl.ds((c * n.y + y) * HALO, HALO), :] = edge


def table_kernel(n, dir_ref, owner_ref, hi_ref, lo_ref, v_ref, place_ref, count_ref):
    gz, dev, xy = (lax.axis_index(a) for a in ("gz", "dev", "xy"))
    index = dir_ref[...]
    bits = THETAS.bit_length() - 1
    polar = (index >> bits).astype(F32)
    azimuth = (index & (THETAS - 1)).astype(F32)
    sin_t, cos_t = sincos(math.pi * (polar + 0.5) / THETAS)
    sin_f, cos_f = sincos(2.0 * math.pi * azimuth / THETAS)
    kx = WAVE_NUMBER * (sin_t * cos_f)
    ky = WAVE_NUMBER * (sin_t * sin_f)
    kz = WAVE_NUMBER * cos_t
    theta = (cos_t * cos_f, cos_t * sin_f, -sin_t)
    phi = (-sin_f, cos_f, jnp.zeros_like(sin_f))
    is_end = jnp.logical_or(gz == 0, gz == n.gz - 1)
    cap_scale = jnp.where(is_end, n.norm, 0.0).astype(F32)
    x_first = (xy * n.x).astype(F32) - (n.nx - 1) / 2.0
    y_first = (dev * n.y).astype(F32) - (n.ny - 1) / 2.0
    z_first = (gz * n.z).astype(F32) - (n.nz - 1) / 2.0
    x_wall = x_first + jnp.where(xy == 0, XB, n.x - 1 - XB).astype(F32)
    z_cap = z_first + jnp.where(gz == 0, ZB, n.z - 1 - ZB).astype(F32)
    row8 = rows_iota((8, LANES))
    row16 = rows_iota((16, LANES))
    fine_x = row8.astype(F32)
    low = row8 < 4
    comp = row8 & 3

    def weights(rows):
        picked = jnp.where(comp == 2, rows[2], rows[3])
        return jnp.where(comp == 0, rows[0], jnp.where(comp == 1, rows[1], picked))

    for t in range(n.tiles):
        lanes = slice(t * LANES, (t + 1) * LANES)
        a, b, c = (v[t : t + 1, :] for v in (kx, ky, kz))
        th = [v[t : t + 1, :] for v in theta]
        ph = [v[t : t + 1, :] for v in phi]
        sf, cf = sincos(a * fine_x)
        for pair in range(n.x // 16):
            if pair % 8 == 0:
                base_x = x_first + 8.0 * 16.0 * (pair // 8)
                coarse_s, coarse_c = sincos(a * (row16.astype(F32) * 8.0 + base_x))
            cosine, sine = [], []
            for h in (2 * (pair % 8), 2 * (pair % 8) + 1):
                cc, cs = coarse_c[h : h + 1, :], coarse_s[h : h + 1, :]
                cosine.append(cc * cf - cs * sf)
                sine.append(cs * cf + cc * sf)
            for part, rows in ((0, cosine), (n.x, sine)):
                high, rest = split(jnp.concatenate(rows, axis=0))
                hi_ref[part + pair * 16 : part + pair * 16 + 16, lanes] = high
                lo_ref[part + pair * 16 : part + pair * 16 + 16, lanes] = rest
        zs, zc = sincos(c * (row16.astype(F32) + z_first))
        for part, rows in ((2 * n.x, zc), (2 * n.x + n.z, zs)):
            high, rest = split(rows)
            hi_ref[part : part + 16, lanes] = high
            lo_ref[part : part + 16, lanes] = rest
        y_of = comp.astype(F32) + y_first
        base_s, base_c = sincos(b * y_of + jnp.where(low, c * z_cap, a * x_wall))
        for face in range(2):
            i, j = ((0, 1), (1, 2))[face]
            scale = cap_scale if face == 0 else n.norm
            w_theta = weights([-th[i], -th[j], -ph[i], -ph[j]]) * scale
            w_phi = weights([-ph[i], -ph[j], th[i], th[j]]) * scale
            for y in range(n.y):
                r = face * 4 + y
                bc, bs = base_c[r : r + 1, :], base_s[r : r + 1, :]
                one = jnp.where(low, bc, -bs)
                two = jnp.where(low, bs, bc)
                for kind, value in enumerate(
                    (one * w_theta, one * w_phi, two * w_theta, two * w_phi)
                ):
                    at = ((face * 4 + kind) * n.y + y) * 8
                    v_ref[at : at + 8, lanes] = value
    for o in range(n.gz):
        count_ref[o] = 0
    which = jnp.where(gz == 0, 0, 1)

    def place(q, carry):
        owner = owner_ref[which, q]
        rank = count_ref[owner]
        count_ref[owner] = rank + 1
        place_ref[q] = owner * n.chunk + 2 + rank
        return carry

    lax.fori_loop(0, n.caps, place, 0)


def block_transpose(values):
    row, block = rows_iota((8, LANES)), lanes_iota((8, LANES)) // PATCH
    for bit in (1, 2, 4):
        wide = PATCH * bit
        ahead = pltpu.roll(pltpu.roll(values, 8 - bit, 0), wide, 1)
        behind = pltpu.roll(pltpu.roll(values, bit, 0), LANES - wide, 1)
        row_bit, block_bit = (row & bit) != 0, (block & bit) != 0
        moved = jnp.where(row_bit, behind, ahead)
        values = jnp.where(row_bit == block_bit, values, moved)
    return values


def turn(values):
    swapped = pltpu.roll(values, 4, 0)
    return jnp.where(rows_iota(values.shape) < 4, -swapped, swapped)


def main_kernel(
    n, own_ref, other_ref, halo_ref, far_halo_ref, spectra_ref, phase_ref, wall_owner_ref, place_ref,
    hi_ref, lo_ref, v_ref, fields_out, spectra_out, far_out, chunk_out, a_ref, m_ref,
):
    gz, dev, xy = (lax.axis_index(a) for a in ("gz", "dev", "xy"))
    gz_even, dev_even = gz % 2 == 0, dev % 2 == 0
    deep = n.z + 8
    lo_ok, hi_ok = gz > 0, gz < n.gz - 1
    if n.both_y:
        y_own = HALO
        y_slots = (
            (0, jnp.logical_not(dev_even), dev > 0),
            (HALO + n.y, dev_even, dev < n.dev - 1),
        )
    else:
        y_own = jnp.where(dev_even, 0, HALO)
        y_slots = ((jnp.where(dev_even, n.y, 0), None, None),)
    pad = jnp.zeros((8 - 2 * HALO, LANES), F32)

    def choose(ref, starts, use_first, length):
        if use_first is None:
            return ref[pl.ds(starts[0], length), :]
        return jnp.where(
            use_first, ref[pl.ds(starts[0], length), :], ref[pl.ds(starts[1], length), :]
        )

    kinds = n.y_kinds
    for half, (block, halo) in enumerate(((own_ref, halo_ref), (other_ref, far_halo_ref))):
        at_x = xy if half == 0 else 1 - xy
        lanes = pl.ds(pl.multiple_of(at_x * n.x, n.x), n.x)

        def rim(first, second):
            high = jnp.where(gz_even, first, second)
            low = jnp.where(gz_even, second, first)
            return jnp.concatenate(
                [jnp.where(hi_ok, high, 0.0), pad, jnp.where(lo_ok, low, 0.0)], axis=0
            )

        for c in range(7):
            for y in range(n.y):
                a_ref[c, y_own + y, 0 : n.z, lanes] = block[pl.ds((c * n.y + y) * n.z, n.z), :]
                at = (c * n.y + y) * HALO
                first = halo[pl.ds(n.starts[kinds] + at, HALO), :]
                second = halo[pl.ds(n.starts[kinds + 1] + at, HALO), :]
                a_ref[c, y_own + y, n.z : deep, lanes] = rim(first, second)
            for start, use_first, ok in y_slots:
                for r in range(HALO):
                    at = (c * HALO + r) * n.z
                    body = choose(halo, [n.starts[k] + at for k in range(kinds)], use_first, n.z)
                    at = (c * HALO + r) * HALO
                    edges = [
                        choose(
                            halo,
                            [n.starts[kinds + 2 + 2 * k + e] + at for k in range(kinds)],
                            use_first,
                            HALO,
                        )
                        for e in range(2)
                    ]
                    edge = rim(*edges)
                    if ok is not None:
                        body, edge = jnp.where(ok, body, 0.0), jnp.where(ok, edge, 0.0)
                    a_ref[c, start + r, 0 : n.z, lanes] = body
                    a_ref[c, start + r, n.z : deep, lanes] = edge

    shape = (deep, n.nx)
    z_row, x_lane = rows_iota(shape), lanes_iota(shape)
    keep = jnp.where(z_row < n.z + HALO, COURANT, jnp.where(lo_ok & (z_row >= deep - HALO), COURANT, 0.0))
    keep = keep.astype(F32)
    last_x, first_x = x_lane == n.nx - 1, x_lane == 0

    def z_next(v):
        return pltpu.roll(v, deep - 1, 0)

    def z_before(v):
        return pltpu.roll(v, 1, 0)

    def x_next(v):
        return jnp.where(last_x, 0.0, pltpu.roll(v, n.nx - 1, 1))

    def x_before(v):
        return jnp.where(first_x, 0.0, pltpu.roll(v, 1, 1))

    angle_row = rows_iota((8, LANES))
    step_of = (angle_row // 2).astype(F32)
    part_of = jnp.where((angle_row & 1) == 0, 0.5, 1.0)
    sines, cosines = sincos(phase_ref[0] + ANGULAR_STEP * (step_of + part_of))
    own_lanes = pl.ds(pl.multiple_of(xy * n.x, n.x), n.x)
    for step in range(STEPS):
        for y in range(n.rows):
            ex, ey, ez = (a_ref[c, y] for c in range(3))
            if y + 1 < n.rows:
                ex_y, ez_y = a_ref[0, y + 1] - ex, a_ref[2, y + 1] - ez
            else:
                ex_y, ez_y = -ex, -ez
            rate = keep
            if n.both_y and y < HALO:
                rate = jnp.where(dev == 0, 0.0, keep)
            a_ref[3, y] = a_ref[3, y] - rate * (ez_y - (z_next(ey) - ey))
            a_ref[4, y] = a_ref[4, y] - rate * ((z_next(ex) - ex) - (x_next(ez) - ez))
            a_ref[5, y] = a_ref[5, y] - rate * ((x_next(ey) - ey) - ex_y)
        for y in range(n.rows):
            hx, hy, hz = (a_ref[c, y] for c in range(3, 6))
            rate = a_ref[6, y]
            if y > 0:
                hx_y, hz_y = hx - a_ref[3, y - 1], hz - a_ref[5, y - 1]
            else:
                hx_y, hz_y = hx, hz
            a_ref[0, y] = a_ref[0, y] + rate * (hz_y - (hy - z_before(hy)))
            a_ref[1, y] = a_ref[1, y] + rate * ((hx - z_before(hx)) - (hz - x_before(hz)))
            a_ref[2, y] = a_ref[2, y] + rate * ((hy - x_before(hy)) - hx_y)
        source = spectra_ref if step == 0 else spectra_out
        for c in range(6):
            row = 2 * step + (1 if c < 3 else 0)
            cosine, sine = cosines[row : row + 1, :], sines[row : row + 1, :]
            for y in range(n.y):
                value = a_ref[c, y_own + y, 0 : n.z, own_lanes]
                spectra_out[c, y] = source[c, y] + value * cosine
                spectra_out[6 + c, y] = source[6 + c, y] - value * sine
                if step == STEPS - 1:
                    fields_out[c, y] = value

    facing_x = jnp.where(xy == 0, -1.0, 1.0).astype(F32)
    facing_z = jnp.where(gz == 0, -1.0, 1.0).astype(F32)
    row8, lane = rows_iota((8, LANES)), lanes_iota((8, LANES))
    sign = jnp.where(((row8 & 3) == 0) | ((row8 & 3) == 3), -1.0, 1.0).astype(F32)
    own_block = lane // PATCH == row8
    block_sign = jnp.sum(jnp.where(own_block, sign, 0.0), axis=0, keepdims=True)
    cap_left, cap_right, wall_left = [], [], []
    chunk_out[...] = jnp.zeros_like(chunk_out)
    for y in range(n.y):
        plane = [
            jnp.where(gz == 0, spectra_out[p, y, ZB : ZB + 1, :], spectra_out[p, y, n.z - 1 - ZB : n.z - ZB, :])
            for p in [k + 6 * im for im in range(2) for k in Z_PICKS]
        ]
        current = jnp.concatenate(plane, axis=0) * (sign * facing_z)
        cap_left.append(current)
        cap_right.append(turn(current))
        m_ref[y * 8 : y * 8 + 8, :] = block_transpose(current)
        stack = jnp.concatenate(
            [spectra_out[k + 6 * im, y] for im in range(2) for k in X_PICKS], axis=0
        )
        across = stack.T
        record = jnp.where(xy == 0, across[XB : XB + 1, :], across[n.x - 1 - XB : n.x - XB, :])
        record = record * (block_sign * facing_x)
        for o in range(n.gz):
            mine = wall_owner_ref[0, y] == o
            at = o * n.chunk
            chunk_out[at : at + 1, :] += jnp.where(mine, record, 0.0)
            chunk_out[at + 1 : at + 2, :] += jnp.where(mine, 1.0, 0.0).astype(F32)
        spread = jnp.where(own_block, record, 0.0)
        for wide in (16, 32, 64):
            spread = spread + pltpu.roll(spread, wide, 1)
        wall_left.append(jnp.where(lane < n.z, spread, turn(spread))[:, : 2 * n.z])
    for q in range(n.caps):
        chunk_out[pl.ds(place_ref[q], 1), :] = m_ref[q : q + 1, :]
    cap = jnp.concatenate(
        [jnp.concatenate(cap_left, axis=0), jnp.concatenate(cap_right, axis=0)], axis=1
    )
    wall = jnp.concatenate(wall_left, axis=0)
    dot = functools.partial(jnp.dot, preferred_element_type=F32)
    wide = min(512, n.dirs)
    for first in range(0, n.dirs, wide):
        sums = []
        for left, rows in ((cap, slice(0, 2 * n.x)), (wall, slice(2 * n.x, 2 * n.x + 2 * n.z))):
            left_hi, left_lo = split(left)
            high, rest = hi_ref[rows, first : first + wide], lo_ref[rows, first : first + wide]
            sums.append(dot(left_hi, high) + (dot(left_lo, high) + dot(left_hi, rest)))
        for t in range(wide // LANES):
            lanes = slice(first + t * LANES, first + (t + 1) * LANES)
            tile = first // LANES + t
            for kind in range(4):
                total = None
                for face in range(2):
                    for y in range(n.y):
                        at = ((face * 4 + kind) * n.y + y) * 8
                        term = v_ref[at : at + 8, lanes] * sums[face][
                            y * 8 : y * 8 + 8, t * LANES : (t + 1) * LANES
                        ]
                        total = term if total is None else total + term
                far_out[kind * n.tiles + tile : kind * n.tiles + tile + 1, :] = jnp.sum(
                    total, axis=0, keepdims=True
                )


def adjoint_kernel(n, far_ref, target_ref, mask_ref, hi_ref, lo_ref, v_ref, intensity_out, owned_out, adjoint_out):
    gz, dev, xy = (lax.axis_index(a) for a in ("gz", "dev", "xy"))
    block = n.far_rows + n.chunk
    parts = []
    for kind in range(4):
        total = None
        for k in range(n.gz):
            at = k * block + kind * n.tiles
            term = far_ref[at : at + n.tiles, :]
            total = term if total is None else total + term
        parts.append(total)
    theta_re, phi_re, theta_im, phi_im = parts
    intensity = theta_re * theta_re + theta_im * theta_im + phi_re * phi_re + phi_im * phi_im
    intensity_out[...] = intensity
    slope = 2.0 * (mask_ref[...].astype(F32) * (intensity - target_ref[...]))
    slopes = [slope * part for part in parts]

    faces = [[], []]
    for face in range(2):
        for t in range(n.tiles):
            lanes = slice(t * LANES, (t + 1) * LANES)
            rows = []
            for y in range(n.y):
                total = None
                for kind in range(4):
                    at = ((face * 4 + kind) * n.y + y) * 8
                    term = v_ref[at : at + 8, lanes] * slopes[kind][t : t + 1, :]
                    total = term if total is None else total + term
                rows.append(total)
            faces[face].append(jnp.concatenate(rows, axis=0))
    dot = functools.partial(
        lax.dot_general,
        dimension_numbers=(((1,), (1,)), ((), ())),
        preferred_element_type=F32,
    )
    sums = []
    for face, rows in ((0, slice(0, 2 * n.x)), (1, slice(2 * n.x, 2 * n.x + 2 * n.z))):
        left_hi, left_lo = split(jnp.concatenate(faces[face], axis=1))
        high, rest = hi_ref[rows, :], lo_ref[rows, :]
        sums.append(dot(left_hi, high) + (dot(left_lo, high) + dot(left_hi, rest)))
    cap, wall = sums
    row8, lane = rows_iota((8, LANES)), lanes_iota((8, LANES))
    own_block = lane // PATCH == row8
    for y in range(n.y):
        at = slice(y * 8, y * 8 + 8)
        gradient = cap[at, : n.x] - turn(cap[at, n.x :])
        adjoint_out[n.walls + y * 8 : n.walls + y * 8 + 8, :] = block_transpose(gradient)
        gradient = wall[at, : n.z] - turn(wall[at, n.z :])
        spread = jnp.concatenate([gradient] * (LANES // n.z), axis=1)
        adjoint_out[y : y + 1, :] = jnp.sum(
            jnp.where(own_block, spread, 0.0), axis=0, keepdims=True
        )
    walls = [jnp.zeros((1, LANES), F32) for _ in range(n.walls)]
    rank = jnp.zeros((1, LANES), F32)
    for s in range(n.gz):
        at = pl.multiple_of((gz ^ s) * block + n.far_rows, 8)
        rows = far_ref[pl.ds(at, 8), :]
        record, flag = rows[0:1, :], rows[1:2, :] > 0.5
        for r in range(n.walls):
            walls[r] = jnp.where(flag & (rank == float(r)), record, walls[r])
        rank = rank + rows[1:2, :]
    for r in range(n.walls):
        owned_out[r : r + 1, :] = walls[r]
    for cap_at, s in enumerate((0, n.gz - 1)):
        at = pl.multiple_of((gz ^ s) * block + n.far_rows, 8)
        rows = far_ref[pl.ds(at, n.chunk), :]
        owned_out[n.walls + cap_at * n.share : n.walls + (cap_at + 1) * n.share, :] = rows[2 : 2 + n.share, :]


def partner(kind, i, n):
    up = (i % 2 == 0) == (kind == 0)
    return (i + 1) % n if up else (i - 1) % n


def exchange(values, axes, image):
    sizes = [lax.axis_size(a) for a in axes]
    pairs = []
    for source in range(math.prod(sizes)):
        rest, where = source, []
        for size in reversed(sizes):
            where.insert(0, rest % size)
            rest //= size
        target = 0
        for size, at in zip(sizes, image(*where)):
            target = target * size + at
        pairs.append((source, target))
    return lax.ppermute(values, axes if len(axes) > 1 else axes[0], pairs)


def local(
    fields, spectra, permittivity, phase_start, wall_owner, cap_owner, dir_index, target, aim_mask
):
    n = Sizes(permittivity.shape, dir_index.shape[0], cap_owner.shape[1])
    gz = lax.axis_index("gz")

    def out(*shape, dtype=F32):
        return jax.ShapeDtypeStruct(shape, dtype)

    own_rows = 7 * n.y * n.z
    packed = pl.pallas_call(
        functools.partial(pack_kernel, n),
        name="pack",
        out_shape=[out(own_rows, n.x)]
        + [out(n.y_rows, n.x)] * n.y_kinds
        + [out(n.z_rows, n.x)] * 2
        + [out(n.e_rows, n.x)] * (2 * n.y_kinds),
        in_specs=[VMEM] * 2,
        out_specs=[VMEM] * (3 + 3 * n.y_kinds),
    )(fields, permittivity)
    own, y_send = packed[0], packed[1 : 1 + n.y_kinds]
    z_send, e_send = packed[1 + n.y_kinds : 3 + n.y_kinds], packed[3 + n.y_kinds :]
    y_got = [
        exchange(v, ("dev",), lambda d, k=k: (partner(k, d, n.dev),)) for k, v in enumerate(y_send)
    ]
    e_got = [
        exchange(
            v,
            ("gz", "dev"),
            lambda g, d, k=k: (partner(k % 2, g, n.gz), partner(k // 2, d, n.dev)),
        )
        for k, v in enumerate(e_send)
    ]
    z_got = [
        exchange(v, ("gz",), lambda g, k=k: (partner(k, g, n.gz),)) for k, v in enumerate(z_send)
    ]
    other = exchange(own, ("xy",), lambda x: (x ^ 1,))
    halo = jnp.concatenate([*y_got, *z_got, *e_got])
    far_halo = exchange(halo, ("xy",), lambda x: (x ^ 1,))

    table_rows, v_rows = 2 * n.x + 2 * n.z, 8 * n.y * 8
    high, rest, v, place = pl.pallas_call(
        functools.partial(table_kernel, n),
        name="tables",
        out_shape=[
            out(table_rows, n.dirs, dtype=BF16),
            out(table_rows, n.dirs, dtype=BF16),
            out(v_rows, n.dirs),
            out(n.caps, dtype=jnp.int32),
        ],
        in_specs=[VMEM, SMEM],
        out_specs=[VMEM] * 3 + [SMEM],
        scratch_shapes=[pltpu.SMEM((n.gz,), jnp.int32)],
        compiler_params=pltpu.CompilerParams(vmem_limit_bytes=24 << 20),
    )(dir_index.reshape(n.tiles, LANES), cap_owner)

    block = tuple(permittivity.shape)
    fields_out, spectra_out, far, chunk = pl.pallas_call(
        functools.partial(main_kernel, n),
        name="window",
        out_shape=[
            out(6, *block),
            out(12, *block),
            out(n.far_rows, LANES),
            out(n.gz * n.chunk, LANES),
        ],
        in_specs=[VMEM] * 5 + [SMEM] * 3 + [VMEM] * 3,
        out_specs=[VMEM] * 4,
        scratch_shapes=[
            pltpu.VMEM((7, n.rows, n.z + 8, n.nx), F32),
            pltpu.VMEM((n.caps, LANES), F32),
        ],
        compiler_params=pltpu.CompilerParams(vmem_limit_bytes=24 << 20),
    )(own, other, halo, far_halo, spectra, phase_start, wall_owner, place, high, rest, v)

    for axis in ("xy", "dev"):
        size = lax.axis_size(axis)
        got = [exchange(far, (axis,), lambda i, k=k: (i ^ k,)) for k in range(1, size)]
        for term in got:
            far = far + term
    payload = [
        jnp.concatenate([far, lax.dynamic_slice_in_dim(chunk, (gz ^ k) * n.chunk, n.chunk)])
        for k in range(n.gz)
    ]
    got = [exchange(payload[k], ("gz",), lambda g, k=k: (g ^ k,)) for k in range(1, n.gz)]
    gathered = jnp.concatenate([payload[0], *got])

    intensity_all, owned, adjoint = pl.pallas_call(
        functools.partial(adjoint_kernel, n),
        name="adjoint",
        out_shape=[
            out(n.tiles, LANES),
            out(n.walls + 2 * n.share, LANES),
            out(n.walls + n.caps, LANES),
        ],
        in_specs=[VMEM] * 6,
        out_specs=[VMEM] * 3,
        compiler_params=pltpu.CompilerParams(vmem_limit_bytes=24 << 20),
    )(gathered, target.reshape(n.tiles, LANES), aim_mask.reshape(n.tiles, LANES), high, rest, v)
    joined = (gz * n.dev + lax.axis_index("dev")) * n.xy + lax.axis_index("xy")
    share = n.dirs // (n.gz * n.dev * n.xy)
    intensity = lax.dynamic_slice_in_dim(intensity_all.reshape(n.dirs), joined * share, share)
    return fields_out, spectra_out, owned[None, None, None], intensity, adjoint[None, None, None]


def solution(mesh):
    placed = (
        P("groups", "dev", "gz", "xy"),
        P("groups", "dev", "gz", "xy"),
        P(("groups", "dev"), "gz", "xy"),
        P("groups"),
        P("gz", None),
        P(),
        P(),
        P("groups"),
        P("groups"),
    )
    return jax.shard_map(
        local,
        mesh=mesh,
        in_specs=placed,
        out_specs=(
            P("groups", "dev", "gz", "xy"),
            P("groups", "dev", "gz", "xy"),
            P(("groups", "gz"), "dev", "xy", None, None),
            P(("groups", "gz", "dev", "xy")),
            P(("groups", "gz"), "dev", "xy", None, None),
        ),
        check_vma=False,
    )
```

time: 345 us -> 46.6 us (0.14); the launches traced: 338 us -> 46.3 us
  waiting for transfers between devices: 112 us -> 11.4 us
  matrix products: 98.6 us -> 0 us
  blocking collectives: 41.1 us -> 0 us
  starting transfers between devices: 49.7 us -> 15.9 us
  between operations: 17 us -> 1.39 us
  Pallas kernels: 0 us -> 9.53 us
  other arithmetic: 6.95 us -> 0.66 us
  local copies, waits for them, and re-layouts: 12.6 us -> 7.4 us
    dot_general x44 -> x0, matrix products: 98.6 us -> none  [the longest x4 12.3 us: adjoint_block(): jnp.dot(slope_block[:6], cosine_table.T, precision=HIGHEST)]
    psum x1 -> x0, waiting for transfers between devices: 83.9 us -> none  [local(): far_total = lax.psum(partial_far, ('gz', 'dev', 'xy'))]
    psum x2 -> x0, blocking collectives: 41.1 us -> none  [the longest x1 21.6 us: broadcast(): return lax.psum(block, axis)]
    ppermute x18 -> x12, starting transfers between devices: 33.9 us -> 15.9 us  [exchange(): return lax.ppermute(values, axes if len(axes) > 1 else axes[0], pairs)]
    ppermute x18 -> x12, waiting for transfers between devices: 28.3 us -> 11.4 us  [exchange(): return lax.ppermute(values, axes if len(axes) > 1 else axes[0], pairs)]
    all_to_all x3 -> x0, starting transfers between devices: 15.8 us -> none  [the longest x1 6.32 us: local(): lax.all_to_all(send_meta, 'gz', split_axis=0, concat_axis=0, tiled=True)]
    pallas_call x0 -> x4, Pallas kernels: none -> 9.53 us  [the longest x1 3.3 us: local(): pl.pallas_call(functools.partial(main_kernel, n), name='window', out_shap...]
  transfers between devices with their start and end apart: 22 -> 12, of which waited for: 12 -> 7; matrix products, arithmetic and copies ran while one was open for 2% -> 0% of each run, Pallas kernels for 0% -> 7%
where the time goes in v1:
time: 46.6 us; the launch traced here: 46.3 us
  starting transfers between devices  15.9 us (34%)
  waiting for transfers between devices  11.4 us (24%)
  Pallas kernels  9.53 us (20%)
  local copies, waits for them, and re-layouts  7.4 us (16%)
  between operations  1.39 us (3%)
  other arithmetic  0.66 us (1%)
    ppermute x12, starting transfers between devices, exchange(): return lax.ppermute(values, axes if len(axes) > 1 else axes[0], pairs)  15.9 us
    ppermute x12, waiting for transfers between devices, exchange(): return lax.ppermute(values, axes if len(axes) > 1 else axes[0], pairs)  11.4 us
    unnamed x26, local copies, waits for them, and re-layouts  6.8 us
    pallas_call x1, Pallas kernels, local(): pl.pallas_call(functools.partial(main_kernel, n), name='window', out_shap...  3.3 us
    pallas_call x1, Pallas kernels, local(): pl.pallas_call(functools.partial(table_kernel, n), name='tables', out_sha...  3.06 us
    pallas_call x1, Pallas kernels, local(): pl.pallas_call(functools.partial(pack_kernel, n), name='pack', out_shape=...  1.74 us
    pallas_call x1, Pallas kernels, local(): pl.pallas_call(functools.partial(adjoint_kernel, n), name='adjoint', out_...  1.43 us
  transfers between devices with their start and end apart: 12, of which 7 were waited for; matrix products, arithmetic and copies ran while one was open for 0% of the time, Pallas kernels for 7%

profile of v1, /device:TPU:0, one launch (start us, length us, event | category | flops | bytes accessed | tf_op | source)
XLA Modules:
  0.0 46.3 jit_solution(15223346032678203674)
XLA Ops:
  0.6 1.7 %pack.1 = (f32[448,128]{1,0:T(8,128)}, f32[336,128]{1,0:T(8,128)}, f32[88,128]{1,0:T(8,128)}, f32[88,128]{1,0:T(8,128)}, f32[64,128]{1,0:T(8,128)}, /*index=5*/f32[64,128]{1,0:T(8,128)}) custom-call(f32[6,4,16,128]{3,2,1,0:T(8,128)} %f_ref.1, f32[4,16,128]{2,1,0:T(8,128)} %eps_ref.1), custom_call_target="tpu_custom_call" | custom-call | tf_op jit(solution)/shard_map/pack/pallas_call | solution.py:509
  2.4 2.9 %collective-permute-start.1 = (f32[336,128]{1,0:T(8,128)}, f32[336,128]{1,0:T(8,128)S(1)}, u32[]{:S(2)}, u32[]{:S(2)}) collective-permute-start(f32[336,128]{1,0:T(8,128)} %get-tuple-element.23), channel_id=1, source_target_pairs={{0,2},{2,0},{1,3},{3,1},{4,6},{6,4},{5,7},{7,5},{8,10},{10,8},{9,1... | collective-permute-start | bytes 516104 | tf_op jit(solution)/shard_map/ppermute | solution.py:496
  5.3 1.6 %collective-permute-start.2 = (f32[88,128]{1,0:T(8,128)}, f32[88,128]{1,0:T(8,128)S(1)}, u32[]{:S(2)}, u32[]{:S(2)}) collective-permute-start(f32[88,128]{1,0:T(8,128)} %get-tuple-element.24), channel_id=1, source_target_pairs={{0,4},{4,0},{8,12},{12,8},{1,5},{5,1},{9,13},{13,9},{2,6},{6,2},{1... | collective-permute-start | bytes 135176 | tf_op jit(solution)/shard_map/ppermute | solution.py:496
  6.9 2.5 %collective-permute-start.3 = (f32[88,128]{1,0:T(8,128)}, f32[88,128]{1,0:T(8,128)S(1)}, u32[]{:S(2)}, u32[]{:S(2)}) collective-permute-start(f32[88,128]{1,0:T(8,128)} %get-tuple-element.25), channel_id=1, source_target_pairs={{0,12},{4,8},{8,4},{12,0},{1,13},{5,9},{9,5},{13,1},{2,14},{6,10},... | collective-permute-start | bytes 135176 | tf_op jit(solution)/shard_map/ppermute | solution.py:496
  9.4 0.6 %collective-permute-start.4 = (f32[64,128]{1,0:T(8,128)}, f32[64,128]{1,0:T(8,128)S(1)}, u32[]{:S(2)}, u32[]{:S(2)}) collective-permute-start(f32[64,128]{1,0:T(8,128)} %get-tuple-element.26), channel_id=1, source_target_pairs={{0,6},{2,4},{4,2},{6,0},{8,14},{10,12},{12,10},{14,8},{1,7},{3,5},... | collective-permute-start | bytes 98312 | tf_op jit(solution)/shard_map/ppermute | solution.py:496
  10.0 1.8 %collective-permute-start.5 = (f32[64,128]{1,0:T(8,128)}, f32[64,128]{1,0:T(8,128)S(1)}, u32[]{:S(2)}, u32[]{:S(2)}) collective-permute-start(f32[64,128]{1,0:T(8,128)} %get-tuple-element.27), channel_id=1, source_target_pairs={{0,14},{2,12},{4,10},{6,8},{8,6},{10,4},{12,2},{14,0},{1,15},{3,13... | collective-permute-start | bytes 98312 | tf_op jit(solution)/shard_map/ppermute | solution.py:496
  11.8 0.0 collective-permute-done.1
  11.9 0.0 collective-permute-done.2
  11.9 1.1 %collective-permute-done.3 = f32[88,128]{1,0:T(8,128)S(1)} collective-permute-done((f32[88,128]{1,0:T(8,128)}, f32[88,128]{1,0:T(8,128)S(1)}, u32[]{:S(2)}, u32[]{:S(2)}) %collective-permute-start.3) | collective-permute-done | bytes 45088 | tf_op jit(solution)/shard_map/ppermute | solution.py:496
  12.9 1.8 %collective-permute-done.4 = f32[64,128]{1,0:T(8,128)S(1)} collective-permute-done((f32[64,128]{1,0:T(8,128)}, f32[64,128]{1,0:T(8,128)S(1)}, u32[]{:S(2)}, u32[]{:S(2)}) %collective-permute-start.4) | collective-permute-done | bytes 32800 | tf_op jit(solution)/shard_map/ppermute | solution.py:496
  14.7 2.1 %collective-permute-done.5 = f32[64,128]{1,0:T(8,128)S(1)} collective-permute-done((f32[64,128]{1,0:T(8,128)}, f32[64,128]{1,0:T(8,128)S(1)}, u32[]{:S(2)}, u32[]{:S(2)}) %collective-permute-start.5) | collective-permute-done | bytes 32800 | tf_op jit(solution)/shard_map/ppermute | solution.py:496
  16.8 0.0 collective-permute-start.6
  16.8 0.5 %collective-permute-start = (f32[448,128]{1,0:T(8,128)}, f32[448,128]{1,0:T(8,128)S(1)}, u32[]{:S(2)}, u32[]{:S(2)}) collective-permute-start(f32[448,128]{1,0:T(8,128)} %get-tuple-element.22.own_ref), channel_id=1, source_target_pairs={{0,1},{1,0},{2,3},{3,2},{4,5},{5,4},{6,7},{7,6},{8,9},{9,8},{10,11... | collective-permute-start | bytes 688136 | tf_op jit(solution)/shard_map/ppermute | solution.py:496
  18.0 0.0 copy-start.6
  18.0 0.7 %copy-done.6 = s32[2048]{0:T(1024)S(1)} copy-done((s32[2048]{0:T(1024)S(1)}, s32[2048]{0:T(1024)}, u32[]{:S(2)}) %copy-start.6) | copy-done | bytes 8216
  18.7 0.0 copy-start.7
  18.7 0.7 %copy-done.7 = s32[2,32]{1,0:T(2,128)S(1)} copy-done((s32[2,32]{1,0:T(2,128)S(1)}, s32[2,32]{1,0:T(2,128)}, u32[]{:S(2)}) %copy-start.7) | copy-done | bytes 280
  19.4 3.1 %tables.1 = (bf16[288,2048]{1,0:T(8,128)(2,1)S(1)}, bf16[288,2048]{1,0:T(8,128)(2,1)S(1)}, f32[256,2048]{1,0:T(8,128)S(1)}, s32[32]{0:T(128)S(1)}) custom-call(s32[16,128]{1,0:T(8,128)S(1)} %bitcast.10, s32[2,32]{1,0:T(2,128)S(1)} %copy-done.7), custom_call_target="tpu_custom_call" | custom-call | tf_op jit(solution)/shard_map/tables/pallas_call | solution.py:540
  22.5 0.0 copy-start
  22.5 0.0 collective-permute-done.other_ref
  22.5 0.0 collective-permute-done.6.far_halo_ref
  22.5 0.0 copy-start.2
  22.5 1.3 %copy-done.2 = f32[12,4,16,128]{3,2,1,0:T(8,128)S(1)} copy-done((f32[12,4,16,128]{3,2,1,0:T(8,128)S(1)}, f32[12,4,16,128]{3,2,1,0:T(8,128)}, u32[]{:S(2)}) %copy-start.2) | copy-done | bytes 393240
  23.8 0.9 %copy-done.3 = f32[448,128]{1,0:T(8,128)S(1)} copy-done((f32[448,128]{1,0:T(8,128)S(1)}, f32[448,128]{1,0:T(8,128)}, u32[]{:S(2)}) %copy-start.3) | copy-done | bytes 229400
  24.7 0.0 copy-start.8
  24.7 0.7 %copy-done.8 = s32[1,4]{1,0:T(1,128)S(1)} copy-done((s32[1,4]{1,0:T(1,128)S(1)}, s32[1,4]{1,0:T(1,128)}, u32[]{:S(2)}) %copy-start.8) | copy-done | bytes 40
  25.4 0.0 copy-start.4
  25.4 3.3 %window.1 = (f32[6,4,16,128]{3,2,1,0:T(8,128)}, f32[12,4,16,128]{3,2,1,0:T(8,128)}, f32[64,128]{1,0:T(8,128)S(1)}, f32[64,128]{1,0:T(8,128)S(1)}) custom-call(f32[448,128]{1,0:T(8,128)S(1)} %copy-done.3, f32[448,128]{1,0:T(8,128)S(1)} %collective-permute-done.other_ref, f32[640,128]{1,0:T(8,128)S(1)} %constant_dynamic-update-slice_fusion.halo_ref, ...), custom_call_target="tpu_custom_call" | custom-call | tf_op jit(solution)/shard_map/window/pallas_call | solution.py:556
  28.7 0.0 copy-done
  28.7 0.1 collective-permute-start.7
  28.8 1.1 %collective-permute-done.7 = f32[64,128]{1,0:T(8,128)S(1)} collective-permute-done((f32[64,128]{1,0:T(8,128)S(1)}, f32[64,128]{1,0:T(8,128)S(1)}, u32[]{:S(2)}, u32[]{:S(2)}) %collective-permute-start.7) | collective-permute-done | bytes 32800 | tf_op jit(solution)/shard_map/ppermute | solution.py:496
  29.9 1.5 %collective-permute-start.8 = (f32[64,128]{1,0:T(8,128)S(1)}, f32[64,128]{1,0:T(8,128)S(1)}, u32[]{:S(2)}, u32[]{:S(2)}) collective-permute-start(f32[64,128]{1,0:T(8,128)S(1)} %add.27), channel_id=1, source_target_pairs={{0,2},{2,0},{1,3},{3,1},{4,6},{6,4},{5,7},{7,5},{8,10},{10,8},{9,1... | collective-permute-start | bytes 98312 | tf_op jit(solution)/shard_map/ppermute | solution.py:496
  31.4 2.4 %collective-permute-done.8 = f32[64,128]{1,0:T(8,128)S(1)} collective-permute-done((f32[64,128]{1,0:T(8,128)S(1)}, f32[64,128]{1,0:T(8,128)S(1)}, u32[]{:S(2)}, u32[]{:S(2)}) %collective-permute-start.8) | collective-permute-done | bytes 32800 | tf_op jit(solution)/shard_map/ppermute | solution.py:496
  33.8 0.6 %pad_maximum_fusion = (f32[80,128]{1,0:T(8,128)S(1)}, f32[80,128]{1,0:T(8,128)}, f32[80,128]{1,0:T(8,128)}) fusion(f32[64,128]{1,0:T(8,128)S(1)} %get-tuple-element.45, f32[16,128]{1,0:T(8,128)S(1)} %get-tuple-element.49, f32[16,128]{1,0:T(8,128)S(1)} %get-tuple-element.50, f32[16,128]{1,0:T(8,128)S(1)} %get-tuple-element.51), kind=kLoop, calls=%fused_computation | loop fusion | flops 30720 | bytes 180224 | tf_op jit(solution)/shard_map/concatenate | solution.py:580
  34.5 0.0 collective-permute-start.9
  34.5 1.5 %collective-permute-start.10 = (f32[80,128]{1,0:T(8,128)}, f32[80,128]{1,0:T(8,128)S(1)}, u32[]{:S(2)}, u32[]{:S(2)}) collective-permute-start(f32[80,128]{1,0:T(8,128)} %get-tuple-element.47), channel_id=1, source_target_pairs={{0,8},{4,12},{8,0},{12,4},{1,9},{5,13},{9,1},{13,5},{2,10},{6,14},... | collective-permute-start | bytes 122888 | tf_op jit(solution)/shard_map/ppermute | solution.py:496
  36.0 2.9 %collective-permute-start.11 = (f32[80,128]{1,0:T(8,128)S(1)}, f32[80,128]{1,0:T(8,128)S(1)}, u32[]{:S(2)}, u32[]{:S(2)}) collective-permute-start(f32[80,128]{1,0:T(8,128)S(1)} %get-tuple-element.46), channel_id=1, source_target_pairs={{0,12},{4,8},{8,4},{12,0},{1,13},{5,9},{9,5},{13,1},{2,14},{6,10},... | collective-permute-start | bytes 122888 | tf_op jit(solution)/shard_map/ppermute | solution.py:496
  38.9 0.0 collective-permute-done.9
  38.9 0.8 %collective-permute-done.10 = f32[80,128]{1,0:T(8,128)S(1)} collective-permute-done((f32[80,128]{1,0:T(8,128)}, f32[80,128]{1,0:T(8,128)S(1)}, u32[]{:S(2)}, u32[]{:S(2)}) %collective-permute-start.10) | collective-permute-done | bytes 40992 | tf_op jit(solution)/shard_map/ppermute | solution.py:496
  39.7 2.0 %collective-permute-done.11 = f32[80,128]{1,0:T(8,128)S(1)} collective-permute-done((f32[80,128]{1,0:T(8,128)S(1)}, f32[80,128]{1,0:T(8,128)S(1)}, u32[]{:S(2)}, u32[]{:S(2)}) %collective-permute-start.11) | collective-permute-done | bytes 40992 | tf_op jit(solution)/shard_map/ppermute | solution.py:496
  41.8 0.0 copy-done.4
  41.8 0.0 copy-done.5
  41.8 0.0 copy-start.1
  41.8 1.3 %copy-done.1 = bf16[288,2048]{1,0:T(8,128)(2,1)S(1)} copy-done((bf16[288,2048]{1,0:T(8,128)(2,1)S(1)}, bf16[288,2048]{1,0:T(8,128)(2,1)}, u32[]{:S(2)}) %copy-start.1) | copy-done | bytes 1179672
  43.0 1.4 %adjoint.1 = (f32[16,128]{1,0:T(8,128)S(1)}, f32[20,128]{1,0:T(8,128)S(1)}, f32[36,128]{1,0:T(8,128)S(1)}) custom-call(f32[320,128]{1,0:T(8,128)S(1)} %constant_dynamic-update-slice_fusion.5.far_ref, f32[16,128]{1,0:T(8,128)S(1)} %bitcast.8, s32[16,128]{1,0:T(8,128)S(1)} %bitcast.9, bf16[288,2048]{1,0:T(8,128)(2,1)S(1)} %get-tuple-element.29.hi_ref, ...), custom_call_target="tpu_custom_call" | custom-call | tf_op jit(solution)/shard_map/adjoint/pallas_call | solution.py:586
  44.5 0.6 %copy.15 = f32[1,1,1,36,128]{4,2,3,1,0:T(1,128)} copy(f32[1,1,1,36,128]{4,3,2,1,0:T(8,128)S(1)} %bitcast.6) | data formatting | bytes 36864
  45.1 0.6 %copy.14 = f32[1,1,1,20,128]{4,2,3,1,0:T(1,128)} copy(f32[1,1,1,20,128]{4,3,2,1,0:T(8,128)S(1)} %bitcast.7) | data formatting | bytes 20480
  45.7 0.6 %dynamic_slice.19 = f32[128]{0:T(128)} dynamic-slice(f32[2048]{0:T(1024)S(1)} %bitcast.11, s32[]{:T(128)S(6)} %select_n.19), dynamic_slice_sizes={128} | dynamic-slice | bytes 1028 | tf_op jit(solution)/shard_map/dynamic_slice | solution.py:600
  (13 shorter events, 0.1 us)
Async XLA Ops:
  2.4 9.5 %collective-permute-start.1 = (f32[336,128]{1,0:T(8,128)}, f32[336,128]{1,0:T(8,128)S(1)}, u32[]{:S(2)}, u32[]{:S(2)}) collective-permute-start(f32[336,128]{1,0:T(8,128)} %get-tuple-element.23), channel_id=1, source_target_pairs={{0,2},{2,0},{1,3},{3,1},{4,6},{6,4},{5,7},{7,5},{8,10},{10,8},{9,1... | collective-permute-start | bytes 516104 | tf_op jit(solution)/shard_map/ppermute | solution.py:496
  5.3 6.6 %collective-permute-start.2 = (f32[88,128]{1,0:T(8,128)}, f32[88,128]{1,0:T(8,128)S(1)}, u32[]{:S(2)}, u32[]{:S(2)}) collective-permute-start(f32[88,128]{1,0:T(8,128)} %get-tuple-element.24), channel_id=1, source_target_pairs={{0,4},{4,0},{8,12},{12,8},{1,5},{5,1},{9,13},{13,9},{2,6},{6,2},{1... | collective-permute-start | bytes 135176 | tf_op jit(solution)/shard_map/ppermute | solution.py:496
  6.9 6.1 %collective-permute-start.3 = (f32[88,128]{1,0:T(8,128)}, f32[88,128]{1,0:T(8,128)S(1)}, u32[]{:S(2)}, u32[]{:S(2)}) collective-permute-start(f32[88,128]{1,0:T(8,128)} %get-tuple-element.25), channel_id=1, source_target_pairs={{0,12},{4,8},{8,4},{12,0},{1,13},{5,9},{9,5},{13,1},{2,14},{6,10},... | collective-permute-start | bytes 135176 | tf_op jit(solution)/shard_map/ppermute | solution.py:496
  9.4 5.4 %collective-permute-start.4 = (f32[64,128]{1,0:T(8,128)}, f32[64,128]{1,0:T(8,128)S(1)}, u32[]{:S(2)}, u32[]{:S(2)}) collective-permute-start(f32[64,128]{1,0:T(8,128)} %get-tuple-element.26), channel_id=1, source_target_pairs={{0,6},{2,4},{4,2},{6,0},{8,14},{10,12},{12,10},{14,8},{1,7},{3,5},... | collective-permute-start | bytes 98312 | tf_op jit(solution)/shard_map/ppermute | solution.py:496
  10.0 6.8 %collective-permute-start.5 = (f32[64,128]{1,0:T(8,128)}, f32[64,128]{1,0:T(8,128)S(1)}, u32[]{:S(2)}, u32[]{:S(2)}) collective-permute-start(f32[64,128]{1,0:T(8,128)} %get-tuple-element.27), channel_id=1, source_target_pairs={{0,14},{2,12},{4,10},{6,8},{8,6},{10,4},{12,2},{14,0},{1,15},{3,13... | collective-permute-start | bytes 98312 | tf_op jit(solution)/shard_map/ppermute | solution.py:496
  16.8 5.6 %collective-permute-start.6 = (f32[640,128]{1,0:T(8,128)S(1)}, f32[640,128]{1,0:T(8,128)S(1)}, u32[]{:S(2)}, u32[]{:S(2)}) collective-permute-start(f32[640,128]{1,0:T(8,128)S(1)} %constant_dynamic-update-slice_fusion.halo_ref), channel_id=1, source_target_pairs={{0,1},{1,0},{2,3},{3,2},{4,5},{5,4},{6,7},{7,6},{8,9},{9,8},{10,11... | collective-permute-start | bytes 983048 | tf_op jit(solution)/shard_map/ppermute | solution.py:496
  16.8 5.6 %collective-permute-start = (f32[448,128]{1,0:T(8,128)}, f32[448,128]{1,0:T(8,128)S(1)}, u32[]{:S(2)}, u32[]{:S(2)}) collective-permute-start(f32[448,128]{1,0:T(8,128)} %get-tuple-element.22.own_ref), channel_id=1, source_target_pairs={{0,1},{1,0},{2,3},{3,2},{4,5},{5,4},{6,7},{7,6},{8,9},{9,8},{10,11... | collective-permute-start | bytes 688136 | tf_op jit(solution)/shard_map/ppermute | solution.py:496
  18.0 0.7 %copy-start.6 = (s32[2048]{0:T(1024)S(1)}, s32[2048]{0:T(1024)}, u32[]{:S(2)}) copy-start(s32[2048]{0:T(1024)} %param.15) | copy-start | bytes 24580
  18.7 0.7 %copy-start.7 = (s32[2,32]{1,0:T(2,128)S(1)}, s32[2,32]{1,0:T(2,128)}, u32[]{:S(2)}) copy-start(s32[2,32]{1,0:T(2,128)} %owner_ref.1) | copy-start | bytes 772
  22.5 6.2 %copy-start = (bf16[288,2048]{1,0:T(8,128)(2,1)}, bf16[288,2048]{1,0:T(8,128)(2,1)S(1)}, u32[]{:S(2)}) copy-start(bf16[288,2048]{1,0:T(8,128)(2,1)S(1)} %get-tuple-element.30.lo_ref) | copy-start | bytes 3538948
  22.5 1.3 %copy-start.2 = (f32[12,4,16,128]{3,2,1,0:T(8,128)S(1)}, f32[12,4,16,128]{3,2,1,0:T(8,128)}, u32[]{:S(2)}) copy-start(f32[12,4,16,128]{3,2,1,0:T(8,128)} %spectra_ref.1) | copy-start | bytes 1179652
  23.8 0.9 %copy-start.3 = (f32[448,128]{1,0:T(8,128)S(1)}, f32[448,128]{1,0:T(8,128)}, u32[]{:S(2)}) copy-start(f32[448,128]{1,0:T(8,128)} %get-tuple-element.22.own_ref) | copy-start | bytes 688132
  24.7 0.7 %copy-start.8 = (s32[1,4]{1,0:T(1,128)S(1)}, s32[1,4]{1,0:T(1,128)}, u32[]{:S(2)}) copy-start(s32[1,4]{1,0:T(1,128)} %wall_owner_ref.1) | copy-start | bytes 52
  25.4 16.4 %copy-start.4 = (f32[2048]{0:T(1024)S(1)}, f32[2048]{0:T(1024)}, u32[]{:S(2)}) copy-start(f32[2048]{0:T(1024)} %param.16) | copy-start | bytes 24580
  25.4 16.4 %copy-start.5 = (s32[2048]{0:T(1024)S(1)}, s32[2048]{0:T(1024)}, u32[]{:S(2)}) copy-start(s32[2048]{0:T(1024)} %param.17) | copy-start | bytes 24580
  28.7 1.2 %collective-permute-start.7 = (f32[64,128]{1,0:T(8,128)S(1)}, f32[64,128]{1,0:T(8,128)S(1)}, u32[]{:S(2)}, u32[]{:S(2)}) collective-permute-start(f32[64,128]{1,0:T(8,128)S(1)} %get-tuple-element.34), channel_id=1, source_target_pairs={{0,1},{1,0},{2,3},{3,2},{4,5},{5,4},{6,7},{7,6},{8,9},{9,8},{10,11... | collective-permute-start | bytes 98312 | tf_op jit(solution)/shard_map/ppermute | solution.py:496
  29.9 3.9 %collective-permute-start.8 = (f32[64,128]{1,0:T(8,128)S(1)}, f32[64,128]{1,0:T(8,128)S(1)}, u32[]{:S(2)}, u32[]{:S(2)}) collective-permute-start(f32[64,128]{1,0:T(8,128)S(1)} %add.27), channel_id=1, source_target_pairs={{0,2},{2,0},{1,3},{3,1},{4,6},{6,4},{5,7},{7,5},{8,10},{10,8},{9,1... | collective-permute-start | bytes 98312 | tf_op jit(solution)/shard_map/ppermute | solution.py:496
  34.5 4.4 %collective-permute-start.9 = (f32[80,128]{1,0:T(8,128)}, f32[80,128]{1,0:T(8,128)S(1)}, u32[]{:S(2)}, u32[]{:S(2)}) collective-permute-start(f32[80,128]{1,0:T(8,128)} %get-tuple-element.48), channel_id=1, source_target_pairs={{0,4},{4,0},{8,12},{12,8},{1,5},{5,1},{9,13},{13,9},{2,6},{6,2},{1... | collective-permute-start | bytes 122888 | tf_op jit(solution)/shard_map/ppermute | solution.py:496
  34.5 5.2 %collective-permute-start.10 = (f32[80,128]{1,0:T(8,128)}, f32[80,128]{1,0:T(8,128)S(1)}, u32[]{:S(2)}, u32[]{:S(2)}) collective-permute-start(f32[80,128]{1,0:T(8,128)} %get-tuple-element.47), channel_id=1, source_target_pairs={{0,8},{4,12},{8,0},{12,4},{1,9},{5,13},{9,1},{13,5},{2,10},{6,14},... | collective-permute-start | bytes 122888 | tf_op jit(solution)/shard_map/ppermute | solution.py:496
  36.0 5.8 %collective-permute-start.11 = (f32[80,128]{1,0:T(8,128)S(1)}, f32[80,128]{1,0:T(8,128)S(1)}, u32[]{:S(2)}, u32[]{:S(2)}) collective-permute-start(f32[80,128]{1,0:T(8,128)S(1)} %get-tuple-element.46), channel_id=1, source_target_pairs={{0,12},{4,8},{8,4},{12,0},{1,13},{5,9},{9,5},{13,1},{2,14},{6,10},... | collective-permute-start | bytes 122888 | tf_op jit(solution)/shard_map/ppermute | solution.py:496
  41.8 1.3 %copy-start.1 = (bf16[288,2048]{1,0:T(8,128)(2,1)S(1)}, bf16[288,2048]{1,0:T(8,128)(2,1)}, u32[]{:S(2)}) copy-start(bf16[288,2048]{1,0:T(8,128)(2,1)} %copy-done) | copy-start | bytes 3538948

commit v2 on v1

--- a/solution.py
+++ b/solution.py
@@ -72,9 +72,11 @@
         self.nx, self.ny, self.nz = self.x * self.xy, self.y * self.dev, self.z * self.gz
         self.dirs = directions
         self.tiles = directions // LANES
+        self.table_rows = 2 * self.x + 2 * self.z
         self.walls = self.y * self.z // PATCH
         self.caps = caps
         self.share = caps // self.gz
+        self.own_dirs = directions // (self.gz * self.dev * self.xy)
         self.chunk = up8(2 + self.share)
         self.far_rows = 4 * self.tiles
         self.norm = 1.0 / math.sqrt(2.0 * (2 * self.ny * self.nz + 2 * self.ny * self.nx))
@@ -82,46 +84,55 @@
         self.z_rows = up8(7 * self.y * HALO)
         self.e_rows = up8(7 * HALO * HALO)
         y_kinds = 2 if self.both_y else 1
-        sizes = [self.y_rows] * y_kinds + [self.z_rows] * 2 + [self.e_rows] * (2 * y_kinds)
+        sizes = [self.y_rows] * y_kinds + [2 * self.z_rows] + [2 * self.e_rows] * y_kinds
         self.starts = [sum(sizes[:i]) for i in range(len(sizes))]
         self.halo_rows = sum(sizes)
         self.y_kinds = y_kinds
 
 
-def pack_kernel(n, f_ref, eps_ref, *outs):
-    own, y_outs, z_outs, e_outs = (
-        outs[0],
-        outs[1 : 1 + n.y_kinds],
-        outs[1 + n.y_kinds : 3 + n.y_kinds],
-        outs[3 + n.y_kinds :],
-    )
-    gz_even = lax.axis_index("gz") % 2 == 0
+def pack_kernel(n, f_ref, eps_ref, own, *y_outs):
     dev_even = lax.axis_index("dev") % 2 == 0
     for c in range(7):
+        at = []
         for y in range(n.y):
             value = f_ref[c, y] if c < 6 else COURANT / eps_ref[y]
             own[pl.ds((c * n.y + y) * n.z, n.z), :] = value
-    for c in range(7):
-        at = lambda y: own[pl.ds((c * n.y + y) * n.z, n.z), :]
+            at.append(value)
         for kind in range(n.y_kinds):
             top = dev_even if kind == 0 else jnp.logical_not(dev_even)
             for r in range(HALO):
-                value = jnp.where(top, at(n.y - HALO + r), at(r))
+                value = jnp.where(top, at[n.y - HALO + r], at[r])
                 y_outs[kind][pl.ds((c * HALO + r) * n.z, n.z), :] = value
-                for z_kind in range(2):
-                    z_top = gz_even if z_kind == 0 else jnp.logical_not(gz_even)
-                    edge = jnp.where(z_top, value[n.z - HALO :], value[:HALO])
-                    e_outs[kind * 2 + z_kind][pl.ds((c * HALO + r) * HALO, HALO), :] = edge
-        for z_kind in range(2):
-            z_top = gz_even if z_kind == 0 else jnp.logical_not(gz_even)
+
+
+def edge_kernel(n, own_ref, other_ref, z_out, *e_outs):
+    xy = lax.axis_index("xy")
+    dev_even = lax.axis_index("dev") % 2 == 0
+    z_top = lax.axis_index("gz") % 2 == xy % 2
+    for half in range(2):
+        mine = xy == half
+
+        def at(c, y):
+            rows = pl.ds((c * n.y + y) * n.z, n.z)
+            value = jnp.where(mine, own_ref[rows, :], other_ref[rows, :])
+            return jnp.where(z_top, value[n.z - HALO :], value[:HALO])
+
+        for c in range(7):
+            edges = [at(c, y) for y in range(n.y)]
             for y in range(n.y):
-                value = at(y)
-                edge = jnp.where(z_top, value[n.z - HALO :], value[:HALO])
-                z_outs[z_kind][pl.ds((c * n.y + y) * HALO, HALO), :] = edge
-
-
-def table_kernel(n, dir_ref, owner_ref, hi_ref, lo_ref, v_ref, place_ref, count_ref):
+                z_out[pl.ds(half * n.z_rows + (c * n.y + y) * HALO, HALO), :] = edges[y]
+            for kind in range(n.y_kinds):
+                top = dev_even if kind == 0 else jnp.logical_not(dev_even)
+                for r in range(HALO):
+                    edge = jnp.where(top, edges[n.y - HALO + r], edges[r])
+                    e_outs[kind][pl.ds(half * n.e_rows + (c * HALO + r) * HALO, HALO), :] = edge
+
+
+def table_kernel(
+    n, dir_ref, owner_ref, wall_owner_ref, phase_ref, hi_lo_ref, v_ref, place_ref, turn_ref, count_ref
+):
     gz, dev, xy = (lax.axis_index(a) for a in ("gz", "dev", "xy"))
+    hi_ref, lo_ref = halves(n, hi_lo_ref)
     index = dir_ref[...]
     bits = THETAS.bit_length() - 1
     polar = (index >> bits).astype(F32)
@@ -184,12 +195,9 @@
             for y in range(n.y):
                 r = face * 4 + y
                 bc, bs = base_c[r : r + 1, :], base_s[r : r + 1, :]
-                one = jnp.where(low, bc, -bs)
-                two = jnp.where(low, bs, bc)
-                for kind, value in enumerate(
-                    (one * w_theta, one * w_phi, two * w_theta, two * w_phi)
-                ):
-                    at = ((face * 4 + kind) * n.y + y) * 8
+                factor = jnp.where(low, bc, -bs)
+                for kind, value in enumerate((factor * w_theta, factor * w_phi)):
+                    at = ((face * 2 + kind) * n.y + y) * 8
                     v_ref[at : at + 8, lanes] = value
     for o in range(n.gz):
         count_ref[o] = 0
@@ -203,6 +211,17 @@
         return carry
 
     lax.fori_loop(0, n.caps, place, 0)
+    for j in range(n.walls):
+        place_ref[n.caps + j] = wall_owner_ref[0, j]
+    step_of = (row8 // 2).astype(F32)
+    part_of = jnp.where((row8 & 1) == 0, 0.5, 1.0)
+    sines, cosines = sincos(phase_ref[0] + ANGULAR_STEP * (step_of + part_of))
+    turn_ref[0:8, :] = cosines
+    turn_ref[8:16, :] = sines
+
+
+def halves(n, hi_lo_ref):
+    return hi_lo_ref.at[0 : n.table_rows], hi_lo_ref.at[n.table_rows : 2 * n.table_rows]
 
 
 def block_transpose(values):
@@ -223,9 +242,12 @@
 
 
 def main_kernel(
-    n, own_ref, other_ref, halo_ref, far_halo_ref, spectra_ref, phase_ref, wall_owner_ref, place_ref,
-    hi_ref, lo_ref, v_ref, fields_out, spectra_out, far_out, chunk_out, a_ref, m_ref,
+    n, own_ref, other_ref, halo_ref, far_halo_ref, spectra_hbm, place_ref, turn_ref, hi_lo_ref, v_ref,
+    fields_hbm, spectra_out_hbm, far_out, chunk_out, a_ref, m_ref, fields_out, spectra_out, sems,
 ):
+    hi_ref, lo_ref = halves(n, hi_lo_ref)
+    spectra_in = pltpu.make_async_copy(spectra_hbm, spectra_out, sems.at[0])
+    spectra_in.start()
     gz, dev, xy = (lax.axis_index(a) for a in ("gz", "dev", "xy"))
     gz_even, dev_even = gz % 2 == 0, dev % 2 == 0
     deep = n.z + 8
@@ -240,6 +262,7 @@
         y_own = jnp.where(dev_even, 0, HALO)
         y_slots = ((jnp.where(dev_even, n.y, 0), None, None),)
     pad = jnp.zeros((8 - 2 * HALO, LANES), F32)
+    near_is_high = gz % 2 == xy % 2
 
     def choose(ref, starts, use_first, length):
         if use_first is None:
@@ -248,43 +271,41 @@
             use_first, ref[pl.ds(starts[0], length), :], ref[pl.ds(starts[1], length), :]
         )
 
+    def rim(near, far):
+        high = jnp.where(near_is_high, near, far)
+        low = jnp.where(near_is_high, far, near)
+        return jnp.concatenate(
+            [jnp.where(hi_ok, high, 0.0), pad, jnp.where(lo_ok, low, 0.0)], axis=0
+        )
+
     kinds = n.y_kinds
+    both = (halo_ref, far_halo_ref)
     for half, (block, halo) in enumerate(((own_ref, halo_ref), (other_ref, far_halo_ref))):
         at_x = xy if half == 0 else 1 - xy
         lanes = pl.ds(pl.multiple_of(at_x * n.x, n.x), n.x)
-
-        def rim(first, second):
-            high = jnp.where(gz_even, first, second)
-            low = jnp.where(gz_even, second, first)
-            return jnp.concatenate(
-                [jnp.where(hi_ok, high, 0.0), pad, jnp.where(lo_ok, low, 0.0)], axis=0
-            )
-
         for c in range(7):
             for y in range(n.y):
                 a_ref[c, y_own + y, 0 : n.z, lanes] = block[pl.ds((c * n.y + y) * n.z, n.z), :]
-                at = (c * n.y + y) * HALO
-                first = halo[pl.ds(n.starts[kinds] + at, HALO), :]
-                second = halo[pl.ds(n.starts[kinds + 1] + at, HALO), :]
-                a_ref[c, y_own + y, n.z : deep, lanes] = rim(first, second)
             for start, use_first, ok in y_slots:
                 for r in range(HALO):
                     at = (c * HALO + r) * n.z
                     body = choose(halo, [n.starts[k] + at for k in range(kinds)], use_first, n.z)
-                    at = (c * HALO + r) * HALO
-                    edges = [
-                        choose(
-                            halo,
-                            [n.starts[kinds + 2 + 2 * k + e] + at for k in range(kinds)],
-                            use_first,
-                            HALO,
-                        )
-                        for e in range(2)
-                    ]
-                    edge = rim(*edges)
                     if ok is not None:
-                        body, edge = jnp.where(ok, body, 0.0), jnp.where(ok, edge, 0.0)
+                        body = jnp.where(ok, body, 0.0)
                     a_ref[c, start + r, 0 : n.z, lanes] = body
+    for half in range(2):
+        lanes = slice(half * n.x, (half + 1) * n.x)
+        for c in range(7):
+            for y in range(n.y):
+                at = n.starts[kinds] + half * n.z_rows + (c * n.y + y) * HALO
+                a_ref[c, y_own + y, n.z : deep, lanes] = rim(*(ref[pl.ds(at, HALO), :] for ref in both))
+            for start, use_first, ok in y_slots:
+                for r in range(HALO):
+                    at = half * n.e_rows + (c * HALO + r) * HALO
+                    starts = [n.starts[kinds + 1 + k] + at for k in range(kinds)]
+                    edge = rim(*(choose(ref, starts, use_first, HALO) for ref in both))
+                    if ok is not None:
+                        edge = jnp.where(ok, edge, 0.0)
                     a_ref[c, start + r, n.z : deep, lanes] = edge
 
     shape = (deep, n.nx)
@@ -305,10 +326,6 @@
     def x_before(v):
         return jnp.where(first_x, 0.0, pltpu.roll(v, 1, 1))
 
-    angle_row = rows_iota((8, LANES))
-    step_of = (angle_row // 2).astype(F32)
-    part_of = jnp.where((angle_row & 1) == 0, 0.5, 1.0)
-    sines, cosines = sincos(phase_ref[0] + ANGULAR_STEP * (step_of + part_of))
     own_lanes = pl.ds(pl.multiple_of(xy * n.x, n.x), n.x)
     for step in range(STEPS):
         for y in range(n.rows):
@@ -333,17 +350,24 @@
             a_ref[0, y] = a_ref[0, y] + rate * (hz_y - (hy - z_before(hy)))
             a_ref[1, y] = a_ref[1, y] + rate * ((hx - z_before(hx)) - (hz - x_before(hz)))
             a_ref[2, y] = a_ref[2, y] + rate * ((hy - x_before(hy)) - hx_y)
-        source = spectra_ref if step == 0 else spectra_out
+        if step == 0:
+            spectra_in.wait()
         for c in range(6):
             row = 2 * step + (1 if c < 3 else 0)
-            cosine, sine = cosines[row : row + 1, :], sines[row : row + 1, :]
+            cosine, sine = turn_ref[row : row + 1, :], turn_ref[8 + row : 9 + row, :]
             for y in range(n.y):
                 value = a_ref[c, y_own + y, 0 : n.z, own_lanes]
-                spectra_out[c, y] = source[c, y] + value * cosine
-                spectra_out[6 + c, y] = source[6 + c, y] - value * sine
+                spectra_out[c, y] = spectra_out[c, y] + value * cosine
+                spectra_out[6 + c, y] = spectra_out[6 + c, y] - value * sine
                 if step == STEPS - 1:
                     fields_out[c, y] = value
 
+    copies = (
+        pltpu.make_async_copy(fields_out, fields_hbm, sems.at[1]),
+        pltpu.make_async_copy(spectra_out, spectra_out_hbm, sems.at[2]),
+    )
+    for copy in copies:
+        copy.start()
     facing_x = jnp.where(xy == 0, -1.0, 1.0).astype(F32)
     facing_z = jnp.where(gz == 0, -1.0, 1.0).astype(F32)
     row8, lane = rows_iota((8, LANES)), lanes_iota((8, LANES))
@@ -368,7 +392,7 @@
         record = jnp.where(xy == 0, across[XB : XB + 1, :], across[n.x - 1 - XB : n.x - XB, :])
         record = record * (block_sign * facing_x)
         for o in range(n.gz):
-            mine = wall_owner_ref[0, y] == o
+            mine = place_ref[n.caps + y] == o
             at = o * n.chunk
             chunk_out[at : at + 1, :] += jnp.where(mine, record, 0.0)
             chunk_out[at + 1 : at + 2, :] += jnp.where(mine, 1.0, 0.0).astype(F32)
@@ -393,21 +417,26 @@
         for t in range(wide // LANES):
             lanes = slice(first + t * LANES, first + (t + 1) * LANES)
             tile = first // LANES + t
-            for kind in range(4):
-                total = None
-                for face in range(2):
-                    for y in range(n.y):
-                        at = ((face * 4 + kind) * n.y + y) * 8
-                        term = v_ref[at : at + 8, lanes] * sums[face][
-                            y * 8 : y * 8 + 8, t * LANES : (t + 1) * LANES
-                        ]
-                        total = term if total is None else total + term
-                far_out[kind * n.tiles + tile : kind * n.tiles + tile + 1, :] = jnp.sum(
-                    total, axis=0, keepdims=True
-                )
-
-
-def adjoint_kernel(n, far_ref, target_ref, mask_ref, hi_ref, lo_ref, v_ref, intensity_out, owned_out, adjoint_out):
+            totals = [None] * 4
+            for face in range(2):
+                for y in range(n.y):
+                    rows = sums[face][y * 8 : y * 8 + 8, t * LANES : (t + 1) * LANES]
+                    turned = -turn(rows)
+                    for kind in range(4):
+                        at = ((face * 2 + kind % 2) * n.y + y) * 8
+                        term = v_ref[at : at + 8, lanes] * (rows if kind < 2 else turned)
+                        totals[kind] = term if totals[kind] is None else totals[kind] + term
+            for kind, total in enumerate(totals):
+                at = kind * n.tiles + tile
+                far_out[at : at + 1, :] = jnp.sum(total, axis=0, keepdims=True)
+    for copy in copies:
+        copy.wait()
+
+
+def adjoint_kernel(
+    n, far_ref, target_ref, mask_ref, hi_lo_ref, v_ref, intensity_out, owned_out, adjoint_out, all_ref
+):
+    hi_ref, lo_ref = halves(n, hi_lo_ref)
     gz, dev, xy = (lax.axis_index(a) for a in ("gz", "dev", "xy"))
     block = n.far_rows + n.chunk
     parts = []
@@ -420,7 +449,12 @@
         parts.append(total)
     theta_re, phi_re, theta_im, phi_im = parts
     intensity = theta_re * theta_re + theta_im * theta_im + phi_re * phi_re + phi_im * phi_im
-    intensity_out[...] = intensity
+    if n.own_dirs % LANES == 0:
+        all_ref[...] = intensity
+        first = ((gz * n.dev + dev) * n.xy + xy) * (n.own_dirs // LANES)
+        intensity_out[...] = all_ref[pl.ds(first, n.own_dirs // LANES), :]
+    else:
+        intensity_out[...] = intensity
     slope = 2.0 * (mask_ref[...].astype(F32) * (intensity - target_ref[...]))
     slopes = [slope * part for part in parts]
 
@@ -430,12 +464,12 @@
             lanes = slice(t * LANES, (t + 1) * LANES)
             rows = []
             for y in range(n.y):
-                total = None
-                for kind in range(4):
-                    at = ((face * 4 + kind) * n.y + y) * 8
-                    term = v_ref[at : at + 8, lanes] * slopes[kind][t : t + 1, :]
-                    total = term if total is None else total + term
-                rows.append(total)
+                at = (face * 2 * n.y + y) * 8
+                one, two = v_ref[at : at + 8, lanes], v_ref[at + n.y * 8 : at + n.y * 8 + 8, lanes]
+                even, odd = (
+                    one * slopes[k][t : t + 1, :] + two * slopes[k + 1][t : t + 1, :] for k in (0, 2)
+                )
+                rows.append(even + turn(odd))
             faces[face].append(jnp.concatenate(rows, axis=0))
     dot = functools.partial(
         lax.dot_general,
@@ -453,10 +487,10 @@
     for y in range(n.y):
         at = slice(y * 8, y * 8 + 8)
         gradient = cap[at, : n.x] - turn(cap[at, n.x :])
-        adjoint_out[n.walls + y * 8 : n.walls + y * 8 + 8, :] = block_transpose(gradient)
+        adjoint_out[n.walls + y * 8 : n.walls + y * 8 + 8, 0, :] = block_transpose(gradient)
         gradient = wall[at, : n.z] - turn(wall[at, n.z :])
         spread = jnp.concatenate([gradient] * (LANES // n.z), axis=1)
-        adjoint_out[y : y + 1, :] = jnp.sum(
+        adjoint_out[y, :, :] = jnp.sum(
             jnp.where(own_block, spread, 0.0), axis=0, keepdims=True
         )
     walls = [jnp.zeros((1, LANES), F32) for _ in range(n.walls)]
@@ -469,11 +503,11 @@
             walls[r] = jnp.where(flag & (rank == float(r)), record, walls[r])
         rank = rank + rows[1:2, :]
     for r in range(n.walls):
-        owned_out[r : r + 1, :] = walls[r]
+        owned_out[r, :, :] = walls[r]
     for cap_at, s in enumerate((0, n.gz - 1)):
         at = pl.multiple_of((gz ^ s) * block + n.far_rows, 8)
         rows = far_ref[pl.ds(at, n.chunk), :]
-        owned_out[n.walls + cap_at * n.share : n.walls + (cap_at + 1) * n.share, :] = rows[2 : 2 + n.share, :]
+        owned_out[n.walls + cap_at * n.share : n.walls + (cap_at + 1) * n.share, 0, :] = rows[2 : 2 + n.share, :]
 
 
 def partner(kind, i, n):
@@ -505,54 +539,60 @@
     def out(*shape, dtype=F32):
         return jax.ShapeDtypeStruct(shape, dtype)
 
-    own_rows = 7 * n.y * n.z
-    packed = pl.pallas_call(
+    def params(mebibytes):
+        return pltpu.CompilerParams(vmem_limit_bytes=mebibytes << 20)
+
+    own, *y_send = pl.pallas_call(
         functools.partial(pack_kernel, n),
         name="pack",
-        out_shape=[out(own_rows, n.x)]
-        + [out(n.y_rows, n.x)] * n.y_kinds
-        + [out(n.z_rows, n.x)] * 2
-        + [out(n.e_rows, n.x)] * (2 * n.y_kinds),
+        out_shape=[out(7 * n.y * n.z, n.x)] + [out(n.y_rows, n.x)] * n.y_kinds,
         in_specs=[VMEM] * 2,
-        out_specs=[VMEM] * (3 + 3 * n.y_kinds),
+        out_specs=[VMEM] * (1 + n.y_kinds),
+        compiler_params=params(4),
     )(fields, permittivity)
-    own, y_send = packed[0], packed[1 : 1 + n.y_kinds]
-    z_send, e_send = packed[1 + n.y_kinds : 3 + n.y_kinds], packed[3 + n.y_kinds :]
     y_got = [
         exchange(v, ("dev",), lambda d, k=k: (partner(k, d, n.dev),)) for k, v in enumerate(y_send)
     ]
+    other = exchange(own, ("xy",), lambda x: (x ^ 1,))
+    z_send, *e_send = pl.pallas_call(
+        functools.partial(edge_kernel, n),
+        name="edges",
+        out_shape=[out(2 * n.z_rows, n.x)] + [out(2 * n.e_rows, n.x)] * n.y_kinds,
+        in_specs=[VMEM] * 2,
+        out_specs=[VMEM] * (1 + n.y_kinds),
+        compiler_params=params(4),
+    )(own, other)
+    z_got = exchange(z_send, ("gz", "xy"), lambda g, x: (partner(x, g, n.gz), x))
     e_got = [
         exchange(
             v,
-            ("gz", "dev"),
-            lambda g, d, k=k: (partner(k % 2, g, n.gz), partner(k // 2, d, n.dev)),
+            ("gz", "dev", "xy"),
+            lambda g, d, x, k=k: (partner(x, g, n.gz), partner(k, d, n.dev), x),
         )
         for k, v in enumerate(e_send)
     ]
-    z_got = [
-        exchange(v, ("gz",), lambda g, k=k: (partner(k, g, n.gz),)) for k, v in enumerate(z_send)
-    ]
-    other = exchange(own, ("xy",), lambda x: (x ^ 1,))
-    halo = jnp.concatenate([*y_got, *z_got, *e_got])
-    far_halo = exchange(halo, ("xy",), lambda x: (x ^ 1,))
-
-    table_rows, v_rows = 2 * n.x + 2 * n.z, 8 * n.y * 8
-    high, rest, v, place = pl.pallas_call(
+
+    table, v, place, turns = pl.pallas_call(
         functools.partial(table_kernel, n),
         name="tables",
         out_shape=[
-            out(table_rows, n.dirs, dtype=BF16),
-            out(table_rows, n.dirs, dtype=BF16),
-            out(v_rows, n.dirs),
-            out(n.caps, dtype=jnp.int32),
+            out(2 * n.table_rows, n.dirs, dtype=BF16),
+            out(4 * n.y * 8, n.dirs),
+            out(n.caps + n.walls, dtype=jnp.int32),
+            out(16, LANES),
         ],
-        in_specs=[VMEM, SMEM],
-        out_specs=[VMEM] * 3 + [SMEM],
+        in_specs=[VMEM] + [SMEM] * 3,
+        out_specs=[VMEM] * 2 + [SMEM, VMEM],
         scratch_shapes=[pltpu.SMEM((n.gz,), jnp.int32)],
-        compiler_params=pltpu.CompilerParams(vmem_limit_bytes=24 << 20),
-    )(dir_index.reshape(n.tiles, LANES), cap_owner)
+        compiler_params=params(8),
+        cost_estimate=pl.CostEstimate(flops=1 << 33, bytes_accessed=16 << 20, transcendentals=0),
+    )(dir_index.reshape(n.tiles, LANES), cap_owner, wall_owner, phase_start)
+    (*y_got, z_got, turns), e_got = lax.optimization_barrier(((*y_got, z_got, turns), e_got))
+    halo = jnp.concatenate([*y_got, z_got, *e_got])
+    far_halo = exchange(halo, ("xy",), lambda x: (x ^ 1,))
 
     block = tuple(permittivity.shape)
+    anywhere = pl.BlockSpec(memory_space=pl.ANY)
     fields_out, spectra_out, far, chunk = pl.pallas_call(
         functools.partial(main_kernel, n),
         name="window",
@@ -562,14 +602,17 @@
             out(n.far_rows, LANES),
             out(n.gz * n.chunk, LANES),
         ],
-        in_specs=[VMEM] * 5 + [SMEM] * 3 + [VMEM] * 3,
-        out_specs=[VMEM] * 4,
+        in_specs=[VMEM] * 4 + [anywhere, SMEM] + [VMEM] * 3,
+        out_specs=[anywhere] * 2 + [VMEM] * 2,
         scratch_shapes=[
             pltpu.VMEM((7, n.rows, n.z + 8, n.nx), F32),
             pltpu.VMEM((n.caps, LANES), F32),
+            pltpu.VMEM((6, *block), F32),
+            pltpu.VMEM((12, *block), F32),
+            pltpu.SemaphoreType.DMA((3,)),
         ],
-        compiler_params=pltpu.CompilerParams(vmem_limit_bytes=24 << 20),
-    )(own, other, halo, far_halo, spectra, phase_start, wall_owner, place, high, rest, v)
+        compiler_params=params(12),
+    )(own, other, halo, far_halo, spectra, place, turns, table, v)
 
     for axis in ("xy", "dev"):
         size = lax.axis_size(axis)
@@ -583,22 +626,26 @@
     got = [exchange(payload[k], ("gz",), lambda g, k=k: (g ^ k,)) for k in range(1, n.gz)]
     gathered = jnp.concatenate([payload[0], *got])
 
-    intensity_all, owned, adjoint = pl.pallas_call(
+    sliced = n.own_dirs % LANES == 0
+    intensity, owned, adjoint = pl.pallas_call(
         functools.partial(adjoint_kernel, n),
         name="adjoint",
         out_shape=[
-            out(n.tiles, LANES),
-            out(n.walls + 2 * n.share, LANES),
-            out(n.walls + n.caps, LANES),
+            out(n.own_dirs // LANES if sliced else n.tiles, LANES),
+            out(n.walls + 2 * n.share, 1, LANES),
+            out(n.walls + n.caps, 1, LANES),
         ],
-        in_specs=[VMEM] * 6,
+        in_specs=[VMEM] * 5,
         out_specs=[VMEM] * 3,
-        compiler_params=pltpu.CompilerParams(vmem_limit_bytes=24 << 20),
-    )(gathered, target.reshape(n.tiles, LANES), aim_mask.reshape(n.tiles, LANES), high, rest, v)
-    joined = (gz * n.dev + lax.axis_index("dev")) * n.xy + lax.axis_index("xy")
-    share = n.dirs // (n.gz * n.dev * n.xy)
-    intensity = lax.dynamic_slice_in_dim(intensity_all.reshape(n.dirs), joined * share, share)
-    return fields_out, spectra_out, owned[None, None, None], intensity, adjoint[None, None, None]
+        scratch_shapes=[pltpu.VMEM((n.tiles, LANES), F32)],
+        compiler_params=params(8),
+    )(gathered, target.reshape(n.tiles, LANES), aim_mask.reshape(n.tiles, LANES), table, v)
+    intensity = intensity.reshape(-1)
+    if not sliced:
+        joined = (gz * n.dev + lax.axis_index("dev")) * n.xy + lax.axis_index("xy")
+        intensity = lax.dynamic_slice_in_dim(intensity, joined * n.own_dirs, n.own_dirs)
+    shape = (1, 1, 1, -1, LANES)
+    return fields_out, spectra_out, owned.reshape(shape), intensity, adjoint.reshape(shape)
 
 
 def solution(mesh):

time: 46.6 us -> 37.4 us (0.80)
  local copies, waits for them, and re-layouts: 7.4 us -> 3.77 us
  starting transfers between devices: 15.9 us -> 13.2 us
  waiting for transfers between devices: 11.4 us -> 10.1 us
  Pallas kernels: 9.53 us -> 8.58 us
  other arithmetic: 0.66 us -> 0.02 us
    unnamed x26 -> x20, local copies, waits for them, and re-layouts: 6.8 us -> 3.75 us
    ppermute x12 -> x10, starting transfers between devices: 15.9 us -> 13.2 us  [exchange(): return lax.ppermute(values, axes if len(axes) > 1 else axes[0], pairs)]
    pallas_call x1, Pallas kernels: 1.74 us -> 0.03 us  [local(): pl.pallas_call(functools.partial(pack_kernel, n), name='pack', out_shape=...]
    ppermute x12 -> x10, waiting for transfers between devices: 11.4 us -> 10.1 us  [exchange(): return lax.ppermute(values, axes if len(axes) > 1 else axes[0], pairs)]
    concatenate x1, other arithmetic: 0.64 us -> 0.01 us  [local(): jnp.concatenate([far, lax.dynamic_slice_in_dim(chunk, (gz ^ k) * n.chunk,...]
    dynamic_slice x1 -> x0, local copies, waits for them, and re-layouts: 0.58 us -> none  [local(): lax.dynamic_slice_in_dim(intensity_all.reshape(n.dirs), joined * share, s...]
    pallas_call x1, Pallas kernels: 1.43 us -> 1.99 us  [local(): pl.pallas_call(functools.partial(adjoint_kernel, n), name='adjoint', out_...]
  transfers between devices with their start and end apart: 12 -> 10, of which waited for: 7 -> 5; matrix products, arithmetic and copies ran while one was open for 0% -> 0% of each run, Pallas kernels for 7% -> 8%
where the time goes in v2:
time: 37.4 us; the launch traced here: 37.1 us
  starting transfers between devices  13.2 us (35%)
  waiting for transfers between devices  10.1 us (27%)
  Pallas kernels  8.58 us (23%)
  local copies, waits for them, and re-layouts  3.77 us (10%)
  between operations  1.42 us (4%)
    ppermute x10, starting transfers between devices, exchange(): return lax.ppermute(values, axes if len(axes) > 1 else axes[0], pairs)  13.2 us
    ppermute x10, waiting for transfers between devices, exchange(): return lax.ppermute(values, axes if len(axes) > 1 else axes[0], pairs)  10.1 us
    unnamed x20, local copies, waits for them, and re-layouts  3.75 us
    pallas_call x1, Pallas kernels, local(): pl.pallas_call(functools.partial(main_kernel, n), name='window', out_shap...  3.54 us
    pallas_call x1, Pallas kernels, local(): pl.pallas_call(functools.partial(table_kernel, n), name='tables', out_sha...  2.95 us
    pallas_call x1, Pallas kernels, local(): pl.pallas_call(functools.partial(adjoint_kernel, n), name='adjoint', out_...  1.99 us
  transfers between devices with their start and end apart: 10, of which 5 were waited for; matrix products, arithmetic and copies ran while one was open for 0% of the time, Pallas kernels for 8%

profile of v2, /device:TPU:0, one launch (start us, length us, event | category | flops | bytes accessed | tf_op | source)
XLA Modules:
  0.0 37.1 jit_solution(17292463279365575931)
XLA Ops:
  0.6 0.0 copy-start.1
  0.6 0.9 %copy-done.1 = f32[6,4,16,128]{3,2,1,0:T(8,128)S(1)} copy-done((f32[6,4,16,128]{3,2,1,0:T(8,128)S(1)}, f32[6,4,16,128]{3,2,1,0:T(8,128)}, u32[]{:S(2)}) %copy-start.1) | copy-done | bytes 196632
  1.6 0.0 copy-start.2
  1.6 0.8 %copy-done.2 = f32[4,16,128]{2,1,0:T(8,128)S(1)} copy-done((f32[4,16,128]{2,1,0:T(8,128)S(1)}, f32[4,16,128]{2,1,0:T(8,128)}, u32[]{:S(2)}) %copy-start.2) | copy-done | bytes 32792
  2.4 0.5 %collective-permute-start = (f32[448,128]{1,0:T(8,128)S(1)}, f32[448,128]{1,0:T(8,128)S(1)}, u32[]{:S(2)}, u32[]{:S(2)}) collective-permute-start(f32[448,128]{1,0:T(8,128)S(1)} %get-tuple-element.24.own_ref), channel_id=1, source_target_pairs={{0,1},{1,0},{2,3},{3,2},{4,5},{5,4},{6,7},{7,6},{8,9},{9,8},{10,11... | collective-permute-start | bytes 688136 | tf_op jit(solution)/shard_map/ppermute | solution.py:530
  2.9 2.6 %collective-permute-start.1 = (f32[336,128]{1,0:T(8,128)S(1)}, f32[336,128]{1,0:T(8,128)S(1)}, u32[]{:S(2)}, u32[]{:S(2)}) collective-permute-start(f32[336,128]{1,0:T(8,128)S(1)} %get-tuple-element.25), channel_id=1, source_target_pairs={{0,2},{2,0},{1,3},{3,1},{4,6},{6,4},{5,7},{7,5},{8,10},{10,8},{9,1... | collective-permute-start | bytes 516104 | tf_op jit(solution)/shard_map/ppermute | solution.py:530
  6.1 0.0 collective-permute-done.other_ref
  6.1 0.1 edges.1
  6.2 1.6 %collective-permute-start.2 = (f32[176,128]{1,0:T(8,128)S(1)}, f32[176,128]{1,0:T(8,128)S(1)}, u32[]{:S(2)}, u32[]{:S(2)}) collective-permute-start(f32[176,128]{1,0:T(8,128)S(1)} %get-tuple-element.26), channel_id=1, source_target_pairs={{0,4},{1,13},{4,0},{5,9},{8,12},{9,5},{12,8},{13,1},{2,6},{3,15},{... | collective-permute-start | bytes 270344 | tf_op jit(solution)/shard_map/ppermute | solution.py:530
  7.8 0.6 %collective-permute-start.3 = (f32[128,128]{1,0:T(8,128)S(1)}, f32[128,128]{1,0:T(8,128)S(1)}, u32[]{:S(2)}, u32[]{:S(2)}) collective-permute-start(f32[128,128]{1,0:T(8,128)S(1)} %get-tuple-element.28), channel_id=1, source_target_pairs={{0,6},{1,15},{2,4},{3,13},{4,2},{5,11},{6,0},{7,9},{8,14},{9,7},{1... | collective-permute-start | bytes 196616 | tf_op jit(solution)/shard_map/ppermute | solution.py:530
  8.4 0.0 copy-start.5
  8.4 0.7 %copy-done.5 = s32[2048]{0:T(1024)S(1)} copy-done((s32[2048]{0:T(1024)S(1)}, s32[2048]{0:T(1024)}, u32[]{:S(2)}) %copy-start.5) | copy-done | bytes 8216
  9.1 0.0 copy-start.6
  9.1 0.7 %copy-done.6 = s32[2,32]{1,0:T(2,128)S(1)} copy-done((s32[2,32]{1,0:T(2,128)S(1)}, s32[2,32]{1,0:T(2,128)}, u32[]{:S(2)}) %copy-start.6) | copy-done | bytes 280
  9.8 0.0 copy-start.7
  9.8 0.7 %copy-done.7 = s32[1,4]{1,0:T(1,128)S(1)} copy-done((s32[1,4]{1,0:T(1,128)S(1)}, s32[1,4]{1,0:T(1,128)}, u32[]{:S(2)}) %copy-start.7) | copy-done | bytes 40
  10.5 0.0 copy-start
  10.5 3.0 %tables.1 = (bf16[576,2048]{1,0:T(8,128)(2,1)S(1)}, f32[128,2048]{1,0:T(8,128)S(1)}, s32[36]{0:T(128)S(1)}, f32[16,128]{1,0:T(8,128)S(1)}) custom-call(s32[16,128]{1,0:T(8,128)S(1)} %bitcast.12, s32[2,32]{1,0:T(2,128)S(1)} %copy-done.6, s32[1,4]{1,0:T(1,128)S(1)} %copy-done.7, f32[1]{0:T(128)S(6)} %copy.22.phase_ref), custom_call_target="tpu_custom_call" | custom-call | flops 8589934592 | bytes 16777216 | tf_op jit(solution)/shard_map/tables/pallas_call | solution.py:575
  13.4 0.0 collective-permute-done.1
  13.4 0.0 collective-permute-done.3
  13.5 0.0 collective-permute-done.2
  13.5 2.1 %collective-permute-start.4 = (f32[640,128]{1,0:T(8,128)S(1)}, f32[640,128]{1,0:T(8,128)S(1)}, u32[]{:S(2)}, u32[]{:S(2)}) collective-permute-start(f32[640,128]{1,0:T(8,128)S(1)} %constant_dynamic-update-slice_fusion.halo_ref), channel_id=1, source_target_pairs={{0,1},{1,0},{2,3},{3,2},{4,5},{5,4},{6,7},{7,6},{8,9},{9,8},{10,11... | collective-permute-start | bytes 983048 | tf_op jit(solution)/shard_map/ppermute | solution.py:530
  15.7 1.3 %collective-permute-done.4.far_halo_ref = f32[640,128]{1,0:T(8,128)S(1)} collective-permute-done((f32[640,128]{1,0:T(8,128)S(1)}, f32[640,128]{1,0:T(8,128)S(1)}, u32[]{:S(2)}, u32[]{:S(2)}) %collective-permute-start.4) | collective-permute-done | bytes 327712 | tf_op jit(solution)/shard_map/ppermute | solution.py:530
  16.9 0.0 copy-done
  16.9 0.0 copy-start.3
  16.9 0.0 copy-start.4
  16.9 3.5 %window.1 = (f32[6,4,16,128]{3,2,1,0:T(8,128)}, f32[12,4,16,128]{3,2,1,0:T(8,128)}, f32[64,128]{1,0:T(8,128)S(1)}, f32[64,128]{1,0:T(8,128)S(1)}) custom-call(f32[448,128]{1,0:T(8,128)S(1)} %get-tuple-element.24.own_ref, f32[448,128]{1,0:T(8,128)S(1)} %collective-permute-done.other_ref, f32[640,128]{1,0:T(8,128)S(1)} %constant_dynamic-update-slice_fusion.halo_ref, ...), custom_call_target="tpu_custom_call" | custom-call | tf_op jit(solution)/shard_map/window/pallas_call | solution.py:596
  20.5 0.5 %collective-permute-start.5 = (f32[64,128]{1,0:T(8,128)S(1)}, f32[64,128]{1,0:T(8,128)S(1)}, u32[]{:S(2)}, u32[]{:S(2)}) collective-permute-start(f32[64,128]{1,0:T(8,128)S(1)} %get-tuple-element.38), channel_id=1, source_target_pairs={{0,1},{1,0},{2,3},{3,2},{4,5},{5,4},{6,7},{7,6},{8,9},{9,8},{10,11... | collective-permute-start | bytes 98312 | tf_op jit(solution)/shard_map/ppermute | solution.py:530
  20.9 0.9 %collective-permute-done.5 = f32[64,128]{1,0:T(8,128)S(1)} collective-permute-done((f32[64,128]{1,0:T(8,128)S(1)}, f32[64,128]{1,0:T(8,128)S(1)}, u32[]{:S(2)}, u32[]{:S(2)}) %collective-permute-start.5) | collective-permute-done | bytes 32800 | tf_op jit(solution)/shard_map/ppermute | solution.py:530
  21.8 0.8 %collective-permute-start.6 = (f32[64,128]{1,0:T(8,128)S(1)}, f32[64,128]{1,0:T(8,128)S(1)}, u32[]{:S(2)}, u32[]{:S(2)}) collective-permute-start(f32[64,128]{1,0:T(8,128)S(1)} %add.18), channel_id=1, source_target_pairs={{0,2},{2,0},{1,3},{3,1},{4,6},{6,4},{5,7},{7,5},{8,10},{10,8},{9,1... | collective-permute-start | bytes 98312 | tf_op jit(solution)/shard_map/ppermute | solution.py:530
  22.6 3.1 %collective-permute-done.6 = f32[64,128]{1,0:T(8,128)S(1)} collective-permute-done((f32[64,128]{1,0:T(8,128)S(1)}, f32[64,128]{1,0:T(8,128)S(1)}, u32[]{:S(2)}, u32[]{:S(2)}) %collective-permute-start.6) | collective-permute-done | bytes 32800 | tf_op jit(solution)/shard_map/ppermute | solution.py:530
  25.7 0.1 collective-permute-start.7
  25.8 3.5 %collective-permute-start.8 = (f32[80,128]{1,0:T(8,128)S(1)}, f32[80,128]{1,0:T(8,128)S(1)}, u32[]{:S(2)}, u32[]{:S(2)}) collective-permute-start(f32[80,128]{1,0:T(8,128)S(1)} %get-tuple-element.51), channel_id=1, source_target_pairs={{0,8},{4,12},{8,0},{12,4},{1,9},{5,13},{9,1},{13,5},{2,10},{6,14},... | collective-permute-start | bytes 122888 | tf_op jit(solution)/shard_map/ppermute | solution.py:530
  29.3 0.9 %collective-permute-start.9 = (f32[80,128]{1,0:T(8,128)S(1)}, f32[80,128]{1,0:T(8,128)S(1)}, u32[]{:S(2)}, u32[]{:S(2)}) collective-permute-start(f32[80,128]{1,0:T(8,128)S(1)} %get-tuple-element.50), channel_id=1, source_target_pairs={{0,12},{4,8},{8,4},{12,0},{1,13},{5,9},{9,5},{13,1},{2,14},{6,10},... | collective-permute-start | bytes 122888 | tf_op jit(solution)/shard_map/ppermute | solution.py:530
  30.2 0.0 collective-permute-done.7
  30.2 1.1 %collective-permute-done.8 = f32[80,128]{1,0:T(8,128)S(1)} collective-permute-done((f32[80,128]{1,0:T(8,128)S(1)}, f32[80,128]{1,0:T(8,128)S(1)}, u32[]{:S(2)}, u32[]{:S(2)}) %collective-permute-start.8) | collective-permute-done | bytes 40992 | tf_op jit(solution)/shard_map/ppermute | solution.py:530
  31.3 3.8 %collective-permute-done.9 = f32[80,128]{1,0:T(8,128)S(1)} collective-permute-done((f32[80,128]{1,0:T(8,128)S(1)}, f32[80,128]{1,0:T(8,128)S(1)}, u32[]{:S(2)}, u32[]{:S(2)}) %collective-permute-start.9) | collective-permute-done | bytes 40992 | tf_op jit(solution)/shard_map/ppermute | solution.py:530
  35.1 0.0 copy-done.3
  35.1 0.0 copy-done.4
  35.1 2.0 %adjoint.1 = (f32[1,128]{1,0:T(1,128)}, f32[20,1,128]{2,1,0:T(1,128)}, f32[36,1,128]{2,1,0:T(1,128)}) custom-call(f32[320,128]{1,0:T(8,128)S(1)} %constant_dynamic-update-slice_fusion.3.far_ref, f32[16,128]{1,0:T(8,128)S(1)} %bitcast.10, s32[16,128]{1,0:T(8,128)S(1)} %bitcast.11, bf16[576,2048]{1,0:T(8,128)(2,1)S(1)} %get-tuple-element.34.hi_lo_ref, ...), custom_call_target="tpu_custom_call" | custom-call | tf_op jit(solution)/shard_map/adjoint/pallas_call | solution.py:630
  (11 shorter events, 0.1 us)
Async XLA Ops:
  0.6 0.9 %copy-start.1 = (f32[6,4,16,128]{3,2,1,0:T(8,128)S(1)}, f32[6,4,16,128]{3,2,1,0:T(8,128)}, u32[]{:S(2)}) copy-start(f32[6,4,16,128]{3,2,1,0:T(8,128)} %f_ref.1) | copy-start | bytes 589828
  1.6 0.8 %copy-start.2 = (f32[4,16,128]{2,1,0:T(8,128)S(1)}, f32[4,16,128]{2,1,0:T(8,128)}, u32[]{:S(2)}) copy-start(f32[4,16,128]{2,1,0:T(8,128)} %eps_ref.1) | copy-start | bytes 98308
  2.4 3.7 %collective-permute-start = (f32[448,128]{1,0:T(8,128)S(1)}, f32[448,128]{1,0:T(8,128)S(1)}, u32[]{:S(2)}, u32[]{:S(2)}) collective-permute-start(f32[448,128]{1,0:T(8,128)S(1)} %get-tuple-element.24.own_ref), channel_id=1, source_target_pairs={{0,1},{1,0},{2,3},{3,2},{4,5},{5,4},{6,7},{7,6},{8,9},{9,8},{10,11... | collective-permute-start | bytes 688136 | tf_op jit(solution)/shard_map/ppermute | solution.py:530
  2.9 10.6 %collective-permute-start.1 = (f32[336,128]{1,0:T(8,128)S(1)}, f32[336,128]{1,0:T(8,128)S(1)}, u32[]{:S(2)}, u32[]{:S(2)}) collective-permute-start(f32[336,128]{1,0:T(8,128)S(1)} %get-tuple-element.25), channel_id=1, source_target_pairs={{0,2},{2,0},{1,3},{3,1},{4,6},{6,4},{5,7},{7,5},{8,10},{10,8},{9,1... | collective-permute-start | bytes 516104 | tf_op jit(solution)/shard_map/ppermute | solution.py:530
  6.2 7.3 %collective-permute-start.2 = (f32[176,128]{1,0:T(8,128)S(1)}, f32[176,128]{1,0:T(8,128)S(1)}, u32[]{:S(2)}, u32[]{:S(2)}) collective-permute-start(f32[176,128]{1,0:T(8,128)S(1)} %get-tuple-element.26), channel_id=1, source_target_pairs={{0,4},{1,13},{4,0},{5,9},{8,12},{9,5},{12,8},{13,1},{2,6},{3,15},{... | collective-permute-start | bytes 270344 | tf_op jit(solution)/shard_map/ppermute | solution.py:530
  7.8 5.6 %collective-permute-start.3 = (f32[128,128]{1,0:T(8,128)S(1)}, f32[128,128]{1,0:T(8,128)S(1)}, u32[]{:S(2)}, u32[]{:S(2)}) collective-permute-start(f32[128,128]{1,0:T(8,128)S(1)} %get-tuple-element.28), channel_id=1, source_target_pairs={{0,6},{1,15},{2,4},{3,13},{4,2},{5,11},{6,0},{7,9},{8,14},{9,7},{1... | collective-permute-start | bytes 196616 | tf_op jit(solution)/shard_map/ppermute | solution.py:530
  8.4 0.7 %copy-start.5 = (s32[2048]{0:T(1024)S(1)}, s32[2048]{0:T(1024)}, u32[]{:S(2)}) copy-start(s32[2048]{0:T(1024)} %param.15) | copy-start | bytes 24580
  9.1 0.7 %copy-start.6 = (s32[2,32]{1,0:T(2,128)S(1)}, s32[2,32]{1,0:T(2,128)}, u32[]{:S(2)}) copy-start(s32[2,32]{1,0:T(2,128)} %owner_ref.1) | copy-start | bytes 772
  9.8 0.7 %copy-start.7 = (s32[1,4]{1,0:T(1,128)S(1)}, s32[1,4]{1,0:T(1,128)}, u32[]{:S(2)}) copy-start(s32[1,4]{1,0:T(1,128)} %wall_owner_ref.1) | copy-start | bytes 52
  10.5 6.4 %copy-start = (f32[12,4,16,128]{3,2,1,0:T(8,128)S(1)}, f32[12,4,16,128]{3,2,1,0:T(8,128)}, u32[]{:S(2)}) copy-start(f32[12,4,16,128]{3,2,1,0:T(8,128)} %spectra_hbm.1) | copy-start | bytes 1179652
  13.5 3.4 %collective-permute-start.4 = (f32[640,128]{1,0:T(8,128)S(1)}, f32[640,128]{1,0:T(8,128)S(1)}, u32[]{:S(2)}, u32[]{:S(2)}) collective-permute-start(f32[640,128]{1,0:T(8,128)S(1)} %constant_dynamic-update-slice_fusion.halo_ref), channel_id=1, source_target_pairs={{0,1},{1,0},{2,3},{3,2},{4,5},{5,4},{6,7},{7,6},{8,9},{9,8},{10,11... | collective-permute-start | bytes 983048 | tf_op jit(solution)/shard_map/ppermute | solution.py:530
  16.9 18.2 %copy-start.3 = (f32[2048]{0:T(1024)S(1)}, f32[2048]{0:T(1024)}, u32[]{:S(2)}) copy-start(f32[2048]{0:T(1024)} %param.16) | copy-start | bytes 24580
  16.9 18.2 %copy-start.4 = (s32[2048]{0:T(1024)S(1)}, s32[2048]{0:T(1024)}, u32[]{:S(2)}) copy-start(s32[2048]{0:T(1024)} %param.17) | copy-start | bytes 24580
  20.5 1.3 %collective-permute-start.5 = (f32[64,128]{1,0:T(8,128)S(1)}, f32[64,128]{1,0:T(8,128)S(1)}, u32[]{:S(2)}, u32[]{:S(2)}) collective-permute-start(f32[64,128]{1,0:T(8,128)S(1)} %get-tuple-element.38), channel_id=1, source_target_pairs={{0,1},{1,0},{2,3},{3,2},{4,5},{5,4},{6,7},{7,6},{8,9},{9,8},{10,11... | collective-permute-start | bytes 98312 | tf_op jit(solution)/shard_map/ppermute | solution.py:530
  21.8 3.9 %collective-permute-start.6 = (f32[64,128]{1,0:T(8,128)S(1)}, f32[64,128]{1,0:T(8,128)S(1)}, u32[]{:S(2)}, u32[]{:S(2)}) collective-permute-start(f32[64,128]{1,0:T(8,128)S(1)} %add.18), channel_id=1, source_target_pairs={{0,2},{2,0},{1,3},{3,1},{4,6},{6,4},{5,7},{7,5},{8,10},{10,8},{9,1... | collective-permute-start | bytes 98312 | tf_op jit(solution)/shard_map/ppermute | solution.py:530
  25.7 4.5 %collective-permute-start.7 = (f32[80,128]{1,0:T(8,128)S(1)}, f32[80,128]{1,0:T(8,128)S(1)}, u32[]{:S(2)}, u32[]{:S(2)}) collective-permute-start(f32[80,128]{1,0:T(8,128)S(1)} %get-tuple-element.52), channel_id=1, source_target_pairs={{0,4},{4,0},{8,12},{12,8},{1,5},{5,1},{9,13},{13,9},{2,6},{6,2},{1... | collective-permute-start | bytes 122888 | tf_op jit(solution)/shard_map/ppermute | solution.py:530
  25.8 5.4 %collective-permute-start.8 = (f32[80,128]{1,0:T(8,128)S(1)}, f32[80,128]{1,0:T(8,128)S(1)}, u32[]{:S(2)}, u32[]{:S(2)}) collective-permute-start(f32[80,128]{1,0:T(8,128)S(1)} %get-tuple-element.51), channel_id=1, source_target_pairs={{0,8},{4,12},{8,0},{12,4},{1,9},{5,13},{9,1},{13,5},{2,10},{6,14},... | collective-permute-start | bytes 122888 | tf_op jit(solution)/shard_map/ppermute | solution.py:530
  29.3 5.8 %collective-permute-start.9 = (f32[80,128]{1,0:T(8,128)S(1)}, f32[80,128]{1,0:T(8,128)S(1)}, u32[]{:S(2)}, u32[]{:S(2)}) collective-permute-start(f32[80,128]{1,0:T(8,128)S(1)} %get-tuple-element.50), channel_id=1, source_target_pairs={{0,12},{4,8},{8,4},{12,0},{1,13},{5,9},{9,5},{13,1},{2,14},{6,10},... | collective-permute-start | bytes 122888 | tf_op jit(solution)/shard_map/ppermute | solution.py:530

commit v3 on v2

--- a/solution.py
+++ b/solution.py
@@ -25,6 +25,7 @@
 BF16 = jnp.bfloat16
 VMEM = pl.BlockSpec(memory_space=pltpu.VMEM)
 SMEM = pl.BlockSpec(memory_space=pltpu.SMEM)
+HBM = pl.BlockSpec(memory_space=pltpu.HBM)
 
 
 def up8(rows):
@@ -90,14 +91,21 @@
         self.y_kinds = y_kinds
 
 
-def pack_kernel(n, f_ref, eps_ref, own, *y_outs):
+def pack_kernel(n, f_hbm, eps_hbm, own, *rest):
+    y_outs, (eps_ref, sems) = rest[: n.y_kinds], rest[n.y_kinds :]
+    copies = (
+        pltpu.make_async_copy(f_hbm, own.at[0:6], sems.at[0]),
+        pltpu.make_async_copy(eps_hbm, eps_ref, sems.at[1]),
+    )
+    for copy in copies:
+        copy.start()
+    for copy in copies:
+        copy.wait()
     dev_even = lax.axis_index("dev") % 2 == 0
+    for y in range(n.y):
+        own[6, y] = COURANT / eps_ref[y]
     for c in range(7):
-        at = []
-        for y in range(n.y):
-            value = f_ref[c, y] if c < 6 else COURANT / eps_ref[y]
-            own[pl.ds((c * n.y + y) * n.z, n.z), :] = value
-            at.append(value)
+        at = [own[c, y] for y in range(n.y)]
         for kind in range(n.y_kinds):
             top = dev_even if kind == 0 else jnp.logical_not(dev_even)
             for r in range(HALO):
@@ -129,10 +137,26 @@
 
 
 def table_kernel(
-    n, dir_ref, owner_ref, wall_owner_ref, phase_ref, hi_lo_ref, v_ref, place_ref, turn_ref, count_ref
+    n, dir_hbm, owner_hbm, wall_owner_hbm, phase_hbm, hi_lo_ref, v_ref, place_ref, turn_ref,
+    count_ref, dir_ref, owner_ref, wall_owner_ref, phase_ref, sems,
 ):
     gz, dev, xy = (lax.axis_index(a) for a in ("gz", "dev", "xy"))
     hi_ref, lo_ref = halves(n, hi_lo_ref)
+    copies = [
+        pltpu.make_async_copy(source, target, sems.at[i])
+        for i, (source, target) in enumerate(
+            (
+                (dir_hbm, dir_ref),
+                (owner_hbm, owner_ref),
+                (wall_owner_hbm, wall_owner_ref),
+                (phase_hbm, phase_ref),
+            )
+        )
+    ]
+    for copy in copies:
+        copy.start()
+    for copy in copies:
+        copy.wait()
     index = dir_ref[...]
     bits = THETAS.bit_length() - 1
     polar = (index >> bits).astype(F32)
@@ -542,14 +566,17 @@
     def params(mebibytes):
         return pltpu.CompilerParams(vmem_limit_bytes=mebibytes << 20)
 
+    block = tuple(permittivity.shape)
     own, *y_send = pl.pallas_call(
         functools.partial(pack_kernel, n),
         name="pack",
-        out_shape=[out(7 * n.y * n.z, n.x)] + [out(n.y_rows, n.x)] * n.y_kinds,
-        in_specs=[VMEM] * 2,
+        out_shape=[out(7, *block)] + [out(n.y_rows, n.x)] * n.y_kinds,
+        in_specs=[HBM] * 2,
         out_specs=[VMEM] * (1 + n.y_kinds),
+        scratch_shapes=[pltpu.VMEM(block, F32), pltpu.SemaphoreType.DMA((2,))],
         compiler_params=params(4),
     )(fields, permittivity)
+    own = own.reshape(7 * n.y * n.z, n.x)
     y_got = [
         exchange(v, ("dev",), lambda d, k=k: (partner(k, d, n.dev),)) for k, v in enumerate(y_send)
     ]
@@ -581,9 +608,16 @@
             out(n.caps + n.walls, dtype=jnp.int32),
             out(16, LANES),
         ],
-        in_specs=[VMEM] + [SMEM] * 3,
+        in_specs=[HBM] * 4,
         out_specs=[VMEM] * 2 + [SMEM, VMEM],
-        scratch_shapes=[pltpu.SMEM((n.gz,), jnp.int32)],
+        scratch_shapes=[
+            pltpu.SMEM((n.gz,), jnp.int32),
+            pltpu.VMEM((n.tiles, LANES), jnp.int32),
+            pltpu.SMEM(cap_owner.shape, jnp.int32),
+            pltpu.SMEM(wall_owner.shape, jnp.int32),
+            pltpu.SMEM(phase_start.shape, F32),
+            pltpu.SemaphoreType.DMA((4,)),
+        ],
         compiler_params=params(8),
         cost_estimate=pl.CostEstimate(flops=1 << 33, bytes_accessed=16 << 20, transcendentals=0),
     )(dir_index.reshape(n.tiles, LANES), cap_owner, wall_owner, phase_start)
@@ -591,7 +625,6 @@
     halo = jnp.concatenate([*y_got, z_got, *e_got])
     far_halo = exchange(halo, ("xy",), lambda x: (x ^ 1,))
 
-    block = tuple(permittivity.shape)
     anywhere = pl.BlockSpec(memory_space=pl.ANY)
     fields_out, spectra_out, far, chunk = pl.pallas_call(
         functools.partial(main_kernel, n),
@@ -623,8 +656,10 @@
         jnp.concatenate([far, lax.dynamic_slice_in_dim(chunk, (gz ^ k) * n.chunk, n.chunk)])
         for k in range(n.gz)
     ]
-    got = [exchange(payload[k], ("gz",), lambda g, k=k: (g ^ k,)) for k in range(1, n.gz)]
-    gathered = jnp.concatenate([payload[0], *got])
+    got = [
+        exchange(payload[k], ("gz",), lambda g, k=k: (g ^ k,)) for k in range(n.gz - 1, 0, -1)
+    ]
+    gathered = jnp.concatenate([payload[0], *reversed(got)])
 
     sliced = n.own_dirs % LANES == 0
     intensity, owned, adjoint = pl.pallas_call(

time: 37.4 us -> 37.7 us (level)
  no operation moved by 1% of the time
where the time goes in v3:
time: 37.7 us; the launch traced here: 37.4 us
  starting transfers between devices  13.2 us (35%)
  waiting for transfers between devices  10.1 us (27%)
  Pallas kernels  8.9 us (24%)
  local copies, waits for them, and re-layouts  3.77 us (10%)
  between operations  1.42 us (4%)
    ppermute x10, starting transfers between devices, exchange(): return lax.ppermute(values, axes if len(axes) > 1 else axes[0], pairs)  13.2 us
    ppermute x10, waiting for transfers between devices, exchange(): return lax.ppermute(values, axes if len(axes) > 1 else axes[0], pairs)  10.1 us
    unnamed x20, local copies, waits for them, and re-layouts  3.75 us
    pallas_call x1, Pallas kernels, local(): pl.pallas_call(functools.partial(main_kernel, n), name='window', out_shap...  3.54 us
    pallas_call x1, Pallas kernels, local(): pl.pallas_call(functools.partial(table_kernel, n), name='tables', out_sha...  3.01 us
    pallas_call x1, Pallas kernels, local(): pl.pallas_call(functools.partial(adjoint_kernel, n), name='adjoint', out_...  1.99 us
  transfers between devices with their start and end apart: 10, of which 5 were waited for; matrix products, arithmetic and copies ran while one was open for 0% of the time, Pallas kernels for 8%

profile of v3, /device:TPU:0, one launch (start us, length us, event | category | flops | bytes accessed | tf_op | source)
XLA Modules:
  0.0 37.4 jit_solution(18023870920313787951)
XLA Ops:
  0.6 0.0 copy-start.1
  0.6 0.9 %copy-done.1 = f32[6,4,16,128]{3,2,1,0:T(8,128)S(1)} copy-done((f32[6,4,16,128]{3,2,1,0:T(8,128)S(1)}, f32[6,4,16,128]{3,2,1,0:T(8,128)}, u32[]{:S(2)}) %copy-start.1) | copy-done | bytes 196632
  1.6 0.0 copy-start.2
  1.6 0.8 %copy-done.2 = f32[4,16,128]{2,1,0:T(8,128)S(1)} copy-done((f32[4,16,128]{2,1,0:T(8,128)S(1)}, f32[4,16,128]{2,1,0:T(8,128)}, u32[]{:S(2)}) %copy-start.2) | copy-done | bytes 32792
  2.3 0.3 pack.1
  2.6 0.5 %collective-permute-start = (f32[448,128]{1,0:T(8,128)S(1)}, f32[448,128]{1,0:T(8,128)S(1)}, u32[]{:S(2)}, u32[]{:S(2)}) collective-permute-start(f32[448,128]{1,0:T(8,128)S(1)} %bitcast.11), channel_id=1, source_target_pairs={{0,1},{1,0},{2,3},{3,2},{4,5},{5,4},{6,7},{7,6},{8,9},{9,8},{10,11... | collective-permute-start | bytes 688136 | tf_op jit(solution)/shard_map/ppermute | solution.py:554
  3.2 2.6 %collective-permute-start.1 = (f32[336,128]{1,0:T(8,128)S(1)}, f32[336,128]{1,0:T(8,128)S(1)}, u32[]{:S(2)}, u32[]{:S(2)}) collective-permute-start(f32[336,128]{1,0:T(8,128)S(1)} %get-tuple-element.25), channel_id=1, source_target_pairs={{0,2},{2,0},{1,3},{3,1},{4,6},{6,4},{5,7},{7,5},{8,10},{10,8},{9,1... | collective-permute-start | bytes 516104 | tf_op jit(solution)/shard_map/ppermute | solution.py:554
  6.4 0.0 collective-permute-done.other_ref
  6.4 0.1 edges.1
  6.4 1.6 %collective-permute-start.2 = (f32[176,128]{1,0:T(8,128)S(1)}, f32[176,128]{1,0:T(8,128)S(1)}, u32[]{:S(2)}, u32[]{:S(2)}) collective-permute-start(f32[176,128]{1,0:T(8,128)S(1)} %get-tuple-element.26), channel_id=1, source_target_pairs={{0,4},{1,13},{4,0},{5,9},{8,12},{9,5},{12,8},{13,1},{2,6},{3,15},{... | collective-permute-start | bytes 270344 | tf_op jit(solution)/shard_map/ppermute | solution.py:554
  8.1 0.6 %collective-permute-start.3 = (f32[128,128]{1,0:T(8,128)S(1)}, f32[128,128]{1,0:T(8,128)S(1)}, u32[]{:S(2)}, u32[]{:S(2)}) collective-permute-start(f32[128,128]{1,0:T(8,128)S(1)} %get-tuple-element.28), channel_id=1, source_target_pairs={{0,6},{1,15},{2,4},{3,13},{4,2},{5,11},{6,0},{7,9},{8,14},{9,7},{1... | collective-permute-start | bytes 196616 | tf_op jit(solution)/shard_map/ppermute | solution.py:554
  8.7 0.0 copy-start.5
  8.7 0.7 %copy-done.5 = s32[2048]{0:T(1024)S(1)} copy-done((s32[2048]{0:T(1024)S(1)}, s32[2048]{0:T(1024)}, u32[]{:S(2)}) %copy-start.5) | copy-done | bytes 8216
  9.4 0.0 copy-start.6
  9.4 0.7 %copy-done.6 = s32[2,32]{1,0:T(2,128)S(1)} copy-done((s32[2,32]{1,0:T(2,128)S(1)}, s32[2,32]{1,0:T(2,128)}, u32[]{:S(2)}) %copy-start.6) | copy-done | bytes 280
  10.1 0.0 copy-start.7
  10.1 0.7 %copy-done.7 = s32[1,4]{1,0:T(1,128)S(1)} copy-done((s32[1,4]{1,0:T(1,128)S(1)}, s32[1,4]{1,0:T(1,128)}, u32[]{:S(2)}) %copy-start.7) | copy-done | bytes 40
  10.8 0.0 copy-start
  10.8 3.0 %tables.1 = (bf16[576,2048]{1,0:T(8,128)(2,1)S(1)}, f32[128,2048]{1,0:T(8,128)S(1)}, s32[36]{0:T(128)S(1)}, f32[16,128]{1,0:T(8,128)S(1)}) custom-call(s32[16,128]{1,0:T(8,128)S(1)} %bitcast.16, s32[2,32]{1,0:T(2,128)S(1)} %copy-done.6, s32[1,4]{1,0:T(1,128)S(1)} %copy-done.7, f32[1]{0:T(128)S(6)} %copy.22.phase_hbm), custom_call_target="tpu_custom_call" | custom-call | flops 8589934592 | bytes 16777216 | tf_op jit(solution)/shard_map/tables/pallas_call | solution.py:602
  13.8 0.0 collective-permute-done.1
  13.8 0.0 collective-permute-done.3
  13.8 0.0 collective-permute-done.2
  13.9 2.1 %collective-permute-start.4 = (f32[640,128]{1,0:T(8,128)S(1)}, f32[640,128]{1,0:T(8,128)S(1)}, u32[]{:S(2)}, u32[]{:S(2)}) collective-permute-start(f32[640,128]{1,0:T(8,128)S(1)} %constant_dynamic-update-slice_fusion.halo_ref), channel_id=1, source_target_pairs={{0,1},{1,0},{2,3},{3,2},{4,5},{5,4},{6,7},{7,6},{8,9},{9,8},{10,11... | collective-permute-start | bytes 983048 | tf_op jit(solution)/shard_map/ppermute | solution.py:554
  15.9 1.3 %collective-permute-done.4.far_halo_ref = f32[640,128]{1,0:T(8,128)S(1)} collective-permute-done((f32[640,128]{1,0:T(8,128)S(1)}, f32[640,128]{1,0:T(8,128)S(1)}, u32[]{:S(2)}, u32[]{:S(2)}) %collective-permute-start.4) | collective-permute-done | bytes 327712 | tf_op jit(solution)/shard_map/ppermute | solution.py:554
  17.2 0.0 copy-done
  17.2 0.0 copy-start.3
  17.2 0.0 copy-start.4
  17.2 3.5 %window.1 = (f32[6,4,16,128]{3,2,1,0:T(8,128)}, f32[12,4,16,128]{3,2,1,0:T(8,128)}, f32[64,128]{1,0:T(8,128)S(1)}, f32[64,128]{1,0:T(8,128)S(1)}) custom-call(f32[448,128]{1,0:T(8,128)S(1)} %bitcast.13, f32[448,128]{1,0:T(8,128)S(1)} %collective-permute-done.other_ref, f32[640,128]{1,0:T(8,128)S(1)} %constant_dynamic-update-slice_fusion.halo_ref, ...), custom_call_target="tpu_custom_call" | custom-call | tf_op jit(solution)/shard_map/window/pallas_call | solution.py:629
  20.7 0.5 %collective-permute-start.5 = (f32[64,128]{1,0:T(8,128)S(1)}, f32[64,128]{1,0:T(8,128)S(1)}, u32[]{:S(2)}, u32[]{:S(2)}) collective-permute-start(f32[64,128]{1,0:T(8,128)S(1)} %get-tuple-element.38), channel_id=1, source_target_pairs={{0,1},{1,0},{2,3},{3,2},{4,5},{5,4},{6,7},{7,6},{8,9},{9,8},{10,11... | collective-permute-start | bytes 98312 | tf_op jit(solution)/shard_map/ppermute | solution.py:554
  21.2 0.9 %collective-permute-done.5 = f32[64,128]{1,0:T(8,128)S(1)} collective-permute-done((f32[64,128]{1,0:T(8,128)S(1)}, f32[64,128]{1,0:T(8,128)S(1)}, u32[]{:S(2)}, u32[]{:S(2)}) %collective-permute-start.5) | collective-permute-done | bytes 32800 | tf_op jit(solution)/shard_map/ppermute | solution.py:554
  22.1 0.8 %collective-permute-start.6 = (f32[64,128]{1,0:T(8,128)S(1)}, f32[64,128]{1,0:T(8,128)S(1)}, u32[]{:S(2)}, u32[]{:S(2)}) collective-permute-start(f32[64,128]{1,0:T(8,128)S(1)} %add.18), channel_id=1, source_target_pairs={{0,2},{2,0},{1,3},{3,1},{4,6},{6,4},{5,7},{7,5},{8,10},{10,8},{9,1... | collective-permute-start | bytes 98312 | tf_op jit(solution)/shard_map/ppermute | solution.py:554
  22.9 3.1 %collective-permute-done.6 = f32[64,128]{1,0:T(8,128)S(1)} collective-permute-done((f32[64,128]{1,0:T(8,128)S(1)}, f32[64,128]{1,0:T(8,128)S(1)}, u32[]{:S(2)}, u32[]{:S(2)}) %collective-permute-start.6) | collective-permute-done | bytes 32800 | tf_op jit(solution)/shard_map/ppermute | solution.py:554
  26.0 0.1 collective-permute-start.7
  26.1 3.5 %collective-permute-start.8 = (f32[80,128]{1,0:T(8,128)S(1)}, f32[80,128]{1,0:T(8,128)S(1)}, u32[]{:S(2)}, u32[]{:S(2)}) collective-permute-start(f32[80,128]{1,0:T(8,128)S(1)} %get-tuple-element.51), channel_id=1, source_target_pairs={{0,8},{4,12},{8,0},{12,4},{1,9},{5,13},{9,1},{13,5},{2,10},{6,14},... | collective-permute-start | bytes 122888 | tf_op jit(solution)/shard_map/ppermute | solution.py:554
  29.6 0.9 %collective-permute-start.9 = (f32[80,128]{1,0:T(8,128)S(1)}, f32[80,128]{1,0:T(8,128)S(1)}, u32[]{:S(2)}, u32[]{:S(2)}) collective-permute-start(f32[80,128]{1,0:T(8,128)S(1)} %get-tuple-element.50), channel_id=1, source_target_pairs={{0,12},{4,8},{8,4},{12,0},{1,13},{5,9},{9,5},{13,1},{2,14},{6,10},... | collective-permute-start | bytes 122888 | tf_op jit(solution)/shard_map/ppermute | solution.py:554
  30.5 0.0 collective-permute-done.7
  30.5 1.1 %collective-permute-done.8 = f32[80,128]{1,0:T(8,128)S(1)} collective-permute-done((f32[80,128]{1,0:T(8,128)S(1)}, f32[80,128]{1,0:T(8,128)S(1)}, u32[]{:S(2)}, u32[]{:S(2)}) %collective-permute-start.8) | collective-permute-done | bytes 40992 | tf_op jit(solution)/shard_map/ppermute | solution.py:554
  31.6 3.8 %collective-permute-done.9 = f32[80,128]{1,0:T(8,128)S(1)} collective-permute-done((f32[80,128]{1,0:T(8,128)S(1)}, f32[80,128]{1,0:T(8,128)S(1)}, u32[]{:S(2)}, u32[]{:S(2)}) %collective-permute-start.9) | collective-permute-done | bytes 40992 | tf_op jit(solution)/shard_map/ppermute | solution.py:554
  35.4 0.0 copy-done.3
  35.4 0.0 copy-done.4
  35.4 2.0 %adjoint.1 = (f32[1,128]{1,0:T(1,128)}, f32[20,1,128]{2,1,0:T(1,128)}, f32[36,1,128]{2,1,0:T(1,128)}) custom-call(f32[320,128]{1,0:T(8,128)S(1)} %constant_dynamic-update-slice_fusion.3.far_ref, f32[16,128]{1,0:T(8,128)S(1)} %bitcast.14, s32[16,128]{1,0:T(8,128)S(1)} %bitcast.15, bf16[576,2048]{1,0:T(8,128)(2,1)S(1)} %get-tuple-element.34.hi_lo_ref, ...), custom_call_target="tpu_custom_call" | custom-call | tf_op jit(solution)/shard_map/adjoint/pallas_call | solution.py:665
  (10 shorter events, 0.1 us)
Async XLA Ops:
  0.6 0.9 %copy-start.1 = (f32[6,4,16,128]{3,2,1,0:T(8,128)S(1)}, f32[6,4,16,128]{3,2,1,0:T(8,128)}, u32[]{:S(2)}) copy-start(f32[6,4,16,128]{3,2,1,0:T(8,128)} %f_hbm.1) | copy-start | bytes 589828
  1.6 0.8 %copy-start.2 = (f32[4,16,128]{2,1,0:T(8,128)S(1)}, f32[4,16,128]{2,1,0:T(8,128)}, u32[]{:S(2)}) copy-start(f32[4,16,128]{2,1,0:T(8,128)} %eps_hbm.1) | copy-start | bytes 98308
  2.6 3.7 %collective-permute-start = (f32[448,128]{1,0:T(8,128)S(1)}, f32[448,128]{1,0:T(8,128)S(1)}, u32[]{:S(2)}, u32[]{:S(2)}) collective-permute-start(f32[448,128]{1,0:T(8,128)S(1)} %bitcast.11), channel_id=1, source_target_pairs={{0,1},{1,0},{2,3},{3,2},{4,5},{5,4},{6,7},{7,6},{8,9},{9,8},{10,11... | collective-permute-start | bytes 688136 | tf_op jit(solution)/shard_map/ppermute | solution.py:554
  3.2 10.6 %collective-permute-start.1 = (f32[336,128]{1,0:T(8,128)S(1)}, f32[336,128]{1,0:T(8,128)S(1)}, u32[]{:S(2)}, u32[]{:S(2)}) collective-permute-start(f32[336,128]{1,0:T(8,128)S(1)} %get-tuple-element.25), channel_id=1, source_target_pairs={{0,2},{2,0},{1,3},{3,1},{4,6},{6,4},{5,7},{7,5},{8,10},{10,8},{9,1... | collective-permute-start | bytes 516104 | tf_op jit(solution)/shard_map/ppermute | solution.py:554
  6.4 7.3 %collective-permute-start.2 = (f32[176,128]{1,0:T(8,128)S(1)}, f32[176,128]{1,0:T(8,128)S(1)}, u32[]{:S(2)}, u32[]{:S(2)}) collective-permute-start(f32[176,128]{1,0:T(8,128)S(1)} %get-tuple-element.26), channel_id=1, source_target_pairs={{0,4},{1,13},{4,0},{5,9},{8,12},{9,5},{12,8},{13,1},{2,6},{3,15},{... | collective-permute-start | bytes 270344 | tf_op jit(solution)/shard_map/ppermute | solution.py:554
  8.1 5.7 %collective-permute-start.3 = (f32[128,128]{1,0:T(8,128)S(1)}, f32[128,128]{1,0:T(8,128)S(1)}, u32[]{:S(2)}, u32[]{:S(2)}) collective-permute-start(f32[128,128]{1,0:T(8,128)S(1)} %get-tuple-element.28), channel_id=1, source_target_pairs={{0,6},{1,15},{2,4},{3,13},{4,2},{5,11},{6,0},{7,9},{8,14},{9,7},{1... | collective-permute-start | bytes 196616 | tf_op jit(solution)/shard_map/ppermute | solution.py:554
  8.7 0.7 %copy-start.5 = (s32[2048]{0:T(1024)S(1)}, s32[2048]{0:T(1024)}, u32[]{:S(2)}) copy-start(s32[2048]{0:T(1024)} %param.15) | copy-start | bytes 24580
  9.4 0.7 %copy-start.6 = (s32[2,32]{1,0:T(2,128)S(1)}, s32[2,32]{1,0:T(2,128)}, u32[]{:S(2)}) copy-start(s32[2,32]{1,0:T(2,128)} %owner_hbm.1) | copy-start | bytes 772
  10.1 0.7 %copy-start.7 = (s32[1,4]{1,0:T(1,128)S(1)}, s32[1,4]{1,0:T(1,128)}, u32[]{:S(2)}) copy-start(s32[1,4]{1,0:T(1,128)} %wall_owner_hbm.1) | copy-start | bytes 52
  10.8 6.4 %copy-start = (f32[12,4,16,128]{3,2,1,0:T(8,128)S(1)}, f32[12,4,16,128]{3,2,1,0:T(8,128)}, u32[]{:S(2)}) copy-start(f32[12,4,16,128]{3,2,1,0:T(8,128)} %spectra_hbm.1) | copy-start | bytes 1179652
  13.9 3.3 %collective-permute-start.4 = (f32[640,128]{1,0:T(8,128)S(1)}, f32[640,128]{1,0:T(8,128)S(1)}, u32[]{:S(2)}, u32[]{:S(2)}) collective-permute-start(f32[640,128]{1,0:T(8,128)S(1)} %constant_dynamic-update-slice_fusion.halo_ref), channel_id=1, source_target_pairs={{0,1},{1,0},{2,3},{3,2},{4,5},{5,4},{6,7},{7,6},{8,9},{9,8},{10,11... | collective-permute-start | bytes 983048 | tf_op jit(solution)/shard_map/ppermute | solution.py:554
  17.2 18.2 %copy-start.3 = (f32[2048]{0:T(1024)S(1)}, f32[2048]{0:T(1024)}, u32[]{:S(2)}) copy-start(f32[2048]{0:T(1024)} %param.16) | copy-start | bytes 24580
  17.2 18.2 %copy-start.4 = (s32[2048]{0:T(1024)S(1)}, s32[2048]{0:T(1024)}, u32[]{:S(2)}) copy-start(s32[2048]{0:T(1024)} %param.17) | copy-start | bytes 24580
  20.7 1.3 %collective-permute-start.5 = (f32[64,128]{1,0:T(8,128)S(1)}, f32[64,128]{1,0:T(8,128)S(1)}, u32[]{:S(2)}, u32[]{:S(2)}) collective-permute-start(f32[64,128]{1,0:T(8,128)S(1)} %get-tuple-element.38), channel_id=1, source_target_pairs={{0,1},{1,0},{2,3},{3,2},{4,5},{5,4},{6,7},{7,6},{8,9},{9,8},{10,11... | collective-permute-start | bytes 98312 | tf_op jit(solution)/shard_map/ppermute | solution.py:554
  22.1 3.9 %collective-permute-start.6 = (f32[64,128]{1,0:T(8,128)S(1)}, f32[64,128]{1,0:T(8,128)S(1)}, u32[]{:S(2)}, u32[]{:S(2)}) collective-permute-start(f32[64,128]{1,0:T(8,128)S(1)} %add.18), channel_id=1, source_target_pairs={{0,2},{2,0},{1,3},{3,1},{4,6},{6,4},{5,7},{7,5},{8,10},{10,8},{9,1... | collective-permute-start | bytes 98312 | tf_op jit(solution)/shard_map/ppermute | solution.py:554
  26.0 4.5 %collective-permute-start.7 = (f32[80,128]{1,0:T(8,128)S(1)}, f32[80,128]{1,0:T(8,128)S(1)}, u32[]{:S(2)}, u32[]{:S(2)}) collective-permute-start(f32[80,128]{1,0:T(8,128)S(1)} %get-tuple-element.52), channel_id=1, source_target_pairs={{0,4},{4,0},{8,12},{12,8},{1,5},{5,1},{9,13},{13,9},{2,6},{6,2},{1... | collective-permute-start | bytes 122888 | tf_op jit(solution)/shard_map/ppermute | solution.py:554
  26.1 5.5 %collective-permute-start.8 = (f32[80,128]{1,0:T(8,128)S(1)}, f32[80,128]{1,0:T(8,128)S(1)}, u32[]{:S(2)}, u32[]{:S(2)}) collective-permute-start(f32[80,128]{1,0:T(8,128)S(1)} %get-tuple-element.51), channel_id=1, source_target_pairs={{0,8},{4,12},{8,0},{12,4},{1,9},{5,13},{9,1},{13,5},{2,10},{6,14},... | collective-permute-start | bytes 122888 | tf_op jit(solution)/shard_map/ppermute | solution.py:554
  29.6 5.8 %collective-permute-start.9 = (f32[80,128]{1,0:T(8,128)S(1)}, f32[80,128]{1,0:T(8,128)S(1)}, u32[]{:S(2)}, u32[]{:S(2)}) collective-permute-start(f32[80,128]{1,0:T(8,128)S(1)} %get-tuple-element.50), channel_id=1, source_target_pairs={{0,12},{4,8},{8,4},{12,0},{1,13},{5,9},{9,5},{13,1},{2,14},{6,10},... | collective-permute-start | bytes 122888 | tf_op jit(solution)/shard_map/ppermute | solution.py:554

commit v4 on v3

--- a/solution.py
+++ b/solution.py
@@ -467,7 +467,7 @@
     for kind in range(4):
         total = None
         for k in range(n.gz):
-            at = k * block + kind * n.tiles
+            at = (n.gz - 1 - k) * block + kind * n.tiles
             term = far_ref[at : at + n.tiles, :]
             total = term if total is None else total + term
         parts.append(total)
@@ -520,7 +520,7 @@
     walls = [jnp.zeros((1, LANES), F32) for _ in range(n.walls)]
     rank = jnp.zeros((1, LANES), F32)
     for s in range(n.gz):
-        at = pl.multiple_of((gz ^ s) * block + n.far_rows, 8)
+        at = pl.multiple_of((n.gz - 1 - (gz ^ s)) * block + n.far_rows, 8)
         rows = far_ref[pl.ds(at, 8), :]
         record, flag = rows[0:1, :], rows[1:2, :] > 0.5
         for r in range(n.walls):
@@ -529,7 +529,7 @@
     for r in range(n.walls):
         owned_out[r, :, :] = walls[r]
     for cap_at, s in enumerate((0, n.gz - 1)):
-        at = pl.multiple_of((gz ^ s) * block + n.far_rows, 8)
+        at = pl.multiple_of((n.gz - 1 - (gz ^ s)) * block + n.far_rows, 8)
         rows = far_ref[pl.ds(at, n.chunk), :]
         owned_out[n.walls + cap_at * n.share : n.walls + (cap_at + 1) * n.share, 0, :] = rows[2 : 2 + n.share, :]
 
@@ -563,6 +563,9 @@
     def out(*shape, dtype=F32):
         return jax.ShapeDtypeStruct(shape, dtype)
 
+    def far_memory(values):
+        return pltpu.with_memory_space_constraint(values, pltpu.HBM)
+
     def params(mebibytes):
         return pltpu.CompilerParams(vmem_limit_bytes=mebibytes << 20)
 
@@ -575,7 +578,7 @@
         out_specs=[VMEM] * (1 + n.y_kinds),
         scratch_shapes=[pltpu.VMEM(block, F32), pltpu.SemaphoreType.DMA((2,))],
         compiler_params=params(4),
-    )(fields, permittivity)
+    )(far_memory(fields), far_memory(permittivity))
     own = own.reshape(7 * n.y * n.z, n.x)
     y_got = [
         exchange(v, ("dev",), lambda d, k=k: (partner(k, d, n.dev),)) for k, v in enumerate(y_send)
@@ -620,7 +623,7 @@
         ],
         compiler_params=params(8),
         cost_estimate=pl.CostEstimate(flops=1 << 33, bytes_accessed=16 << 20, transcendentals=0),
-    )(dir_index.reshape(n.tiles, LANES), cap_owner, wall_owner, phase_start)
+    )(*map(far_memory, (dir_index.reshape(n.tiles, LANES), cap_owner, wall_owner)), phase_start)
     (*y_got, z_got, turns), e_got = lax.optimization_barrier(((*y_got, z_got, turns), e_got))
     halo = jnp.concatenate([*y_got, z_got, *e_got])
     far_halo = exchange(halo, ("xy",), lambda x: (x ^ 1,))
@@ -659,7 +662,7 @@
     got = [
         exchange(payload[k], ("gz",), lambda g, k=k: (g ^ k,)) for k in range(n.gz - 1, 0, -1)
     ]
-    gathered = jnp.concatenate([payload[0], *reversed(got)])
+    gathered = jnp.concatenate([*got, payload[0]])
 
     sliced = n.own_dirs % LANES == 0
     intensity, owned, adjoint = pl.pallas_call(

time: 37.7 us -> 35 us (0.928)
  local copies, waits for them, and re-layouts: 3.77 us -> 0.07 us
  Pallas kernels: 8.9 us -> 9.82 us
  waiting for transfers between devices: 10.1 us -> 9.32 us
  other arithmetic: 0.02 us -> 0.67 us
  starting transfers between devices: 13.2 us -> 13.6 us
    unnamed x20 -> x12, local copies, waits for them, and re-layouts: 3.75 us -> 0.05 us
    ppermute x10, waiting for transfers between devices: 10.1 us -> 9.32 us  [exchange(): return lax.ppermute(values, axes if len(axes) > 1 else axes[0], pairs)]
    pallas_call x1, Pallas kernels: 0.31 us -> 0.97 us  [local(): pl.pallas_call(functools.partial(pack_kernel, n), name='pack', out_shape=...]
    concatenate x1, other arithmetic: 0.01 us -> 0.66 us  [local(): jnp.concatenate([far, lax.dynamic_slice_in_dim(chunk, (gz ^ k) * n.chunk,...]
    ppermute x10, starting transfers between devices: 13.2 us -> 13.6 us  [exchange(): return lax.ppermute(values, axes if len(axes) > 1 else axes[0], pairs)]
  transfers between devices with their start and end apart: 10 -> 10, of which waited for: 5 -> 6; matrix products, arithmetic and copies ran while one was open for 0% -> 0% of each run, Pallas kernels for 8% -> 10%
where the time goes in v4:
time: 35 us; the launch traced here: 34.9 us
  starting transfers between devices  13.6 us (39%)
  Pallas kernels  9.82 us (28%)
  waiting for transfers between devices  9.32 us (27%)
  between operations  1.41 us (4%)
  other arithmetic  0.67 us (2%)
    ppermute x10, starting transfers between devices, exchange(): return lax.ppermute(values, axes if len(axes) > 1 else axes[0], pairs)  13.6 us
    ppermute x10, waiting for transfers between devices, exchange(): return lax.ppermute(values, axes if len(axes) > 1 else axes[0], pairs)  9.32 us
    pallas_call x1, Pallas kernels, local(): pl.pallas_call(functools.partial(main_kernel, n), name='window', out_shap...  3.53 us
    pallas_call x1, Pallas kernels, local(): pl.pallas_call(functools.partial(table_kernel, n), name='tables', out_sha...  3.27 us
    pallas_call x1, Pallas kernels, local(): pl.pallas_call(functools.partial(adjoint_kernel, n), name='adjoint', out_...  1.99 us
    pallas_call x1, Pallas kernels, local(): pl.pallas_call(functools.partial(pack_kernel, n), name='pack', out_shape=...  0.97 us
  transfers between devices with their start and end apart: 10, of which 6 were waited for; matrix products, arithmetic and copies ran while one was open for 0% of the time, Pallas kernels for 10%

profile of v4, /device:TPU:0, one launch (start us, length us, event | category | flops | bytes accessed | tf_op | source)
XLA Modules:
  0.0 34.9 jit_solution(5812202184935023046)
XLA Ops:
  0.6 1.0 %pack.1 = (f32[7,4,16,128]{3,2,1,0:T(8,128)S(1)}, f32[336,128]{1,0:T(8,128)S(1)}) custom-call(f32[6,4,16,128]{3,2,1,0:T(8,128)} %f_hbm.1, f32[4,16,128]{2,1,0:T(8,128)} %eps_hbm.1), custom_call_target="tpu_custom_call" | custom-call | tf_op jit(solution)/shard_map/pack/pallas_call | solution.py:573
  1.6 0.5 %collective-permute-start = (f32[448,128]{1,0:T(8,128)S(1)}, f32[448,128]{1,0:T(8,128)S(1)}, u32[]{:S(2)}, u32[]{:S(2)}) collective-permute-start(f32[448,128]{1,0:T(8,128)S(1)} %bitcast.11), channel_id=1, source_target_pairs={{0,1},{1,0},{2,3},{3,2},{4,5},{5,4},{6,7},{7,6},{8,9},{9,8},{10,11... | collective-permute-start | bytes 688136 | tf_op jit(solution)/shard_map/ppermute | solution.py:554
  2.1 2.6 %collective-permute-start.1 = (f32[336,128]{1,0:T(8,128)S(1)}, f32[336,128]{1,0:T(8,128)S(1)}, u32[]{:S(2)}, u32[]{:S(2)}) collective-permute-start(f32[336,128]{1,0:T(8,128)S(1)} %get-tuple-element.25), channel_id=1, source_target_pairs={{0,2},{2,0},{1,3},{3,1},{4,6},{6,4},{5,7},{7,5},{8,10},{10,8},{9,1... | collective-permute-start | bytes 516104 | tf_op jit(solution)/shard_map/ppermute | solution.py:554
  5.3 0.0 collective-permute-done.other_ref
  5.4 0.1 edges.1
  5.4 1.6 %collective-permute-start.2 = (f32[176,128]{1,0:T(8,128)S(1)}, f32[176,128]{1,0:T(8,128)S(1)}, u32[]{:S(2)}, u32[]{:S(2)}) collective-permute-start(f32[176,128]{1,0:T(8,128)S(1)} %get-tuple-element.26), channel_id=1, source_target_pairs={{0,4},{1,13},{4,0},{5,9},{8,12},{9,5},{12,8},{13,1},{2,6},{3,15},{... | collective-permute-start | bytes 270344 | tf_op jit(solution)/shard_map/ppermute | solution.py:554
  7.1 0.6 %collective-permute-start.3 = (f32[128,128]{1,0:T(8,128)S(1)}, f32[128,128]{1,0:T(8,128)S(1)}, u32[]{:S(2)}, u32[]{:S(2)}) collective-permute-start(f32[128,128]{1,0:T(8,128)S(1)} %get-tuple-element.28), channel_id=1, source_target_pairs={{0,6},{1,15},{2,4},{3,13},{4,2},{5,11},{6,0},{7,9},{8,14},{9,7},{1... | collective-permute-start | bytes 196616 | tf_op jit(solution)/shard_map/ppermute | solution.py:554
  7.7 0.0 copy-start
  7.7 3.3 %tables.1 = (bf16[576,2048]{1,0:T(8,128)(2,1)S(1)}, f32[128,2048]{1,0:T(8,128)S(1)}, s32[36]{0:T(128)S(1)}, f32[16,128]{1,0:T(8,128)S(1)}) custom-call(s32[16,128]{1,0:T(8,128)} %bitcast.18, s32[2,32]{1,0:T(2,128)} %owner_hbm.1, s32[1,4]{1,0:T(1,128)} %wall_owner_hbm.1, f32[1]{0:T(128)S(6)} %copy.22.phase_hbm), custom_call_target="tpu_custom_call" | custom-call | flops 8589934592 | bytes 16777216 | tf_op jit(solution)/shard_map/tables/pallas_call | solution.py:605
  11.0 0.0 collective-permute-done.1
  11.0 1.2 %collective-permute-done.3 = f32[128,128]{1,0:T(8,128)S(1)} collective-permute-done((f32[128,128]{1,0:T(8,128)S(1)}, f32[128,128]{1,0:T(8,128)S(1)}, u32[]{:S(2)}, u32[]{:S(2)}) %collective-permute-start.3) | collective-permute-done | bytes 65568 | tf_op jit(solution)/shard_map/ppermute | solution.py:554
  12.2 0.0 collective-permute-done.2
  12.3 2.6 %collective-permute-start.4 = (f32[640,128]{1,0:T(8,128)S(1)}, f32[640,128]{1,0:T(8,128)S(1)}, u32[]{:S(2)}, u32[]{:S(2)}) collective-permute-start(f32[640,128]{1,0:T(8,128)S(1)} %constant_dynamic-update-slice_fusion.halo_ref), channel_id=1, source_target_pairs={{0,1},{1,0},{2,3},{3,2},{4,5},{5,4},{6,7},{7,6},{8,9},{9,8},{10,11... | collective-permute-start | bytes 983048 | tf_op jit(solution)/shard_map/ppermute | solution.py:554
  14.9 1.3 %collective-permute-done.4.far_halo_ref = f32[640,128]{1,0:T(8,128)S(1)} collective-permute-done((f32[640,128]{1,0:T(8,128)S(1)}, f32[640,128]{1,0:T(8,128)S(1)}, u32[]{:S(2)}, u32[]{:S(2)}) %collective-permute-start.4) | collective-permute-done | bytes 327712 | tf_op jit(solution)/shard_map/ppermute | solution.py:554
  16.2 0.0 copy-done
  16.2 0.0 copy-start.1
  16.2 0.0 copy-start.2
  16.2 3.5 %window.1 = (f32[6,4,16,128]{3,2,1,0:T(8,128)}, f32[12,4,16,128]{3,2,1,0:T(8,128)}, f32[64,128]{1,0:T(8,128)S(1)}, f32[64,128]{1,0:T(8,128)S(1)}) custom-call(f32[448,128]{1,0:T(8,128)S(1)} %bitcast.13, f32[448,128]{1,0:T(8,128)S(1)} %collective-permute-done.other_ref, f32[640,128]{1,0:T(8,128)S(1)} %constant_dynamic-update-slice_fusion.halo_ref, ...), custom_call_target="tpu_custom_call" | custom-call | tf_op jit(solution)/shard_map/window/pallas_call | solution.py:632
  19.7 0.5 %collective-permute-start.5 = (f32[64,128]{1,0:T(8,128)S(1)}, f32[64,128]{1,0:T(8,128)S(1)}, u32[]{:S(2)}, u32[]{:S(2)}) collective-permute-start(f32[64,128]{1,0:T(8,128)S(1)} %get-tuple-element.38), channel_id=1, source_target_pairs={{0,1},{1,0},{2,3},{3,2},{4,5},{5,4},{6,7},{7,6},{8,9},{9,8},{10,11... | collective-permute-start | bytes 98312 | tf_op jit(solution)/shard_map/ppermute | solution.py:554
  20.2 0.9 %collective-permute-done.5 = f32[64,128]{1,0:T(8,128)S(1)} collective-permute-done((f32[64,128]{1,0:T(8,128)S(1)}, f32[64,128]{1,0:T(8,128)S(1)}, u32[]{:S(2)}, u32[]{:S(2)}) %collective-permute-start.5) | collective-permute-done | bytes 32800 | tf_op jit(solution)/shard_map/ppermute | solution.py:554
  21.0 0.7 %collective-permute-start.6 = (f32[64,128]{1,0:T(8,128)S(1)}, f32[64,128]{1,0:T(8,128)S(1)}, u32[]{:S(2)}, u32[]{:S(2)}) collective-permute-start(f32[64,128]{1,0:T(8,128)S(1)} %add.18), channel_id=1, source_target_pairs={{0,2},{2,0},{1,3},{3,1},{4,6},{6,4},{5,7},{7,5},{8,10},{10,8},{9,1... | collective-permute-start | bytes 98312 | tf_op jit(solution)/shard_map/ppermute | solution.py:554
  21.8 3.2 %collective-permute-done.6 = f32[64,128]{1,0:T(8,128)S(1)} collective-permute-done((f32[64,128]{1,0:T(8,128)S(1)}, f32[64,128]{1,0:T(8,128)S(1)}, u32[]{:S(2)}, u32[]{:S(2)}) %collective-permute-start.6) | collective-permute-done | bytes 32800 | tf_op jit(solution)/shard_map/ppermute | solution.py:554
  25.0 0.7 %pad_maximum_fusion = (f32[80,128]{1,0:T(8,128)}, f32[80,128]{1,0:T(8,128)}, f32[80,128]{1,0:T(8,128)}) fusion(f32[64,128]{1,0:T(8,128)S(1)} %add.19, f32[16,128]{1,0:T(8,128)S(1)} %get-tuple-element.51, f32[16,128]{1,0:T(8,128)S(1)} %get-tuple-element.52, f32[16,128]{1,0:T(8,128)S(1)} %get-tuple-element.53), kind=kLoop, calls=%fused_computation | loop fusion | flops 30720 | bytes 180224 | tf_op jit(solution)/shard_map/concatenate | solution.py:659
  25.6 1.8 %collective-permute-start.7 = (f32[80,128]{1,0:T(8,128)}, f32[80,128]{1,0:T(8,128)S(1)}, u32[]{:S(2)}, u32[]{:S(2)}) collective-permute-start(f32[80,128]{1,0:T(8,128)} %get-tuple-element.50), channel_id=1, source_target_pairs={{0,12},{4,8},{8,4},{12,0},{1,13},{5,9},{9,5},{13,1},{2,14},{6,10},... | collective-permute-start | bytes 122888 | tf_op jit(solution)/shard_map/ppermute | solution.py:554
  27.4 0.0 collective-permute-start.8
  27.4 2.6 %collective-permute-start.9 = (f32[80,128]{1,0:T(8,128)}, f32[80,128]{1,0:T(8,128)S(1)}, u32[]{:S(2)}, u32[]{:S(2)}) collective-permute-start(f32[80,128]{1,0:T(8,128)} %get-tuple-element.48), channel_id=1, source_target_pairs={{0,4},{4,0},{8,12},{12,8},{1,5},{5,1},{9,13},{13,9},{2,6},{6,2},{1... | collective-permute-start | bytes 122888 | tf_op jit(solution)/shard_map/ppermute | solution.py:554
  30.0 2.0 %collective-permute-done.7 = f32[80,128]{1,0:T(8,128)S(1)} collective-permute-done((f32[80,128]{1,0:T(8,128)}, f32[80,128]{1,0:T(8,128)S(1)}, u32[]{:S(2)}, u32[]{:S(2)}) %collective-permute-start.7) | collective-permute-done | bytes 40992 | tf_op jit(solution)/shard_map/ppermute | solution.py:554
  32.0 0.8 %collective-permute-done.8 = f32[80,128]{1,0:T(8,128)S(1)} collective-permute-done((f32[80,128]{1,0:T(8,128)}, f32[80,128]{1,0:T(8,128)S(1)}, u32[]{:S(2)}, u32[]{:S(2)}) %collective-permute-start.8) | collective-permute-done | bytes 40992 | tf_op jit(solution)/shard_map/ppermute | solution.py:554
  32.8 0.0 collective-permute-done.9
  32.8 0.0 copy-done.1
  32.9 0.0 copy-done.2
  32.9 2.0 %adjoint.1 = (f32[1,128]{1,0:T(1,128)}, f32[20,1,128]{2,1,0:T(1,128)}, f32[36,1,128]{2,1,0:T(1,128)}) custom-call(f32[320,128]{1,0:T(8,128)S(1)} %constant_dynamic-update-slice_fusion.3.far_ref, f32[16,128]{1,0:T(8,128)S(1)} %bitcast.14, s32[16,128]{1,0:T(8,128)S(1)} %bitcast.15, bf16[576,2048]{1,0:T(8,128)(2,1)S(1)} %get-tuple-element.34.hi_lo_ref, ...), custom_call_target="tpu_custom_call" | custom-call | tf_op jit(solution)/shard_map/adjoint/pallas_call | solution.py:668
  (11 shorter events, 0.1 us)
Async XLA Ops:
  1.6 3.7 %collective-permute-start = (f32[448,128]{1,0:T(8,128)S(1)}, f32[448,128]{1,0:T(8,128)S(1)}, u32[]{:S(2)}, u32[]{:S(2)}) collective-permute-start(f32[448,128]{1,0:T(8,128)S(1)} %bitcast.11), channel_id=1, source_target_pairs={{0,1},{1,0},{2,3},{3,2},{4,5},{5,4},{6,7},{7,6},{8,9},{9,8},{10,11... | collective-permute-start | bytes 688136 | tf_op jit(solution)/shard_map/ppermute | solution.py:554
  2.1 8.9 %collective-permute-start.1 = (f32[336,128]{1,0:T(8,128)S(1)}, f32[336,128]{1,0:T(8,128)S(1)}, u32[]{:S(2)}, u32[]{:S(2)}) collective-permute-start(f32[336,128]{1,0:T(8,128)S(1)} %get-tuple-element.25), channel_id=1, source_target_pairs={{0,2},{2,0},{1,3},{3,1},{4,6},{6,4},{5,7},{7,5},{8,10},{10,8},{9,1... | collective-permute-start | bytes 516104 | tf_op jit(solution)/shard_map/ppermute | solution.py:554
  5.4 6.8 %collective-permute-start.2 = (f32[176,128]{1,0:T(8,128)S(1)}, f32[176,128]{1,0:T(8,128)S(1)}, u32[]{:S(2)}, u32[]{:S(2)}) collective-permute-start(f32[176,128]{1,0:T(8,128)S(1)} %get-tuple-element.26), channel_id=1, source_target_pairs={{0,4},{1,13},{4,0},{5,9},{8,12},{9,5},{12,8},{13,1},{2,6},{3,15},{... | collective-permute-start | bytes 270344 | tf_op jit(solution)/shard_map/ppermute | solution.py:554
  7.1 5.2 %collective-permute-start.3 = (f32[128,128]{1,0:T(8,128)S(1)}, f32[128,128]{1,0:T(8,128)S(1)}, u32[]{:S(2)}, u32[]{:S(2)}) collective-permute-start(f32[128,128]{1,0:T(8,128)S(1)} %get-tuple-element.28), channel_id=1, source_target_pairs={{0,6},{1,15},{2,4},{3,13},{4,2},{5,11},{6,0},{7,9},{8,14},{9,7},{1... | collective-permute-start | bytes 196616 | tf_op jit(solution)/shard_map/ppermute | solution.py:554
  7.7 8.5 %copy-start = (f32[12,4,16,128]{3,2,1,0:T(8,128)S(1)}, f32[12,4,16,128]{3,2,1,0:T(8,128)}, u32[]{:S(2)}) copy-start(f32[12,4,16,128]{3,2,1,0:T(8,128)} %spectra_hbm.1) | copy-start | bytes 1179652
  12.3 3.9 %collective-permute-start.4 = (f32[640,128]{1,0:T(8,128)S(1)}, f32[640,128]{1,0:T(8,128)S(1)}, u32[]{:S(2)}, u32[]{:S(2)}) collective-permute-start(f32[640,128]{1,0:T(8,128)S(1)} %constant_dynamic-update-slice_fusion.halo_ref), channel_id=1, source_target_pairs={{0,1},{1,0},{2,3},{3,2},{4,5},{5,4},{6,7},{7,6},{8,9},{9,8},{10,11... | collective-permute-start | bytes 983048 | tf_op jit(solution)/shard_map/ppermute | solution.py:554
  16.2 16.7 %copy-start.1 = (f32[2048]{0:T(1024)S(1)}, f32[2048]{0:T(1024)}, u32[]{:S(2)}) copy-start(f32[2048]{0:T(1024)} %param.16) | copy-start | bytes 24580
  16.2 16.7 %copy-start.2 = (s32[2048]{0:T(1024)S(1)}, s32[2048]{0:T(1024)}, u32[]{:S(2)}) copy-start(s32[2048]{0:T(1024)} %param.17) | copy-start | bytes 24580
  19.7 1.3 %collective-permute-start.5 = (f32[64,128]{1,0:T(8,128)S(1)}, f32[64,128]{1,0:T(8,128)S(1)}, u32[]{:S(2)}, u32[]{:S(2)}) collective-permute-start(f32[64,128]{1,0:T(8,128)S(1)} %get-tuple-element.38), channel_id=1, source_target_pairs={{0,1},{1,0},{2,3},{3,2},{4,5},{5,4},{6,7},{7,6},{8,9},{9,8},{10,11... | collective-permute-start | bytes 98312 | tf_op jit(solution)/shard_map/ppermute | solution.py:554
  21.0 3.9 %collective-permute-start.6 = (f32[64,128]{1,0:T(8,128)S(1)}, f32[64,128]{1,0:T(8,128)S(1)}, u32[]{:S(2)}, u32[]{:S(2)}) collective-permute-start(f32[64,128]{1,0:T(8,128)S(1)} %add.18), channel_id=1, source_target_pairs={{0,2},{2,0},{1,3},{3,1},{4,6},{6,4},{5,7},{7,5},{8,10},{10,8},{9,1... | collective-permute-start | bytes 98312 | tf_op jit(solution)/shard_map/ppermute | solution.py:554
  25.6 6.4 %collective-permute-start.7 = (f32[80,128]{1,0:T(8,128)}, f32[80,128]{1,0:T(8,128)S(1)}, u32[]{:S(2)}, u32[]{:S(2)}) collective-permute-start(f32[80,128]{1,0:T(8,128)} %get-tuple-element.50), channel_id=1, source_target_pairs={{0,12},{4,8},{8,4},{12,0},{1,13},{5,9},{9,5},{13,1},{2,14},{6,10},... | collective-permute-start | bytes 122888 | tf_op jit(solution)/shard_map/ppermute | solution.py:554
  27.4 5.4 %collective-permute-start.8 = (f32[80,128]{1,0:T(8,128)}, f32[80,128]{1,0:T(8,128)S(1)}, u32[]{:S(2)}, u32[]{:S(2)}) collective-permute-start(f32[80,128]{1,0:T(8,128)} %get-tuple-element.49), channel_id=1, source_target_pairs={{0,8},{4,12},{8,0},{12,4},{1,9},{5,13},{9,1},{13,5},{2,10},{6,14},... | collective-permute-start | bytes 122888 | tf_op jit(solution)/shard_map/ppermute | solution.py:554
  27.4 5.4 %collective-permute-start.9 = (f32[80,128]{1,0:T(8,128)}, f32[80,128]{1,0:T(8,128)S(1)}, u32[]{:S(2)}, u32[]{:S(2)}) collective-permute-start(f32[80,128]{1,0:T(8,128)} %get-tuple-element.48), channel_id=1, source_target_pairs={{0,4},{4,0},{8,12},{12,8},{1,5},{5,1},{9,13},{13,9},{2,6},{6,2},{1... | collective-permute-start | bytes 122888 | tf_op jit(solution)/shard_map/ppermute | solution.py:554

commit v5 on v4

--- a/solution.py
+++ b/solution.py
@@ -216,13 +216,11 @@
             scale = cap_scale if face == 0 else n.norm
             w_theta = weights([-th[i], -th[j], -ph[i], -ph[j]]) * scale
             w_phi = weights([-ph[i], -ph[j], th[i], th[j]]) * scale
-            for y in range(n.y):
-                r = face * 4 + y
-                bc, bs = base_c[r : r + 1, :], base_s[r : r + 1, :]
-                factor = jnp.where(low, bc, -bs)
-                for kind, value in enumerate((factor * w_theta, factor * w_phi)):
-                    at = ((face * 2 + kind) * n.y + y) * 8
-                    v_ref[at : at + 8, lanes] = value
+            for kind, value in enumerate((w_theta, w_phi)):
+                at = 16 + (face * 2 + kind) * 8
+                v_ref[at : at + 8, lanes] = value
+        v_ref[0:8, lanes] = base_c
+        v_ref[8:16, lanes] = base_s
     for o in range(n.gz):
         count_ref[o] = 0
     which = jnp.where(gz == 0, 0, 1)
@@ -258,6 +256,17 @@
         moved = jnp.where(row_bit, behind, ahead)
         values = jnp.where(row_bit == block_bit, values, moved)
     return values
+
+
+def patch_factors(n, v_ref, face, lanes):
+    low = rows_iota((8, LANES)) < 4
+    base_c, base_s = v_ref[0:8, lanes], v_ref[8:16, lanes]
+    at = [face * 4 + y for y in range(n.y)]
+    return [jnp.where(low, base_c[r : r + 1, :], -base_s[r : r + 1, :]) for r in at]
+
+
+def face_weights(v_ref, face, lanes):
+    return (v_ref[16 + face * 16 + 8 * kind : 24 + face * 16 + 8 * kind, lanes] for kind in range(2))
 
 
 def turn(values):
@@ -441,15 +450,16 @@
         for t in range(wide // LANES):
             lanes = slice(first + t * LANES, first + (t + 1) * LANES)
             tile = first // LANES + t
-            totals = [None] * 4
+            totals = [0.0] * 4
             for face in range(2):
-                for y in range(n.y):
+                even, odd = 0.0, 0.0
+                for y, factor in enumerate(patch_factors(n, v_ref, face, lanes)):
                     rows = sums[face][y * 8 : y * 8 + 8, t * LANES : (t + 1) * LANES]
-                    turned = -turn(rows)
-                    for kind in range(4):
-                        at = ((face * 2 + kind % 2) * n.y + y) * 8
-                        term = v_ref[at : at + 8, lanes] * (rows if kind < 2 else turned)
-                        totals[kind] = term if totals[kind] is None else totals[kind] + term
+                    even = even + factor * rows
+                    odd = odd - factor * turn(rows)
+                w_theta, w_phi = face_weights(v_ref, face, lanes)
+                for kind, term in enumerate((w_theta * even, w_phi * even, w_theta * odd, w_phi * odd)):
+                    totals[kind] = totals[kind] + term
             for kind, total in enumerate(totals):
                 at = kind * n.tiles + tile
                 far_out[at : at + 1, :] = jnp.sum(total, axis=0, keepdims=True)
@@ -486,14 +496,13 @@
     for face in range(2):
         for t in range(n.tiles):
             lanes = slice(t * LANES, (t + 1) * LANES)
-            rows = []
-            for y in range(n.y):
-                at = (face * 2 * n.y + y) * 8
-                one, two = v_ref[at : at + 8, lanes], v_ref[at + n.y * 8 : at + n.y * 8 + 8, lanes]
-                even, odd = (
-                    one * slopes[k][t : t + 1, :] + two * slopes[k + 1][t : t + 1, :] for k in (0, 2)
-                )
-                rows.append(even + turn(odd))
+            w_theta, w_phi = face_weights(v_ref, face, lanes)
+            even, odd = (
+                w_theta * slopes[k][t : t + 1, :] + w_phi * slopes[k + 1][t : t + 1, :] for k in (0, 2)
+            )
+            rows = [
+                factor * even + turn(factor * odd) for factor in patch_factors(n, v_ref, face, lanes)
+            ]
             faces[face].append(jnp.concatenate(rows, axis=0))
     dot = functools.partial(
         lax.dot_general,
@@ -607,7 +616,7 @@
         name="tables",
         out_shape=[
             out(2 * n.table_rows, n.dirs, dtype=BF16),
-            out(4 * n.y * 8, n.dirs),
+            out(48, n.dirs),
             out(n.caps + n.walls, dtype=jnp.int32),
             out(16, LANES),
         ],

time: 35 us -> 34.5 us (0.986)
  other arithmetic: 0.67 us -> 0.02 us
    concatenate x1, other arithmetic: 0.66 us -> 0.01 us  [local(): jnp.concatenate([far, lax.dynamic_slice_in_dim(chunk, (gz ^ k) * n.chunk,...]
  transfers between devices with their start and end apart: 10 -> 10, of which waited for: 6 -> 6; matrix products, arithmetic and copies ran while one was open for 0% -> 0% of each run, Pallas kernels for 10% -> 9%
where the time goes in v5:
time: 34.5 us; the launch traced here: 34.3 us
  starting transfers between devices  13.6 us (39%)
  Pallas kernels  9.98 us (29%)
  waiting for transfers between devices  9.23 us (27%)
  between operations  1.41 us (4%)
    ppermute x10, starting transfers between devices, exchange(): return lax.ppermute(values, axes if len(axes) > 1 else axes[0], pairs)  13.6 us
    ppermute x10, waiting for transfers between devices, exchange(): return lax.ppermute(values, axes if len(axes) > 1 else axes[0], pairs)  9.23 us
    pallas_call x1, Pallas kernels, local(): pl.pallas_call(functools.partial(main_kernel, n), name='window', out_shap...  3.8 us
    pallas_call x1, Pallas kernels, local(): pl.pallas_call(functools.partial(table_kernel, n), name='tables', out_sha...  3.16 us
    pallas_call x1, Pallas kernels, local(): pl.pallas_call(functools.partial(adjoint_kernel, n), name='adjoint', out_...  1.99 us
    pallas_call x1, Pallas kernels, local(): pl.pallas_call(functools.partial(pack_kernel, n), name='pack', out_shape=...  0.97 us
  transfers between devices with their start and end apart: 10, of which 6 were waited for; matrix products, arithmetic and copies ran while one was open for 0% of the time, Pallas kernels for 9%

profile of v5, /device:TPU:0, one launch (start us, length us, event | category | flops | bytes accessed | tf_op | source)
XLA Modules:
  0.0 34.3 jit_solution(9443909045213477621)
XLA Ops:
  0.6 1.0 %pack.1 = (f32[7,4,16,128]{3,2,1,0:T(8,128)S(1)}, f32[336,128]{1,0:T(8,128)S(1)}) custom-call(f32[6,4,16,128]{3,2,1,0:T(8,128)} %f_hbm.1, f32[4,16,128]{2,1,0:T(8,128)} %eps_hbm.1), custom_call_target="tpu_custom_call" | custom-call | tf_op jit(solution)/shard_map/pack/pallas_call | solution.py:582
  1.6 0.5 %collective-permute-start = (f32[448,128]{1,0:T(8,128)S(1)}, f32[448,128]{1,0:T(8,128)S(1)}, u32[]{:S(2)}, u32[]{:S(2)}) collective-permute-start(f32[448,128]{1,0:T(8,128)S(1)} %bitcast.11), channel_id=1, source_target_pairs={{0,1},{1,0},{2,3},{3,2},{4,5},{5,4},{6,7},{7,6},{8,9},{9,8},{10,11... | collective-permute-start | bytes 688136 | tf_op jit(solution)/shard_map/ppermute | solution.py:563
  2.1 2.6 %collective-permute-start.1 = (f32[336,128]{1,0:T(8,128)S(1)}, f32[336,128]{1,0:T(8,128)S(1)}, u32[]{:S(2)}, u32[]{:S(2)}) collective-permute-start(f32[336,128]{1,0:T(8,128)S(1)} %get-tuple-element.25), channel_id=1, source_target_pairs={{0,2},{2,0},{1,3},{3,1},{4,6},{6,4},{5,7},{7,5},{8,10},{10,8},{9,1... | collective-permute-start | bytes 516104 | tf_op jit(solution)/shard_map/ppermute | solution.py:563
  5.3 0.0 collective-permute-done.other_ref
  5.4 0.1 edges.1
  5.4 1.6 %collective-permute-start.2 = (f32[176,128]{1,0:T(8,128)S(1)}, f32[176,128]{1,0:T(8,128)S(1)}, u32[]{:S(2)}, u32[]{:S(2)}) collective-permute-start(f32[176,128]{1,0:T(8,128)S(1)} %get-tuple-element.26), channel_id=1, source_target_pairs={{0,4},{1,13},{4,0},{5,9},{8,12},{9,5},{12,8},{13,1},{2,6},{3,15},{... | collective-permute-start | bytes 270344 | tf_op jit(solution)/shard_map/ppermute | solution.py:563
  7.1 0.6 %collective-permute-start.3 = (f32[128,128]{1,0:T(8,128)S(1)}, f32[128,128]{1,0:T(8,128)S(1)}, u32[]{:S(2)}, u32[]{:S(2)}) collective-permute-start(f32[128,128]{1,0:T(8,128)S(1)} %get-tuple-element.28), channel_id=1, source_target_pairs={{0,6},{1,15},{2,4},{3,13},{4,2},{5,11},{6,0},{7,9},{8,14},{9,7},{1... | collective-permute-start | bytes 196616 | tf_op jit(solution)/shard_map/ppermute | solution.py:563
  7.7 0.0 copy-start
  7.7 3.2 %tables.1 = (bf16[576,2048]{1,0:T(8,128)(2,1)S(1)}, f32[48,2048]{1,0:T(8,128)S(1)}, s32[36]{0:T(128)S(1)}, f32[16,128]{1,0:T(8,128)S(1)}) custom-call(s32[16,128]{1,0:T(8,128)} %bitcast.18, s32[2,32]{1,0:T(2,128)} %owner_hbm.1, s32[1,4]{1,0:T(1,128)} %wall_owner_hbm.1, f32[1]{0:T(128)S(6)} %copy.22.phase_hbm), custom_call_target="tpu_custom_call" | custom-call | flops 8589934592 | bytes 16777216 | tf_op jit(solution)/shard_map/tables/pallas_call | solution.py:614
  10.9 0.0 collective-permute-done.1
  10.9 1.4 %collective-permute-done.3 = f32[128,128]{1,0:T(8,128)S(1)} collective-permute-done((f32[128,128]{1,0:T(8,128)S(1)}, f32[128,128]{1,0:T(8,128)S(1)}, u32[]{:S(2)}, u32[]{:S(2)}) %collective-permute-start.3) | collective-permute-done | bytes 65568 | tf_op jit(solution)/shard_map/ppermute | solution.py:563
  12.2 0.0 collective-permute-done.2
  12.3 2.6 %collective-permute-start.4 = (f32[640,128]{1,0:T(8,128)S(1)}, f32[640,128]{1,0:T(8,128)S(1)}, u32[]{:S(2)}, u32[]{:S(2)}) collective-permute-start(f32[640,128]{1,0:T(8,128)S(1)} %constant_dynamic-update-slice_fusion.halo_ref), channel_id=1, source_target_pairs={{0,1},{1,0},{2,3},{3,2},{4,5},{5,4},{6,7},{7,6},{8,9},{9,8},{10,11... | collective-permute-start | bytes 983048 | tf_op jit(solution)/shard_map/ppermute | solution.py:563
  14.9 1.3 %collective-permute-done.4.far_halo_ref = f32[640,128]{1,0:T(8,128)S(1)} collective-permute-done((f32[640,128]{1,0:T(8,128)S(1)}, f32[640,128]{1,0:T(8,128)S(1)}, u32[]{:S(2)}, u32[]{:S(2)}) %collective-permute-start.4) | collective-permute-done | bytes 327712 | tf_op jit(solution)/shard_map/ppermute | solution.py:563
  16.2 0.0 copy-done
  16.2 0.0 copy-start.1
  16.2 0.0 copy-start.2
  16.2 3.8 %window.1 = (f32[6,4,16,128]{3,2,1,0:T(8,128)}, f32[12,4,16,128]{3,2,1,0:T(8,128)}, f32[64,128]{1,0:T(8,128)S(1)}, f32[64,128]{1,0:T(8,128)S(1)}) custom-call(f32[448,128]{1,0:T(8,128)S(1)} %bitcast.13, f32[448,128]{1,0:T(8,128)S(1)} %collective-permute-done.other_ref, f32[640,128]{1,0:T(8,128)S(1)} %constant_dynamic-update-slice_fusion.halo_ref, ...), custom_call_target="tpu_custom_call" | custom-call | tf_op jit(solution)/shard_map/window/pallas_call | solution.py:641
  20.0 0.5 %collective-permute-start.5 = (f32[64,128]{1,0:T(8,128)S(1)}, f32[64,128]{1,0:T(8,128)S(1)}, u32[]{:S(2)}, u32[]{:S(2)}) collective-permute-start(f32[64,128]{1,0:T(8,128)S(1)} %get-tuple-element.38), channel_id=1, source_target_pairs={{0,1},{1,0},{2,3},{3,2},{4,5},{5,4},{6,7},{7,6},{8,9},{9,8},{10,11... | collective-permute-start | bytes 98312 | tf_op jit(solution)/shard_map/ppermute | solution.py:563
  20.4 0.9 %collective-permute-done.5 = f32[64,128]{1,0:T(8,128)S(1)} collective-permute-done((f32[64,128]{1,0:T(8,128)S(1)}, f32[64,128]{1,0:T(8,128)S(1)}, u32[]{:S(2)}, u32[]{:S(2)}) %collective-permute-start.5) | collective-permute-done | bytes 32800 | tf_op jit(solution)/shard_map/ppermute | solution.py:563
  21.3 0.7 %collective-permute-start.6 = (f32[64,128]{1,0:T(8,128)S(1)}, f32[64,128]{1,0:T(8,128)S(1)}, u32[]{:S(2)}, u32[]{:S(2)}) collective-permute-start(f32[64,128]{1,0:T(8,128)S(1)} %add.18), channel_id=1, source_target_pairs={{0,2},{2,0},{1,3},{3,1},{4,6},{6,4},{5,7},{7,5},{8,10},{10,8},{9,1... | collective-permute-start | bytes 98312 | tf_op jit(solution)/shard_map/ppermute | solution.py:563
  22.1 3.2 %collective-permute-done.6 = f32[64,128]{1,0:T(8,128)S(1)} collective-permute-done((f32[64,128]{1,0:T(8,128)S(1)}, f32[64,128]{1,0:T(8,128)S(1)}, u32[]{:S(2)}, u32[]{:S(2)}) %collective-permute-start.6) | collective-permute-done | bytes 32800 | tf_op jit(solution)/shard_map/ppermute | solution.py:563
  25.2 1.9 %collective-permute-start.7 = (f32[80,128]{1,0:T(8,128)S(1)}, f32[80,128]{1,0:T(8,128)S(1)}, u32[]{:S(2)}, u32[]{:S(2)}) collective-permute-start(f32[80,128]{1,0:T(8,128)S(1)} %get-tuple-element.50), channel_id=1, source_target_pairs={{0,12},{4,8},{8,4},{12,0},{1,13},{5,9},{9,5},{13,1},{2,14},{6,10},... | collective-permute-start | bytes 122888 | tf_op jit(solution)/shard_map/ppermute | solution.py:563
  27.1 0.0 collective-permute-start.8
  27.1 2.6 %collective-permute-start.9 = (f32[80,128]{1,0:T(8,128)S(1)}, f32[80,128]{1,0:T(8,128)S(1)}, u32[]{:S(2)}, u32[]{:S(2)}) collective-permute-start(f32[80,128]{1,0:T(8,128)S(1)} %get-tuple-element.48), channel_id=1, source_target_pairs={{0,4},{4,0},{8,12},{12,8},{1,5},{5,1},{9,13},{13,9},{2,6},{6,2},{1... | collective-permute-start | bytes 122888 | tf_op jit(solution)/shard_map/ppermute | solution.py:563
  29.7 1.8 %collective-permute-done.7 = f32[80,128]{1,0:T(8,128)S(1)} collective-permute-done((f32[80,128]{1,0:T(8,128)S(1)}, f32[80,128]{1,0:T(8,128)S(1)}, u32[]{:S(2)}, u32[]{:S(2)}) %collective-permute-start.7) | collective-permute-done | bytes 40992 | tf_op jit(solution)/shard_map/ppermute | solution.py:563
  31.5 0.8 %collective-permute-done.8 = f32[80,128]{1,0:T(8,128)S(1)} collective-permute-done((f32[80,128]{1,0:T(8,128)S(1)}, f32[80,128]{1,0:T(8,128)S(1)}, u32[]{:S(2)}, u32[]{:S(2)}) %collective-permute-start.8) | collective-permute-done | bytes 40992 | tf_op jit(solution)/shard_map/ppermute | solution.py:563
  32.3 0.0 collective-permute-done.9
  32.3 0.0 copy-done.1
  32.3 0.0 copy-done.2
  32.4 2.0 %adjoint.1 = (f32[1,128]{1,0:T(1,128)}, f32[20,1,128]{2,1,0:T(1,128)}, f32[36,1,128]{2,1,0:T(1,128)}) custom-call(f32[320,128]{1,0:T(8,128)S(1)} %constant_dynamic-update-slice_fusion.3.far_ref, f32[16,128]{1,0:T(8,128)S(1)} %bitcast.14, s32[16,128]{1,0:T(8,128)S(1)} %bitcast.15, bf16[576,2048]{1,0:T(8,128)(2,1)S(1)} %get-tuple-element.34.hi_lo_ref, ...), custom_call_target="tpu_custom_call" | custom-call | tf_op jit(solution)/shard_map/adjoint/pallas_call | solution.py:677
  (12 shorter events, 0.1 us)
Async XLA Ops:
  1.6 3.7 %collective-permute-start = (f32[448,128]{1,0:T(8,128)S(1)}, f32[448,128]{1,0:T(8,128)S(1)}, u32[]{:S(2)}, u32[]{:S(2)}) collective-permute-start(f32[448,128]{1,0:T(8,128)S(1)} %bitcast.11), channel_id=1, source_target_pairs={{0,1},{1,0},{2,3},{3,2},{4,5},{5,4},{6,7},{7,6},{8,9},{9,8},{10,11... | collective-permute-start | bytes 688136 | tf_op jit(solution)/shard_map/ppermute | solution.py:563
  2.1 8.7 %collective-permute-start.1 = (f32[336,128]{1,0:T(8,128)S(1)}, f32[336,128]{1,0:T(8,128)S(1)}, u32[]{:S(2)}, u32[]{:S(2)}) collective-permute-start(f32[336,128]{1,0:T(8,128)S(1)} %get-tuple-element.25), channel_id=1, source_target_pairs={{0,2},{2,0},{1,3},{3,1},{4,6},{6,4},{5,7},{7,5},{8,10},{10,8},{9,1... | collective-permute-start | bytes 516104 | tf_op jit(solution)/shard_map/ppermute | solution.py:563
  5.4 6.8 %collective-permute-start.2 = (f32[176,128]{1,0:T(8,128)S(1)}, f32[176,128]{1,0:T(8,128)S(1)}, u32[]{:S(2)}, u32[]{:S(2)}) collective-permute-start(f32[176,128]{1,0:T(8,128)S(1)} %get-tuple-element.26), channel_id=1, source_target_pairs={{0,4},{1,13},{4,0},{5,9},{8,12},{9,5},{12,8},{13,1},{2,6},{3,15},{... | collective-permute-start | bytes 270344 | tf_op jit(solution)/shard_map/ppermute | solution.py:563
  7.1 5.2 %collective-permute-start.3 = (f32[128,128]{1,0:T(8,128)S(1)}, f32[128,128]{1,0:T(8,128)S(1)}, u32[]{:S(2)}, u32[]{:S(2)}) collective-permute-start(f32[128,128]{1,0:T(8,128)S(1)} %get-tuple-element.28), channel_id=1, source_target_pairs={{0,6},{1,15},{2,4},{3,13},{4,2},{5,11},{6,0},{7,9},{8,14},{9,7},{1... | collective-permute-start | bytes 196616 | tf_op jit(solution)/shard_map/ppermute | solution.py:563
  7.7 8.5 %copy-start = (f32[12,4,16,128]{3,2,1,0:T(8,128)S(1)}, f32[12,4,16,128]{3,2,1,0:T(8,128)}, u32[]{:S(2)}) copy-start(f32[12,4,16,128]{3,2,1,0:T(8,128)} %spectra_hbm.1) | copy-start | bytes 1179652
  12.3 3.9 %collective-permute-start.4 = (f32[640,128]{1,0:T(8,128)S(1)}, f32[640,128]{1,0:T(8,128)S(1)}, u32[]{:S(2)}, u32[]{:S(2)}) collective-permute-start(f32[640,128]{1,0:T(8,128)S(1)} %constant_dynamic-update-slice_fusion.halo_ref), channel_id=1, source_target_pairs={{0,1},{1,0},{2,3},{3,2},{4,5},{5,4},{6,7},{7,6},{8,9},{9,8},{10,11... | collective-permute-start | bytes 983048 | tf_op jit(solution)/shard_map/ppermute | solution.py:563
  16.2 16.2 %copy-start.1 = (f32[2048]{0:T(1024)S(1)}, f32[2048]{0:T(1024)}, u32[]{:S(2)}) copy-start(f32[2048]{0:T(1024)} %param.16) | copy-start | bytes 24580
  16.2 16.2 %copy-start.2 = (s32[2048]{0:T(1024)S(1)}, s32[2048]{0:T(1024)}, u32[]{:S(2)}) copy-start(s32[2048]{0:T(1024)} %param.17) | copy-start | bytes 24580
  20.0 1.3 %collective-permute-start.5 = (f32[64,128]{1,0:T(8,128)S(1)}, f32[64,128]{1,0:T(8,128)S(1)}, u32[]{:S(2)}, u32[]{:S(2)}) collective-permute-start(f32[64,128]{1,0:T(8,128)S(1)} %get-tuple-element.38), channel_id=1, source_target_pairs={{0,1},{1,0},{2,3},{3,2},{4,5},{5,4},{6,7},{7,6},{8,9},{9,8},{10,11... | collective-permute-start | bytes 98312 | tf_op jit(solution)/shard_map/ppermute | solution.py:563
  21.3 3.9 %collective-permute-start.6 = (f32[64,128]{1,0:T(8,128)S(1)}, f32[64,128]{1,0:T(8,128)S(1)}, u32[]{:S(2)}, u32[]{:S(2)}) collective-permute-start(f32[64,128]{1,0:T(8,128)S(1)} %add.18), channel_id=1, source_target_pairs={{0,2},{2,0},{1,3},{3,1},{4,6},{6,4},{5,7},{7,5},{8,10},{10,8},{9,1... | collective-permute-start | bytes 98312 | tf_op jit(solution)/shard_map/ppermute | solution.py:563
  25.2 6.3 %collective-permute-start.7 = (f32[80,128]{1,0:T(8,128)S(1)}, f32[80,128]{1,0:T(8,128)S(1)}, u32[]{:S(2)}, u32[]{:S(2)}) collective-permute-start(f32[80,128]{1,0:T(8,128)S(1)} %get-tuple-element.50), channel_id=1, source_target_pairs={{0,12},{4,8},{8,4},{12,0},{1,13},{5,9},{9,5},{13,1},{2,14},{6,10},... | collective-permute-start | bytes 122888 | tf_op jit(solution)/shard_map/ppermute | solution.py:563
  27.1 5.2 %collective-permute-start.8 = (f32[80,128]{1,0:T(8,128)S(1)}, f32[80,128]{1,0:T(8,128)S(1)}, u32[]{:S(2)}, u32[]{:S(2)}) collective-permute-start(f32[80,128]{1,0:T(8,128)S(1)} %get-tuple-element.49), channel_id=1, source_target_pairs={{0,8},{4,12},{8,0},{12,4},{1,9},{5,13},{9,1},{13,5},{2,10},{6,14},... | collective-permute-start | bytes 122888 | tf_op jit(solution)/shard_map/ppermute | solution.py:563
  27.1 5.2 %collective-permute-start.9 = (f32[80,128]{1,0:T(8,128)S(1)}, f32[80,128]{1,0:T(8,128)S(1)}, u32[]{:S(2)}, u32[]{:S(2)}) collective-permute-start(f32[80,128]{1,0:T(8,128)S(1)} %get-tuple-element.48), channel_id=1, source_target_pairs={{0,4},{4,0},{8,12},{12,8},{1,5},{5,1},{9,13},{13,9},{2,6},{6,2},{1... | collective-permute-start | bytes 122888 | tf_op jit(solution)/shard_map/ppermute | solution.py:563

commit v6 on v5

--- a/solution.py
+++ b/solution.py
@@ -137,8 +137,8 @@
 
 
 def table_kernel(
-    n, dir_hbm, owner_hbm, wall_owner_hbm, phase_hbm, hi_lo_ref, v_ref, place_ref, turn_ref,
-    count_ref, dir_ref, owner_ref, wall_owner_ref, phase_ref, sems,
+    n, dir_hbm, owner_hbm, wall_owner_hbm, phase_ref, hi_lo_ref, v_ref, place_ref, turn_ref,
+    count_ref, dir_ref, owner_ref, wall_owner_ref, sems,
 ):
     gz, dev, xy = (lax.axis_index(a) for a in ("gz", "dev", "xy"))
     hi_ref, lo_ref = halves(n, hi_lo_ref)
@@ -149,7 +149,6 @@
                 (dir_hbm, dir_ref),
                 (owner_hbm, owner_ref),
                 (wall_owner_hbm, wall_owner_ref),
-                (phase_hbm, phase_ref),
             )
         )
     ]
@@ -217,10 +216,11 @@
             w_theta = weights([-th[i], -th[j], -ph[i], -ph[j]]) * scale
             w_phi = weights([-ph[i], -ph[j], th[i], th[j]]) * scale
             for kind, value in enumerate((w_theta, w_phi)):
-                at = 16 + (face * 2 + kind) * 8
+                at = 16 * n.y + (face * 2 + kind) * 8
                 v_ref[at : at + 8, lanes] = value
-        v_ref[0:8, lanes] = base_c
-        v_ref[8:16, lanes] = base_s
+        for r in range(2 * n.y):
+            factor = jnp.where(low, base_c[r : r + 1, :], -base_s[r : r + 1, :])
+            v_ref[8 * r : 8 * r + 8, lanes] = factor
     for o in range(n.gz):
         count_ref[o] = 0
     which = jnp.where(gz == 0, 0, 1)
@@ -259,14 +259,13 @@
 
 
 def patch_factors(n, v_ref, face, lanes):
-    low = rows_iota((8, LANES)) < 4
-    base_c, base_s = v_ref[0:8, lanes], v_ref[8:16, lanes]
-    at = [face * 4 + y for y in range(n.y)]
-    return [jnp.where(low, base_c[r : r + 1, :], -base_s[r : r + 1, :]) for r in at]
-
-
-def face_weights(v_ref, face, lanes):
-    return (v_ref[16 + face * 16 + 8 * kind : 24 + face * 16 + 8 * kind, lanes] for kind in range(2))
+    at = [(face * n.y + y) * 8 for y in range(n.y)]
+    return [v_ref[r : r + 8, lanes] for r in at]
+
+
+def face_weights(n, v_ref, face, lanes):
+    at = [16 * n.y + (face * 2 + kind) * 8 for kind in range(2)]
+    return [v_ref[r : r + 8, lanes] for r in at]
 
 
 def turn(values):
@@ -457,7 +456,7 @@
                     rows = sums[face][y * 8 : y * 8 + 8, t * LANES : (t + 1) * LANES]
                     even = even + factor * rows
                     odd = odd - factor * turn(rows)
-                w_theta, w_phi = face_weights(v_ref, face, lanes)
+                w_theta, w_phi = face_weights(n, v_ref, face, lanes)
                 for kind, term in enumerate((w_theta * even, w_phi * even, w_theta * odd, w_phi * odd)):
                     totals[kind] = totals[kind] + term
             for kind, total in enumerate(totals):
@@ -496,7 +495,7 @@
     for face in range(2):
         for t in range(n.tiles):
             lanes = slice(t * LANES, (t + 1) * LANES)
-            w_theta, w_phi = face_weights(v_ref, face, lanes)
+            w_theta, w_phi = face_weights(n, v_ref, face, lanes)
             even, odd = (
                 w_theta * slopes[k][t : t + 1, :] + w_phi * slopes[k + 1][t : t + 1, :] for k in (0, 2)
             )
@@ -616,19 +615,18 @@
         name="tables",
         out_shape=[
             out(2 * n.table_rows, n.dirs, dtype=BF16),
-            out(48, n.dirs),
+            out(16 * n.y + 32, n.dirs),
             out(n.caps + n.walls, dtype=jnp.int32),
             out(16, LANES),
         ],
-        in_specs=[HBM] * 4,
+        in_specs=[HBM] * 3 + [SMEM],
         out_specs=[VMEM] * 2 + [SMEM, VMEM],
         scratch_shapes=[
             pltpu.SMEM((n.gz,), jnp.int32),
             pltpu.VMEM((n.tiles, LANES), jnp.int32),
             pltpu.SMEM(cap_owner.shape, jnp.int32),
             pltpu.SMEM(wall_owner.shape, jnp.int32),
-            pltpu.SMEM(phase_start.shape, F32),
-            pltpu.SemaphoreType.DMA((4,)),
+            pltpu.SemaphoreType.DMA((3,)),
         ],
         compiler_params=params(8),
         cost_estimate=pl.CostEstimate(flops=1 << 33, bytes_accessed=16 << 20, transcendentals=0),

time: 34.5 us -> 34.4 us (level)
  transfers between devices with their start and end apart: 10 -> 10, of which waited for: 6 -> 6; matrix products, arithmetic and copies ran while one was open for 0% -> 0% of each run, Pallas kernels for 9% -> 10%
where the time goes in v6:
time: 34.4 us; the launch traced here: 34.3 us
  starting transfers between devices  13.6 us (40%)
  Pallas kernels  9.95 us (29%)
  waiting for transfers between devices  9.18 us (27%)
  between operations  1.41 us (4%)
    ppermute x10, starting transfers between devices, exchange(): return lax.ppermute(values, axes if len(axes) > 1 else axes[0], pairs)  13.6 us
    ppermute x10, waiting for transfers between devices, exchange(): return lax.ppermute(values, axes if len(axes) > 1 else axes[0], pairs)  9.18 us
    pallas_call x1, Pallas kernels, local(): pl.pallas_call(functools.partial(main_kernel, n), name='window', out_shap...  3.73 us
    pallas_call x1, Pallas kernels, local(): pl.pallas_call(functools.partial(table_kernel, n), name='tables', out_sha...  3.2 us
    pallas_call x1, Pallas kernels, local(): pl.pallas_call(functools.partial(adjoint_kernel, n), name='adjoint', out_...  1.99 us
    pallas_call x1, Pallas kernels, local(): pl.pallas_call(functools.partial(pack_kernel, n), name='pack', out_shape=...  0.97 us
  transfers between devices with their start and end apart: 10, of which 6 were waited for; matrix products, arithmetic and copies ran while one was open for 0% of the time, Pallas kernels for 10%

profile of v6, /device:TPU:0, one launch (start us, length us, event | category | flops | bytes accessed | tf_op | source)
XLA Modules:
  0.0 34.3 jit_solution(1321552113366575496)
XLA Ops:
  0.6 1.0 %pack.1 = (f32[7,4,16,128]{3,2,1,0:T(8,128)S(1)}, f32[336,128]{1,0:T(8,128)S(1)}) custom-call(f32[6,4,16,128]{3,2,1,0:T(8,128)} %f_hbm.1, f32[4,16,128]{2,1,0:T(8,128)} %eps_hbm.1), custom_call_target="tpu_custom_call" | custom-call | tf_op jit(solution)/shard_map/pack/pallas_call | solution.py:581
  1.6 0.5 %collective-permute-start = (f32[448,128]{1,0:T(8,128)S(1)}, f32[448,128]{1,0:T(8,128)S(1)}, u32[]{:S(2)}, u32[]{:S(2)}) collective-permute-start(f32[448,128]{1,0:T(8,128)S(1)} %bitcast.11), channel_id=1, source_target_pairs={{0,1},{1,0},{2,3},{3,2},{4,5},{5,4},{6,7},{7,6},{8,9},{9,8},{10,11... | collective-permute-start | bytes 688136 | tf_op jit(solution)/shard_map/ppermute | solution.py:562
  2.1 2.6 %collective-permute-start.1 = (f32[336,128]{1,0:T(8,128)S(1)}, f32[336,128]{1,0:T(8,128)S(1)}, u32[]{:S(2)}, u32[]{:S(2)}) collective-permute-start(f32[336,128]{1,0:T(8,128)S(1)} %get-tuple-element.25), channel_id=1, source_target_pairs={{0,2},{2,0},{1,3},{3,1},{4,6},{6,4},{5,7},{7,5},{8,10},{10,8},{9,1... | collective-permute-start | bytes 516104 | tf_op jit(solution)/shard_map/ppermute | solution.py:562
  5.3 0.0 collective-permute-done.other_ref
  5.4 0.1 edges.1
  5.4 1.6 %collective-permute-start.2 = (f32[176,128]{1,0:T(8,128)S(1)}, f32[176,128]{1,0:T(8,128)S(1)}, u32[]{:S(2)}, u32[]{:S(2)}) collective-permute-start(f32[176,128]{1,0:T(8,128)S(1)} %get-tuple-element.26), channel_id=1, source_target_pairs={{0,4},{1,13},{4,0},{5,9},{8,12},{9,5},{12,8},{13,1},{2,6},{3,15},{... | collective-permute-start | bytes 270344 | tf_op jit(solution)/shard_map/ppermute | solution.py:562
  7.1 0.6 %collective-permute-start.3 = (f32[128,128]{1,0:T(8,128)S(1)}, f32[128,128]{1,0:T(8,128)S(1)}, u32[]{:S(2)}, u32[]{:S(2)}) collective-permute-start(f32[128,128]{1,0:T(8,128)S(1)} %get-tuple-element.28), channel_id=1, source_target_pairs={{0,6},{1,15},{2,4},{3,13},{4,2},{5,11},{6,0},{7,9},{8,14},{9,7},{1... | collective-permute-start | bytes 196616 | tf_op jit(solution)/shard_map/ppermute | solution.py:562
  7.7 0.0 copy-start
  7.7 3.2 %tables.1 = (bf16[576,2048]{1,0:T(8,128)(2,1)S(1)}, f32[96,2048]{1,0:T(8,128)S(1)}, s32[36]{0:T(128)S(1)}, f32[16,128]{1,0:T(8,128)S(1)}) custom-call(s32[16,128]{1,0:T(8,128)} %bitcast.18, s32[2,32]{1,0:T(2,128)} %owner_hbm.1, s32[1,4]{1,0:T(1,128)} %wall_owner_hbm.1, f32[1]{0:T(128)S(6)} %copy.22.phase_ref), custom_call_target="tpu_custom_call" | custom-call | flops 8589934592 | bytes 16777216 | tf_op jit(solution)/shard_map/tables/pallas_call | solution.py:613
  10.9 0.0 collective-permute-done.1
  10.9 1.3 %collective-permute-done.3 = f32[128,128]{1,0:T(8,128)S(1)} collective-permute-done((f32[128,128]{1,0:T(8,128)S(1)}, f32[128,128]{1,0:T(8,128)S(1)}, u32[]{:S(2)}, u32[]{:S(2)}) %collective-permute-start.3) | collective-permute-done | bytes 65568 | tf_op jit(solution)/shard_map/ppermute | solution.py:562
  12.2 0.0 collective-permute-done.2
  12.3 2.6 %collective-permute-start.4 = (f32[640,128]{1,0:T(8,128)S(1)}, f32[640,128]{1,0:T(8,128)S(1)}, u32[]{:S(2)}, u32[]{:S(2)}) collective-permute-start(f32[640,128]{1,0:T(8,128)S(1)} %constant_dynamic-update-slice_fusion.halo_ref), channel_id=1, source_target_pairs={{0,1},{1,0},{2,3},{3,2},{4,5},{5,4},{6,7},{7,6},{8,9},{9,8},{10,11... | collective-permute-start | bytes 983048 | tf_op jit(solution)/shard_map/ppermute | solution.py:562
  14.9 1.3 %collective-permute-done.4.far_halo_ref = f32[640,128]{1,0:T(8,128)S(1)} collective-permute-done((f32[640,128]{1,0:T(8,128)S(1)}, f32[640,128]{1,0:T(8,128)S(1)}, u32[]{:S(2)}, u32[]{:S(2)}) %collective-permute-start.4) | collective-permute-done | bytes 327712 | tf_op jit(solution)/shard_map/ppermute | solution.py:562
  16.2 0.0 copy-done
  16.2 0.0 copy-start.1
  16.2 0.0 copy-start.2
  16.2 3.7 %window.1 = (f32[6,4,16,128]{3,2,1,0:T(8,128)}, f32[12,4,16,128]{3,2,1,0:T(8,128)}, f32[64,128]{1,0:T(8,128)S(1)}, f32[64,128]{1,0:T(8,128)S(1)}) custom-call(f32[448,128]{1,0:T(8,128)S(1)} %bitcast.13, f32[448,128]{1,0:T(8,128)S(1)} %collective-permute-done.other_ref, f32[640,128]{1,0:T(8,128)S(1)} %constant_dynamic-update-slice_fusion.halo_ref, ...), custom_call_target="tpu_custom_call" | custom-call | tf_op jit(solution)/shard_map/window/pallas_call | solution.py:639
  19.9 0.5 %collective-permute-start.5 = (f32[64,128]{1,0:T(8,128)S(1)}, f32[64,128]{1,0:T(8,128)S(1)}, u32[]{:S(2)}, u32[]{:S(2)}) collective-permute-start(f32[64,128]{1,0:T(8,128)S(1)} %get-tuple-element.38), channel_id=1, source_target_pairs={{0,1},{1,0},{2,3},{3,2},{4,5},{5,4},{6,7},{7,6},{8,9},{9,8},{10,11... | collective-permute-start | bytes 98312 | tf_op jit(solution)/shard_map/ppermute | solution.py:562
  20.4 0.9 %collective-permute-done.5 = f32[64,128]{1,0:T(8,128)S(1)} collective-permute-done((f32[64,128]{1,0:T(8,128)S(1)}, f32[64,128]{1,0:T(8,128)S(1)}, u32[]{:S(2)}, u32[]{:S(2)}) %collective-permute-start.5) | collective-permute-done | bytes 32800 | tf_op jit(solution)/shard_map/ppermute | solution.py:562
  21.2 0.7 %collective-permute-start.6 = (f32[64,128]{1,0:T(8,128)S(1)}, f32[64,128]{1,0:T(8,128)S(1)}, u32[]{:S(2)}, u32[]{:S(2)}) collective-permute-start(f32[64,128]{1,0:T(8,128)S(1)} %add.18), channel_id=1, source_target_pairs={{0,2},{2,0},{1,3},{3,1},{4,6},{6,4},{5,7},{7,5},{8,10},{10,8},{9,1... | collective-permute-start | bytes 98312 | tf_op jit(solution)/shard_map/ppermute | solution.py:562
  22.0 3.2 %collective-permute-done.6 = f32[64,128]{1,0:T(8,128)S(1)} collective-permute-done((f32[64,128]{1,0:T(8,128)S(1)}, f32[64,128]{1,0:T(8,128)S(1)}, u32[]{:S(2)}, u32[]{:S(2)}) %collective-permute-start.6) | collective-permute-done | bytes 32800 | tf_op jit(solution)/shard_map/ppermute | solution.py:562
  25.2 1.9 %collective-permute-start.7 = (f32[80,128]{1,0:T(8,128)S(1)}, f32[80,128]{1,0:T(8,128)S(1)}, u32[]{:S(2)}, u32[]{:S(2)}) collective-permute-start(f32[80,128]{1,0:T(8,128)S(1)} %get-tuple-element.50), channel_id=1, source_target_pairs={{0,12},{4,8},{8,4},{12,0},{1,13},{5,9},{9,5},{13,1},{2,14},{6,10},... | collective-permute-start | bytes 122888 | tf_op jit(solution)/shard_map/ppermute | solution.py:562
  27.0 0.0 collective-permute-start.8
  27.0 2.6 %collective-permute-start.9 = (f32[80,128]{1,0:T(8,128)S(1)}, f32[80,128]{1,0:T(8,128)S(1)}, u32[]{:S(2)}, u32[]{:S(2)}) collective-permute-start(f32[80,128]{1,0:T(8,128)S(1)} %get-tuple-element.48), channel_id=1, source_target_pairs={{0,4},{4,0},{8,12},{12,8},{1,5},{5,1},{9,13},{13,9},{2,6},{6,2},{1... | collective-permute-start | bytes 122888 | tf_op jit(solution)/shard_map/ppermute | solution.py:562
  29.6 1.8 %collective-permute-done.7 = f32[80,128]{1,0:T(8,128)S(1)} collective-permute-done((f32[80,128]{1,0:T(8,128)S(1)}, f32[80,128]{1,0:T(8,128)S(1)}, u32[]{:S(2)}, u32[]{:S(2)}) %collective-permute-start.7) | collective-permute-done | bytes 40992 | tf_op jit(solution)/shard_map/ppermute | solution.py:562
  31.4 0.8 %collective-permute-done.8 = f32[80,128]{1,0:T(8,128)S(1)} collective-permute-done((f32[80,128]{1,0:T(8,128)S(1)}, f32[80,128]{1,0:T(8,128)S(1)}, u32[]{:S(2)}, u32[]{:S(2)}) %collective-permute-start.8) | collective-permute-done | bytes 40992 | tf_op jit(solution)/shard_map/ppermute | solution.py:562
  32.2 0.0 collective-permute-done.9
  32.3 0.0 copy-done.1
  32.3 0.0 copy-done.2
  32.3 2.0 %adjoint.1 = (f32[1,128]{1,0:T(1,128)}, f32[20,1,128]{2,1,0:T(1,128)}, f32[36,1,128]{2,1,0:T(1,128)}) custom-call(f32[320,128]{1,0:T(8,128)S(1)} %constant_dynamic-update-slice_fusion.3.far_ref, f32[16,128]{1,0:T(8,128)S(1)} %bitcast.14, s32[16,128]{1,0:T(8,128)S(1)} %bitcast.15, bf16[576,2048]{1,0:T(8,128)(2,1)S(1)} %get-tuple-element.34.hi_lo_ref, ...), custom_call_target="tpu_custom_call" | custom-call | tf_op jit(solution)/shard_map/adjoint/pallas_call | solution.py:675
  (12 shorter events, 0.1 us)
Async XLA Ops:
  1.6 3.7 %collective-permute-start = (f32[448,128]{1,0:T(8,128)S(1)}, f32[448,128]{1,0:T(8,128)S(1)}, u32[]{:S(2)}, u32[]{:S(2)}) collective-permute-start(f32[448,128]{1,0:T(8,128)S(1)} %bitcast.11), channel_id=1, source_target_pairs={{0,1},{1,0},{2,3},{3,2},{4,5},{5,4},{6,7},{7,6},{8,9},{9,8},{10,11... | collective-permute-start | bytes 688136 | tf_op jit(solution)/shard_map/ppermute | solution.py:562
  2.1 8.8 %collective-permute-start.1 = (f32[336,128]{1,0:T(8,128)S(1)}, f32[336,128]{1,0:T(8,128)S(1)}, u32[]{:S(2)}, u32[]{:S(2)}) collective-permute-start(f32[336,128]{1,0:T(8,128)S(1)} %get-tuple-element.25), channel_id=1, source_target_pairs={{0,2},{2,0},{1,3},{3,1},{4,6},{6,4},{5,7},{7,5},{8,10},{10,8},{9,1... | collective-permute-start | bytes 516104 | tf_op jit(solution)/shard_map/ppermute | solution.py:562
  5.4 6.8 %collective-permute-start.2 = (f32[176,128]{1,0:T(8,128)S(1)}, f32[176,128]{1,0:T(8,128)S(1)}, u32[]{:S(2)}, u32[]{:S(2)}) collective-permute-start(f32[176,128]{1,0:T(8,128)S(1)} %get-tuple-element.26), channel_id=1, source_target_pairs={{0,4},{1,13},{4,0},{5,9},{8,12},{9,5},{12,8},{13,1},{2,6},{3,15},{... | collective-permute-start | bytes 270344 | tf_op jit(solution)/shard_map/ppermute | solution.py:562
  7.1 5.2 %collective-permute-start.3 = (f32[128,128]{1,0:T(8,128)S(1)}, f32[128,128]{1,0:T(8,128)S(1)}, u32[]{:S(2)}, u32[]{:S(2)}) collective-permute-start(f32[128,128]{1,0:T(8,128)S(1)} %get-tuple-element.28), channel_id=1, source_target_pairs={{0,6},{1,15},{2,4},{3,13},{4,2},{5,11},{6,0},{7,9},{8,14},{9,7},{1... | collective-permute-start | bytes 196616 | tf_op jit(solution)/shard_map/ppermute | solution.py:562
  7.7 8.5 %copy-start = (f32[12,4,16,128]{3,2,1,0:T(8,128)S(1)}, f32[12,4,16,128]{3,2,1,0:T(8,128)}, u32[]{:S(2)}) copy-start(f32[12,4,16,128]{3,2,1,0:T(8,128)} %spectra_hbm.1) | copy-start | bytes 1179652
  12.3 3.9 %collective-permute-start.4 = (f32[640,128]{1,0:T(8,128)S(1)}, f32[640,128]{1,0:T(8,128)S(1)}, u32[]{:S(2)}, u32[]{:S(2)}) collective-permute-start(f32[640,128]{1,0:T(8,128)S(1)} %constant_dynamic-update-slice_fusion.halo_ref), channel_id=1, source_target_pairs={{0,1},{1,0},{2,3},{3,2},{4,5},{5,4},{6,7},{7,6},{8,9},{9,8},{10,11... | collective-permute-start | bytes 983048 | tf_op jit(solution)/shard_map/ppermute | solution.py:562
  16.2 16.1 %copy-start.1 = (f32[2048]{0:T(1024)S(1)}, f32[2048]{0:T(1024)}, u32[]{:S(2)}) copy-start(f32[2048]{0:T(1024)} %param.16) | copy-start | bytes 24580
  16.2 16.1 %copy-start.2 = (s32[2048]{0:T(1024)S(1)}, s32[2048]{0:T(1024)}, u32[]{:S(2)}) copy-start(s32[2048]{0:T(1024)} %param.17) | copy-start | bytes 24580
  19.9 1.3 %collective-permute-start.5 = (f32[64,128]{1,0:T(8,128)S(1)}, f32[64,128]{1,0:T(8,128)S(1)}, u32[]{:S(2)}, u32[]{:S(2)}) collective-permute-start(f32[64,128]{1,0:T(8,128)S(1)} %get-tuple-element.38), channel_id=1, source_target_pairs={{0,1},{1,0},{2,3},{3,2},{4,5},{5,4},{6,7},{7,6},{8,9},{9,8},{10,11... | collective-permute-start | bytes 98312 | tf_op jit(solution)/shard_map/ppermute | solution.py:562
  21.2 3.9 %collective-permute-start.6 = (f32[64,128]{1,0:T(8,128)S(1)}, f32[64,128]{1,0:T(8,128)S(1)}, u32[]{:S(2)}, u32[]{:S(2)}) collective-permute-start(f32[64,128]{1,0:T(8,128)S(1)} %add.18), channel_id=1, source_target_pairs={{0,2},{2,0},{1,3},{3,1},{4,6},{6,4},{5,7},{7,5},{8,10},{10,8},{9,1... | collective-permute-start | bytes 98312 | tf_op jit(solution)/shard_map/ppermute | solution.py:562
  25.2 6.3 %collective-permute-start.7 = (f32[80,128]{1,0:T(8,128)S(1)}, f32[80,128]{1,0:T(8,128)S(1)}, u32[]{:S(2)}, u32[]{:S(2)}) collective-permute-start(f32[80,128]{1,0:T(8,128)S(1)} %get-tuple-element.50), channel_id=1, source_target_pairs={{0,12},{4,8},{8,4},{12,0},{1,13},{5,9},{9,5},{13,1},{2,14},{6,10},... | collective-permute-start | bytes 122888 | tf_op jit(solution)/shard_map/ppermute | solution.py:562
  27.0 5.2 %collective-permute-start.8 = (f32[80,128]{1,0:T(8,128)S(1)}, f32[80,128]{1,0:T(8,128)S(1)}, u32[]{:S(2)}, u32[]{:S(2)}) collective-permute-start(f32[80,128]{1,0:T(8,128)S(1)} %get-tuple-element.49), channel_id=1, source_target_pairs={{0,8},{4,12},{8,0},{12,4},{1,9},{5,13},{9,1},{13,5},{2,10},{6,14},... | collective-permute-start | bytes 122888 | tf_op jit(solution)/shard_map/ppermute | solution.py:562
  27.0 5.2 %collective-permute-start.9 = (f32[80,128]{1,0:T(8,128)S(1)}, f32[80,128]{1,0:T(8,128)S(1)}, u32[]{:S(2)}, u32[]{:S(2)}) collective-permute-start(f32[80,128]{1,0:T(8,128)S(1)} %get-tuple-element.48), channel_id=1, source_target_pairs={{0,4},{4,0},{8,12},{12,8},{1,5},{5,1},{9,13},{13,9},{2,6},{6,2},{1... | collective-permute-start | bytes 122888 | tf_op jit(solution)/shard_map/ppermute | solution.py:562

commit v7 on v6

--- a/solution.py
+++ b/solution.py
@@ -137,7 +137,7 @@
 
 
 def table_kernel(
-    n, dir_hbm, owner_hbm, wall_owner_hbm, phase_ref, hi_lo_ref, v_ref, place_ref, turn_ref,
+    n, dir_hbm, owner_hbm, wall_owner_hbm, hi_lo_ref, v_ref, place_ref,
     count_ref, dir_ref, owner_ref, wall_owner_ref, sems,
 ):
     gz, dev, xy = (lax.axis_index(a) for a in ("gz", "dev", "xy"))
@@ -235,11 +235,6 @@
     lax.fori_loop(0, n.caps, place, 0)
     for j in range(n.walls):
         place_ref[n.caps + j] = wall_owner_ref[0, j]
-    step_of = (row8 // 2).astype(F32)
-    part_of = jnp.where((row8 & 1) == 0, 0.5, 1.0)
-    sines, cosines = sincos(phase_ref[0] + ANGULAR_STEP * (step_of + part_of))
-    turn_ref[0:8, :] = cosines
-    turn_ref[8:16, :] = sines
 
 
 def halves(n, hi_lo_ref):
@@ -274,7 +269,7 @@
 
 
 def main_kernel(
-    n, own_ref, other_ref, halo_ref, far_halo_ref, spectra_hbm, place_ref, turn_ref, hi_lo_ref, v_ref,
+    n, own_ref, other_ref, halo_ref, far_halo_ref, spectra_hbm, place_ref, phase_ref, hi_lo_ref, v_ref,
     fields_hbm, spectra_out_hbm, far_out, chunk_out, a_ref, m_ref, fields_out, spectra_out, sems,
 ):
     hi_ref, lo_ref = halves(n, hi_lo_ref)
@@ -359,6 +354,10 @@
         return jnp.where(first_x, 0.0, pltpu.roll(v, 1, 1))
 
     own_lanes = pl.ds(pl.multiple_of(xy * n.x, n.x), n.x)
+    angle_row = rows_iota((8, LANES))
+    step_of = (angle_row // 2).astype(F32)
+    part_of = jnp.where((angle_row & 1) == 0, 0.5, 1.0)
+    sines, cosines = sincos(phase_ref[0] + ANGULAR_STEP * (step_of + part_of))
     for step in range(STEPS):
         for y in range(n.rows):
             ex, ey, ez = (a_ref[c, y] for c in range(3))
@@ -386,7 +385,7 @@
             spectra_in.wait()
         for c in range(6):
             row = 2 * step + (1 if c < 3 else 0)
-            cosine, sine = turn_ref[row : row + 1, :], turn_ref[8 + row : 9 + row, :]
+            cosine, sine = cosines[row : row + 1, :], sines[row : row + 1, :]
             for y in range(n.y):
                 value = a_ref[c, y_own + y, 0 : n.z, own_lanes]
                 spectra_out[c, y] = spectra_out[c, y] + value * cosine
@@ -610,17 +609,16 @@
         for k, v in enumerate(e_send)
     ]
 
-    table, v, place, turns = pl.pallas_call(
+    table, v, place = pl.pallas_call(
         functools.partial(table_kernel, n),
         name="tables",
         out_shape=[
             out(2 * n.table_rows, n.dirs, dtype=BF16),
             out(16 * n.y + 32, n.dirs),
             out(n.caps + n.walls, dtype=jnp.int32),
-            out(16, LANES),
         ],
-        in_specs=[HBM] * 3 + [SMEM],
-        out_specs=[VMEM] * 2 + [SMEM, VMEM],
+        in_specs=[HBM] * 3,
+        out_specs=[VMEM] * 2 + [SMEM],
         scratch_shapes=[
             pltpu.SMEM((n.gz,), jnp.int32),
             pltpu.VMEM((n.tiles, LANES), jnp.int32),
@@ -630,8 +628,8 @@
         ],
         compiler_params=params(8),
         cost_estimate=pl.CostEstimate(flops=1 << 33, bytes_accessed=16 << 20, transcendentals=0),
-    )(*map(far_memory, (dir_index.reshape(n.tiles, LANES), cap_owner, wall_owner)), phase_start)
-    (*y_got, z_got, turns), e_got = lax.optimization_barrier(((*y_got, z_got, turns), e_got))
+    )(*map(far_memory, (dir_index.reshape(n.tiles, LANES), cap_owner, wall_owner)))
+    (*y_got, z_got, place), e_got = lax.optimization_barrier(((*y_got, z_got, place), e_got))
     halo = jnp.concatenate([*y_got, z_got, *e_got])
     far_halo = exchange(halo, ("xy",), lambda x: (x ^ 1,))
 
@@ -645,7 +643,7 @@
             out(n.far_rows, LANES),
             out(n.gz * n.chunk, LANES),
         ],
-        in_specs=[VMEM] * 4 + [anywhere, SMEM] + [VMEM] * 3,
+        in_specs=[VMEM] * 4 + [anywhere, SMEM, SMEM] + [VMEM] * 2,
         out_specs=[anywhere] * 2 + [VMEM] * 2,
         scratch_shapes=[
             pltpu.VMEM((7, n.rows, n.z + 8, n.nx), F32),
@@ -655,7 +653,7 @@
             pltpu.SemaphoreType.DMA((3,)),
         ],
         compiler_params=params(12),
-    )(own, other, halo, far_halo, spectra, place, turns, table, v)
+    )(own, other, halo, far_halo, spectra, place, phase_start, table, v)
 
     for axis in ("xy", "dev"):
         size = lax.axis_size(axis)

time: 34.4 us -> 34.1 us (level)
  waiting for transfers between devices: 9.18 us -> 7.96 us
  starting transfers between devices: 13.6 us -> 14.5 us
    ppermute x10, waiting for transfers between devices: 9.18 us -> 7.96 us  [exchange(): return lax.ppermute(values, axes if len(axes) > 1 else axes[0], pairs)]
    ppermute x10, starting transfers between devices: 13.6 us -> 14.5 us  [exchange(): return lax.ppermute(values, axes if len(axes) > 1 else axes[0], pairs)]
where the time goes in v7:
time: 34.1 us; the launch traced here: 33.9 us
  starting transfers between devices  14.5 us (43%)
  Pallas kernels  9.94 us (29%)
  waiting for transfers between devices  7.96 us (23%)
  between operations  1.4 us (4%)
    ppermute x10, starting transfers between devices, exchange(): return lax.ppermute(values, axes if len(axes) > 1 else axes[0], pairs)  14.5 us
    ppermute x10, waiting for transfers between devices, exchange(): return lax.ppermute(values, axes if len(axes) > 1 else axes[0], pairs)  7.96 us
    pallas_call x1, Pallas kernels, local(): pl.pallas_call(functools.partial(main_kernel, n), name='window', out_shap...  3.72 us
    pallas_call x1, Pallas kernels, local(): pl.pallas_call(functools.partial(table_kernel, n), name='tables', out_sha...  3.2 us
    pallas_call x1, Pallas kernels, local(): pl.pallas_call(functools.partial(adjoint_kernel, n), name='adjoint', out_...  1.99 us
    pallas_call x1, Pallas kernels, local(): pl.pallas_call(functools.partial(pack_kernel, n), name='pack', out_shape=...  0.97 us
  transfers between devices with their start and end apart: 10, of which 6 were waited for; matrix products, arithmetic and copies ran while one was open for 0% of the time, Pallas kernels for 10%

profile of v7, /device:TPU:0, one launch (start us, length us, event | category | flops | bytes accessed | tf_op | source)
XLA Modules:
  0.0 33.9 jit_solution(8578869867919236536)
XLA Ops:
  0.6 1.0 %pack.1 = (f32[7,4,16,128]{3,2,1,0:T(8,128)S(1)}, f32[336,128]{1,0:T(8,128)S(1)}) custom-call(f32[6,4,16,128]{3,2,1,0:T(8,128)} %f_hbm.1, f32[4,16,128]{2,1,0:T(8,128)} %eps_hbm.1), custom_call_target="tpu_custom_call" | custom-call | tf_op jit(solution)/shard_map/pack/pallas_call | solution.py:580
  1.6 0.5 %collective-permute-start = (f32[448,128]{1,0:T(8,128)S(1)}, f32[448,128]{1,0:T(8,128)S(1)}, u32[]{:S(2)}, u32[]{:S(2)}) collective-permute-start(f32[448,128]{1,0:T(8,128)S(1)} %bitcast.11), channel_id=1, source_target_pairs={{0,1},{1,0},{2,3},{3,2},{4,5},{5,4},{6,7},{7,6},{8,9},{9,8},{10,11... | collective-permute-start | bytes 688136 | tf_op jit(solution)/shard_map/ppermute | solution.py:561
  2.1 2.6 %collective-permute-start.1 = (f32[336,128]{1,0:T(8,128)S(1)}, f32[336,128]{1,0:T(8,128)S(1)}, u32[]{:S(2)}, u32[]{:S(2)}) collective-permute-start(f32[336,128]{1,0:T(8,128)S(1)} %get-tuple-element.24), channel_id=1, source_target_pairs={{0,2},{2,0},{1,3},{3,1},{4,6},{6,4},{5,7},{7,5},{8,10},{10,8},{9,1... | collective-permute-start | bytes 516104 | tf_op jit(solution)/shard_map/ppermute | solution.py:561
  4.7 0.0 collective-permute-done.other_ref
  4.7 0.1 edges.1
  4.8 1.6 %collective-permute-start.2 = (f32[176,128]{1,0:T(8,128)S(1)}, f32[176,128]{1,0:T(8,128)S(1)}, u32[]{:S(2)}, u32[]{:S(2)}) collective-permute-start(f32[176,128]{1,0:T(8,128)S(1)} %get-tuple-element.25), channel_id=1, source_target_pairs={{0,4},{1,13},{4,0},{5,9},{8,12},{9,5},{12,8},{13,1},{2,6},{3,15},{... | collective-permute-start | bytes 270344 | tf_op jit(solution)/shard_map/ppermute | solution.py:561
  6.4 1.3 %collective-permute-start.3 = (f32[128,128]{1,0:T(8,128)S(1)}, f32[128,128]{1,0:T(8,128)S(1)}, u32[]{:S(2)}, u32[]{:S(2)}) collective-permute-start(f32[128,128]{1,0:T(8,128)S(1)} %get-tuple-element.27), channel_id=1, source_target_pairs={{0,6},{1,15},{2,4},{3,13},{4,2},{5,11},{6,0},{7,9},{8,14},{9,7},{1... | collective-permute-start | bytes 196616 | tf_op jit(solution)/shard_map/ppermute | solution.py:561
  7.7 0.0 copy-start
  7.7 3.2 %tables.1 = (bf16[576,2048]{1,0:T(8,128)(2,1)S(1)}, f32[96,2048]{1,0:T(8,128)S(1)}, s32[36]{0:T(128)S(1)}) custom-call(s32[16,128]{1,0:T(8,128)} %bitcast.18, s32[2,32]{1,0:T(2,128)} %owner_hbm.1, s32[1,4]{1,0:T(1,128)} %wall_owner_hbm.1), custom_call_target="tpu_custom_call" | custom-call | flops 8589934592 | bytes 16777216 | tf_op jit(solution)/shard_map/tables/pallas_call | solution.py:612
  10.9 0.0 collective-permute-done.1
  10.9 1.1 %collective-permute-done.3 = f32[128,128]{1,0:T(8,128)S(1)} collective-permute-done((f32[128,128]{1,0:T(8,128)S(1)}, f32[128,128]{1,0:T(8,128)S(1)}, u32[]{:S(2)}, u32[]{:S(2)}) %collective-permute-start.3) | collective-permute-done | bytes 65568 | tf_op jit(solution)/shard_map/ppermute | solution.py:561
  12.0 0.0 collective-permute-done.2
  12.1 2.2 %collective-permute-start.4 = (f32[640,128]{1,0:T(8,128)S(1)}, f32[640,128]{1,0:T(8,128)S(1)}, u32[]{:S(2)}, u32[]{:S(2)}) collective-permute-start(f32[640,128]{1,0:T(8,128)S(1)} %constant_dynamic-update-slice_fusion.halo_ref), channel_id=1, source_target_pairs={{0,1},{1,0},{2,3},{3,2},{4,5},{5,4},{6,7},{7,6},{8,9},{9,8},{10,11... | collective-permute-start | bytes 983048 | tf_op jit(solution)/shard_map/ppermute | solution.py:561
  14.9 0.6 %collective-permute-done.4.far_halo_ref = f32[640,128]{1,0:T(8,128)S(1)} collective-permute-done((f32[640,128]{1,0:T(8,128)S(1)}, f32[640,128]{1,0:T(8,128)S(1)}, u32[]{:S(2)}, u32[]{:S(2)}) %collective-permute-start.4) | collective-permute-done | bytes 327712 | tf_op jit(solution)/shard_map/ppermute | solution.py:561
  15.5 0.0 copy-done
  15.5 0.0 copy-start.1
  15.5 0.0 copy-start.2
  15.5 3.7 %window.1 = (f32[6,4,16,128]{3,2,1,0:T(8,128)}, f32[12,4,16,128]{3,2,1,0:T(8,128)}, f32[64,128]{1,0:T(8,128)S(1)}, f32[64,128]{1,0:T(8,128)S(1)}) custom-call(f32[448,128]{1,0:T(8,128)S(1)} %bitcast.13, f32[448,128]{1,0:T(8,128)S(1)} %collective-permute-done.other_ref, f32[640,128]{1,0:T(8,128)S(1)} %constant_dynamic-update-slice_fusion.halo_ref, ...), custom_call_target="tpu_custom_call" | custom-call | tf_op jit(solution)/shard_map/window/pallas_call | solution.py:637
  19.2 0.5 %collective-permute-start.5 = (f32[64,128]{1,0:T(8,128)S(1)}, f32[64,128]{1,0:T(8,128)S(1)}, u32[]{:S(2)}, u32[]{:S(2)}) collective-permute-start(f32[64,128]{1,0:T(8,128)S(1)} %get-tuple-element.36), channel_id=1, source_target_pairs={{0,1},{1,0},{2,3},{3,2},{4,5},{5,4},{6,7},{7,6},{8,9},{9,8},{10,11... | collective-permute-start | bytes 98312 | tf_op jit(solution)/shard_map/ppermute | solution.py:561
  19.7 0.9 %collective-permute-done.5 = f32[64,128]{1,0:T(8,128)S(1)} collective-permute-done((f32[64,128]{1,0:T(8,128)S(1)}, f32[64,128]{1,0:T(8,128)S(1)}, u32[]{:S(2)}, u32[]{:S(2)}) %collective-permute-start.5) | collective-permute-done | bytes 32800 | tf_op jit(solution)/shard_map/ppermute | solution.py:561
  20.6 1.4 %collective-permute-start.6 = (f32[64,128]{1,0:T(8,128)S(1)}, f32[64,128]{1,0:T(8,128)S(1)}, u32[]{:S(2)}, u32[]{:S(2)}) collective-permute-start(f32[64,128]{1,0:T(8,128)S(1)} %add.18), channel_id=1, source_target_pairs={{0,2},{2,0},{1,3},{3,1},{4,6},{6,4},{5,7},{7,5},{8,10},{10,8},{9,1... | collective-permute-start | bytes 98312 | tf_op jit(solution)/shard_map/ppermute | solution.py:561
  22.0 2.5 %collective-permute-done.6 = f32[64,128]{1,0:T(8,128)S(1)} collective-permute-done((f32[64,128]{1,0:T(8,128)S(1)}, f32[64,128]{1,0:T(8,128)S(1)}, u32[]{:S(2)}, u32[]{:S(2)}) %collective-permute-start.6) | collective-permute-done | bytes 32800 | tf_op jit(solution)/shard_map/ppermute | solution.py:561
  24.5 2.4 %collective-permute-start.7 = (f32[80,128]{1,0:T(8,128)S(1)}, f32[80,128]{1,0:T(8,128)S(1)}, u32[]{:S(2)}, u32[]{:S(2)}) collective-permute-start(f32[80,128]{1,0:T(8,128)S(1)} %get-tuple-element.48), channel_id=1, source_target_pairs={{0,12},{4,8},{8,4},{12,0},{1,13},{5,9},{9,5},{13,1},{2,14},{6,10},... | collective-permute-start | bytes 122888 | tf_op jit(solution)/shard_map/ppermute | solution.py:561
  26.9 0.0 collective-permute-start.8
  26.9 2.0 %collective-permute-start.9 = (f32[80,128]{1,0:T(8,128)S(1)}, f32[80,128]{1,0:T(8,128)S(1)}, u32[]{:S(2)}, u32[]{:S(2)}) collective-permute-start(f32[80,128]{1,0:T(8,128)S(1)} %get-tuple-element.46), channel_id=1, source_target_pairs={{0,4},{4,0},{8,12},{12,8},{1,5},{5,1},{9,13},{13,9},{2,6},{6,2},{1... | collective-permute-start | bytes 122888 | tf_op jit(solution)/shard_map/ppermute | solution.py:561
  28.9 1.5 %collective-permute-done.7 = f32[80,128]{1,0:T(8,128)S(1)} collective-permute-done((f32[80,128]{1,0:T(8,128)S(1)}, f32[80,128]{1,0:T(8,128)S(1)}, u32[]{:S(2)}, u32[]{:S(2)}) %collective-permute-start.7) | collective-permute-done | bytes 40992 | tf_op jit(solution)/shard_map/ppermute | solution.py:561
  30.5 1.4 %collective-permute-done.8 = f32[80,128]{1,0:T(8,128)S(1)} collective-permute-done((f32[80,128]{1,0:T(8,128)S(1)}, f32[80,128]{1,0:T(8,128)S(1)}, u32[]{:S(2)}, u32[]{:S(2)}) %collective-permute-start.8) | collective-permute-done | bytes 40992 | tf_op jit(solution)/shard_map/ppermute | solution.py:561
  31.8 0.0 collective-permute-done.9
  31.9 0.0 copy-done.1
  31.9 0.0 copy-done.2
  31.9 2.0 %adjoint.1 = (f32[1,128]{1,0:T(1,128)}, f32[20,1,128]{2,1,0:T(1,128)}, f32[36,1,128]{2,1,0:T(1,128)}) custom-call(f32[320,128]{1,0:T(8,128)S(1)} %constant_dynamic-update-slice_fusion.3.far_ref, f32[16,128]{1,0:T(8,128)S(1)} %bitcast.14, s32[16,128]{1,0:T(8,128)S(1)} %bitcast.15, bf16[576,2048]{1,0:T(8,128)(2,1)S(1)} %get-tuple-element.32.hi_lo_ref, ...), custom_call_target="tpu_custom_call" | custom-call | tf_op jit(solution)/shard_map/adjoint/pallas_call | solution.py:673
  (12 shorter events, 0.1 us)
Async XLA Ops:
  1.6 3.1 %collective-permute-start = (f32[448,128]{1,0:T(8,128)S(1)}, f32[448,128]{1,0:T(8,128)S(1)}, u32[]{:S(2)}, u32[]{:S(2)}) collective-permute-start(f32[448,128]{1,0:T(8,128)S(1)} %bitcast.11), channel_id=1, source_target_pairs={{0,1},{1,0},{2,3},{3,2},{4,5},{5,4},{6,7},{7,6},{8,9},{9,8},{10,11... | collective-permute-start | bytes 688136 | tf_op jit(solution)/shard_map/ppermute | solution.py:561
  2.1 8.8 %collective-permute-start.1 = (f32[336,128]{1,0:T(8,128)S(1)}, f32[336,128]{1,0:T(8,128)S(1)}, u32[]{:S(2)}, u32[]{:S(2)}) collective-permute-start(f32[336,128]{1,0:T(8,128)S(1)} %get-tuple-element.24), channel_id=1, source_target_pairs={{0,2},{2,0},{1,3},{3,1},{4,6},{6,4},{5,7},{7,5},{8,10},{10,8},{9,1... | collective-permute-start | bytes 516104 | tf_op jit(solution)/shard_map/ppermute | solution.py:561
  4.8 7.3 %collective-permute-start.2 = (f32[176,128]{1,0:T(8,128)S(1)}, f32[176,128]{1,0:T(8,128)S(1)}, u32[]{:S(2)}, u32[]{:S(2)}) collective-permute-start(f32[176,128]{1,0:T(8,128)S(1)} %get-tuple-element.25), channel_id=1, source_target_pairs={{0,4},{1,13},{4,0},{5,9},{8,12},{9,5},{12,8},{13,1},{2,6},{3,15},{... | collective-permute-start | bytes 270344 | tf_op jit(solution)/shard_map/ppermute | solution.py:561
  6.4 5.6 %collective-permute-start.3 = (f32[128,128]{1,0:T(8,128)S(1)}, f32[128,128]{1,0:T(8,128)S(1)}, u32[]{:S(2)}, u32[]{:S(2)}) collective-permute-start(f32[128,128]{1,0:T(8,128)S(1)} %get-tuple-element.27), channel_id=1, source_target_pairs={{0,6},{1,15},{2,4},{3,13},{4,2},{5,11},{6,0},{7,9},{8,14},{9,7},{1... | collective-permute-start | bytes 196616 | tf_op jit(solution)/shard_map/ppermute | solution.py:561
  7.7 7.8 %copy-start = (f32[12,4,16,128]{3,2,1,0:T(8,128)S(1)}, f32[12,4,16,128]{3,2,1,0:T(8,128)}, u32[]{:S(2)}) copy-start(f32[12,4,16,128]{3,2,1,0:T(8,128)} %spectra_hbm.1) | copy-start | bytes 1179652
  12.1 3.4 %collective-permute-start.4 = (f32[640,128]{1,0:T(8,128)S(1)}, f32[640,128]{1,0:T(8,128)S(1)}, u32[]{:S(2)}, u32[]{:S(2)}) collective-permute-start(f32[640,128]{1,0:T(8,128)S(1)} %constant_dynamic-update-slice_fusion.halo_ref), channel_id=1, source_target_pairs={{0,1},{1,0},{2,3},{3,2},{4,5},{5,4},{6,7},{7,6},{8,9},{9,8},{10,11... | collective-permute-start | bytes 983048 | tf_op jit(solution)/shard_map/ppermute | solution.py:561
  15.5 16.4 %copy-start.1 = (f32[2048]{0:T(1024)S(1)}, f32[2048]{0:T(1024)}, u32[]{:S(2)}) copy-start(f32[2048]{0:T(1024)} %param.16) | copy-start | bytes 24580
  15.5 16.4 %copy-start.2 = (s32[2048]{0:T(1024)S(1)}, s32[2048]{0:T(1024)}, u32[]{:S(2)}) copy-start(s32[2048]{0:T(1024)} %param.17) | copy-start | bytes 24580
  19.2 1.3 %collective-permute-start.5 = (f32[64,128]{1,0:T(8,128)S(1)}, f32[64,128]{1,0:T(8,128)S(1)}, u32[]{:S(2)}, u32[]{:S(2)}) collective-permute-start(f32[64,128]{1,0:T(8,128)S(1)} %get-tuple-element.36), channel_id=1, source_target_pairs={{0,1},{1,0},{2,3},{3,2},{4,5},{5,4},{6,7},{7,6},{8,9},{9,8},{10,11... | collective-permute-start | bytes 98312 | tf_op jit(solution)/shard_map/ppermute | solution.py:561
  20.6 3.9 %collective-permute-start.6 = (f32[64,128]{1,0:T(8,128)S(1)}, f32[64,128]{1,0:T(8,128)S(1)}, u32[]{:S(2)}, u32[]{:S(2)}) collective-permute-start(f32[64,128]{1,0:T(8,128)S(1)} %add.18), channel_id=1, source_target_pairs={{0,2},{2,0},{1,3},{3,1},{4,6},{6,4},{5,7},{7,5},{8,10},{10,8},{9,1... | collective-permute-start | bytes 98312 | tf_op jit(solution)/shard_map/ppermute | solution.py:561
  24.5 6.0 %collective-permute-start.7 = (f32[80,128]{1,0:T(8,128)S(1)}, f32[80,128]{1,0:T(8,128)S(1)}, u32[]{:S(2)}, u32[]{:S(2)}) collective-permute-start(f32[80,128]{1,0:T(8,128)S(1)} %get-tuple-element.48), channel_id=1, source_target_pairs={{0,12},{4,8},{8,4},{12,0},{1,13},{5,9},{9,5},{13,1},{2,14},{6,10},... | collective-permute-start | bytes 122888 | tf_op jit(solution)/shard_map/ppermute | solution.py:561
  26.9 4.9 %collective-permute-start.8 = (f32[80,128]{1,0:T(8,128)S(1)}, f32[80,128]{1,0:T(8,128)S(1)}, u32[]{:S(2)}, u32[]{:S(2)}) collective-permute-start(f32[80,128]{1,0:T(8,128)S(1)} %get-tuple-element.47), channel_id=1, source_target_pairs={{0,8},{4,12},{8,0},{12,4},{1,9},{5,13},{9,1},{13,5},{2,10},{6,14},... | collective-permute-start | bytes 122888 | tf_op jit(solution)/shard_map/ppermute | solution.py:561
  26.9 4.9 %collective-permute-start.9 = (f32[80,128]{1,0:T(8,128)S(1)}, f32[80,128]{1,0:T(8,128)S(1)}, u32[]{:S(2)}, u32[]{:S(2)}) collective-permute-start(f32[80,128]{1,0:T(8,128)S(1)} %get-tuple-element.46), channel_id=1, source_target_pairs={{0,4},{4,0},{8,12},{12,8},{1,5},{5,1},{9,13},{13,9},{2,6},{6,2},{1... | collective-permute-start | bytes 122888 | tf_op jit(solution)/shard_map/ppermute | solution.py:561

commit v8 on v7

--- a/solution.py
+++ b/solution.py
@@ -54,6 +54,13 @@
 def split(values):
     high = values.astype(BF16)
     return high, (values - high.astype(F32)).astype(BF16)
+
+
+def three_products(dot, left, high, rest):
+    left_hi, left_lo = split(left)
+    both = dot(jnp.concatenate([left_hi, left_lo], axis=0), high)
+    rows = left.shape[0]
+    return both[:rows] + (both[rows:] + dot(left_hi, rest))
 
 
 def rows_iota(shape):
@@ -442,9 +449,8 @@
     for first in range(0, n.dirs, wide):
         sums = []
         for left, rows in ((cap, slice(0, 2 * n.x)), (wall, slice(2 * n.x, 2 * n.x + 2 * n.z))):
-            left_hi, left_lo = split(left)
             high, rest = hi_ref[rows, first : first + wide], lo_ref[rows, first : first + wide]
-            sums.append(dot(left_hi, high) + (dot(left_lo, high) + dot(left_hi, rest)))
+            sums.append(three_products(dot, left, high, rest))
         for t in range(wide // LANES):
             lanes = slice(first + t * LANES, first + (t + 1) * LANES)
             tile = first // LANES + t
@@ -509,9 +515,8 @@
     )
     sums = []
     for face, rows in ((0, slice(0, 2 * n.x)), (1, slice(2 * n.x, 2 * n.x + 2 * n.z))):
-        left_hi, left_lo = split(jnp.concatenate(faces[face], axis=1))
-        high, rest = hi_ref[rows, :], lo_ref[rows, :]
-        sums.append(dot(left_hi, high) + (dot(left_lo, high) + dot(left_hi, rest)))
+        left = jnp.concatenate(faces[face], axis=1)
+        sums.append(three_products(dot, left, hi_ref[rows, :], lo_ref[rows, :]))
     cap, wall = sums
     row8, lane = rows_iota((8, LANES)), lanes_iota((8, LANES))
     own_block = lane // PATCH == row8

time: 34.1 us -> 33.5 us (0.982)
  Pallas kernels: 9.94 us -> 9.42 us
where the time goes in v8:
time: 33.5 us; the launch traced here: 33.4 us
  starting transfers between devices  14.5 us (43%)
  Pallas kernels  9.42 us (28%)
  waiting for transfers between devices  7.96 us (24%)
  between operations  1.4 us (4%)
    ppermute x10, starting transfers between devices, exchange(): return lax.ppermute(values, axes if len(axes) > 1 else axes[0], pairs)  14.5 us
    ppermute x10, waiting for transfers between devices, exchange(): return lax.ppermute(values, axes if len(axes) > 1 else axes[0], pairs)  7.96 us
    pallas_call x1, Pallas kernels, local(): pl.pallas_call(functools.partial(main_kernel, n), name='window', out_shap...  3.49 us
    pallas_call x1, Pallas kernels, local(): pl.pallas_call(functools.partial(table_kernel, n), name='tables', out_sha...  3.2 us
    pallas_call x1, Pallas kernels, local(): pl.pallas_call(functools.partial(adjoint_kernel, n), name='adjoint', out_...  1.7 us
    pallas_call x1, Pallas kernels, local(): pl.pallas_call(functools.partial(pack_kernel, n), name='pack', out_shape=...  0.97 us
  transfers between devices with their start and end apart: 10, of which 6 were waited for; matrix products, arithmetic and copies ran while one was open for 0% of the time, Pallas kernels for 10%

profile of v8, /device:TPU:0, one launch (start us, length us, event | category | flops | bytes accessed | tf_op | source)
XLA Modules:
  0.0 33.4 jit_solution(3070524286217901353)
XLA Ops:
  0.6 1.0 %pack.1 = (f32[7,4,16,128]{3,2,1,0:T(8,128)S(1)}, f32[336,128]{1,0:T(8,128)S(1)}) custom-call(f32[6,4,16,128]{3,2,1,0:T(8,128)} %f_hbm.1, f32[4,16,128]{2,1,0:T(8,128)} %eps_hbm.1), custom_call_target="tpu_custom_call" | custom-call | tf_op jit(solution)/shard_map/pack/pallas_call | solution.py:585
  1.6 0.5 %collective-permute-start = (f32[448,128]{1,0:T(8,128)S(1)}, f32[448,128]{1,0:T(8,128)S(1)}, u32[]{:S(2)}, u32[]{:S(2)}) collective-permute-start(f32[448,128]{1,0:T(8,128)S(1)} %bitcast.11), channel_id=1, source_target_pairs={{0,1},{1,0},{2,3},{3,2},{4,5},{5,4},{6,7},{7,6},{8,9},{9,8},{10,11... | collective-permute-start | bytes 688136 | tf_op jit(solution)/shard_map/ppermute | solution.py:566
  2.1 2.6 %collective-permute-start.1 = (f32[336,128]{1,0:T(8,128)S(1)}, f32[336,128]{1,0:T(8,128)S(1)}, u32[]{:S(2)}, u32[]{:S(2)}) collective-permute-start(f32[336,128]{1,0:T(8,128)S(1)} %get-tuple-element.24), channel_id=1, source_target_pairs={{0,2},{2,0},{1,3},{3,1},{4,6},{6,4},{5,7},{7,5},{8,10},{10,8},{9,1... | collective-permute-start | bytes 516104 | tf_op jit(solution)/shard_map/ppermute | solution.py:566
  4.7 0.0 collective-permute-done.other_ref
  4.7 0.1 edges.1
  4.8 1.6 %collective-permute-start.2 = (f32[176,128]{1,0:T(8,128)S(1)}, f32[176,128]{1,0:T(8,128)S(1)}, u32[]{:S(2)}, u32[]{:S(2)}) collective-permute-start(f32[176,128]{1,0:T(8,128)S(1)} %get-tuple-element.25), channel_id=1, source_target_pairs={{0,4},{1,13},{4,0},{5,9},{8,12},{9,5},{12,8},{13,1},{2,6},{3,15},{... | collective-permute-start | bytes 270344 | tf_op jit(solution)/shard_map/ppermute | solution.py:566
  6.4 1.3 %collective-permute-start.3 = (f32[128,128]{1,0:T(8,128)S(1)}, f32[128,128]{1,0:T(8,128)S(1)}, u32[]{:S(2)}, u32[]{:S(2)}) collective-permute-start(f32[128,128]{1,0:T(8,128)S(1)} %get-tuple-element.27), channel_id=1, source_target_pairs={{0,6},{1,15},{2,4},{3,13},{4,2},{5,11},{6,0},{7,9},{8,14},{9,7},{1... | collective-permute-start | bytes 196616 | tf_op jit(solution)/shard_map/ppermute | solution.py:566
  7.7 0.0 copy-start
  7.7 3.2 %tables.1 = (bf16[576,2048]{1,0:T(8,128)(2,1)S(1)}, f32[96,2048]{1,0:T(8,128)S(1)}, s32[36]{0:T(128)S(1)}) custom-call(s32[16,128]{1,0:T(8,128)} %bitcast.18, s32[2,32]{1,0:T(2,128)} %owner_hbm.1, s32[1,4]{1,0:T(1,128)} %wall_owner_hbm.1), custom_call_target="tpu_custom_call" | custom-call | flops 8589934592 | bytes 16777216 | tf_op jit(solution)/shard_map/tables/pallas_call | solution.py:617
  10.9 0.0 collective-permute-done.1
  10.9 1.1 %collective-permute-done.3 = f32[128,128]{1,0:T(8,128)S(1)} collective-permute-done((f32[128,128]{1,0:T(8,128)S(1)}, f32[128,128]{1,0:T(8,128)S(1)}, u32[]{:S(2)}, u32[]{:S(2)}) %collective-permute-start.3) | collective-permute-done | bytes 65568 | tf_op jit(solution)/shard_map/ppermute | solution.py:566
  12.0 0.0 collective-permute-done.2
  12.1 2.2 %collective-permute-start.4 = (f32[640,128]{1,0:T(8,128)S(1)}, f32[640,128]{1,0:T(8,128)S(1)}, u32[]{:S(2)}, u32[]{:S(2)}) collective-permute-start(f32[640,128]{1,0:T(8,128)S(1)} %constant_dynamic-update-slice_fusion.halo_ref), channel_id=1, source_target_pairs={{0,1},{1,0},{2,3},{3,2},{4,5},{5,4},{6,7},{7,6},{8,9},{9,8},{10,11... | collective-permute-start | bytes 983048 | tf_op jit(solution)/shard_map/ppermute | solution.py:566
  14.9 0.6 %collective-permute-done.4.far_halo_ref = f32[640,128]{1,0:T(8,128)S(1)} collective-permute-done((f32[640,128]{1,0:T(8,128)S(1)}, f32[640,128]{1,0:T(8,128)S(1)}, u32[]{:S(2)}, u32[]{:S(2)}) %collective-permute-start.4) | collective-permute-done | bytes 327712 | tf_op jit(solution)/shard_map/ppermute | solution.py:566
  15.5 0.0 copy-done
  15.5 0.0 copy-start.1
  15.5 0.0 copy-start.2
  15.5 3.5 %window.1 = (f32[6,4,16,128]{3,2,1,0:T(8,128)}, f32[12,4,16,128]{3,2,1,0:T(8,128)}, f32[64,128]{1,0:T(8,128)S(1)}, f32[64,128]{1,0:T(8,128)S(1)}) custom-call(f32[448,128]{1,0:T(8,128)S(1)} %bitcast.13, f32[448,128]{1,0:T(8,128)S(1)} %collective-permute-done.other_ref, f32[640,128]{1,0:T(8,128)S(1)} %constant_dynamic-update-slice_fusion.halo_ref, ...), custom_call_target="tpu_custom_call" | custom-call | tf_op jit(solution)/shard_map/window/pallas_call | solution.py:642
  19.0 0.5 %collective-permute-start.5 = (f32[64,128]{1,0:T(8,128)S(1)}, f32[64,128]{1,0:T(8,128)S(1)}, u32[]{:S(2)}, u32[]{:S(2)}) collective-permute-start(f32[64,128]{1,0:T(8,128)S(1)} %get-tuple-element.36), channel_id=1, source_target_pairs={{0,1},{1,0},{2,3},{3,2},{4,5},{5,4},{6,7},{7,6},{8,9},{9,8},{10,11... | collective-permute-start | bytes 98312 | tf_op jit(solution)/shard_map/ppermute | solution.py:566
  19.5 0.9 %collective-permute-done.5 = f32[64,128]{1,0:T(8,128)S(1)} collective-permute-done((f32[64,128]{1,0:T(8,128)S(1)}, f32[64,128]{1,0:T(8,128)S(1)}, u32[]{:S(2)}, u32[]{:S(2)}) %collective-permute-start.5) | collective-permute-done | bytes 32800 | tf_op jit(solution)/shard_map/ppermute | solution.py:566
  20.3 1.4 %collective-permute-start.6 = (f32[64,128]{1,0:T(8,128)S(1)}, f32[64,128]{1,0:T(8,128)S(1)}, u32[]{:S(2)}, u32[]{:S(2)}) collective-permute-start(f32[64,128]{1,0:T(8,128)S(1)} %add.18), channel_id=1, source_target_pairs={{0,2},{2,0},{1,3},{3,1},{4,6},{6,4},{5,7},{7,5},{8,10},{10,8},{9,1... | collective-permute-start | bytes 98312 | tf_op jit(solution)/shard_map/ppermute | solution.py:566
  21.8 2.5 %collective-permute-done.6 = f32[64,128]{1,0:T(8,128)S(1)} collective-permute-done((f32[64,128]{1,0:T(8,128)S(1)}, f32[64,128]{1,0:T(8,128)S(1)}, u32[]{:S(2)}, u32[]{:S(2)}) %collective-permute-start.6) | collective-permute-done | bytes 32800 | tf_op jit(solution)/shard_map/ppermute | solution.py:566
  24.3 2.4 %collective-permute-start.7 = (f32[80,128]{1,0:T(8,128)S(1)}, f32[80,128]{1,0:T(8,128)S(1)}, u32[]{:S(2)}, u32[]{:S(2)}) collective-permute-start(f32[80,128]{1,0:T(8,128)S(1)} %get-tuple-element.48), channel_id=1, source_target_pairs={{0,12},{4,8},{8,4},{12,0},{1,13},{5,9},{9,5},{13,1},{2,14},{6,10},... | collective-permute-start | bytes 122888 | tf_op jit(solution)/shard_map/ppermute | solution.py:566
  26.7 0.0 collective-permute-start.8
  26.7 2.0 %collective-permute-start.9 = (f32[80,128]{1,0:T(8,128)S(1)}, f32[80,128]{1,0:T(8,128)S(1)}, u32[]{:S(2)}, u32[]{:S(2)}) collective-permute-start(f32[80,128]{1,0:T(8,128)S(1)} %get-tuple-element.46), channel_id=1, source_target_pairs={{0,4},{4,0},{8,12},{12,8},{1,5},{5,1},{9,13},{13,9},{2,6},{6,2},{1... | collective-permute-start | bytes 122888 | tf_op jit(solution)/shard_map/ppermute | solution.py:566
  28.7 1.5 %collective-permute-done.7 = f32[80,128]{1,0:T(8,128)S(1)} collective-permute-done((f32[80,128]{1,0:T(8,128)S(1)}, f32[80,128]{1,0:T(8,128)S(1)}, u32[]{:S(2)}, u32[]{:S(2)}) %collective-permute-start.7) | collective-permute-done | bytes 40992 | tf_op jit(solution)/shard_map/ppermute | solution.py:566
  30.2 1.4 %collective-permute-done.8 = f32[80,128]{1,0:T(8,128)S(1)} collective-permute-done((f32[80,128]{1,0:T(8,128)S(1)}, f32[80,128]{1,0:T(8,128)S(1)}, u32[]{:S(2)}, u32[]{:S(2)}) %collective-permute-start.8) | collective-permute-done | bytes 40992 | tf_op jit(solution)/shard_map/ppermute | solution.py:566
  31.6 0.0 collective-permute-done.9
  31.7 0.0 copy-done.1
  31.7 0.0 copy-done.2
  31.7 1.7 %adjoint.1 = (f32[1,128]{1,0:T(1,128)}, f32[20,1,128]{2,1,0:T(1,128)}, f32[36,1,128]{2,1,0:T(1,128)}) custom-call(f32[320,128]{1,0:T(8,128)S(1)} %constant_dynamic-update-slice_fusion.3.far_ref, f32[16,128]{1,0:T(8,128)S(1)} %bitcast.14, s32[16,128]{1,0:T(8,128)S(1)} %bitcast.15, bf16[576,2048]{1,0:T(8,128)(2,1)S(1)} %get-tuple-element.32.hi_lo_ref, ...), custom_call_target="tpu_custom_call" | custom-call | tf_op jit(solution)/shard_map/adjoint/pallas_call | solution.py:678
  (12 shorter events, 0.1 us)
Async XLA Ops:
  1.6 3.1 %collective-permute-start = (f32[448,128]{1,0:T(8,128)S(1)}, f32[448,128]{1,0:T(8,128)S(1)}, u32[]{:S(2)}, u32[]{:S(2)}) collective-permute-start(f32[448,128]{1,0:T(8,128)S(1)} %bitcast.11), channel_id=1, source_target_pairs={{0,1},{1,0},{2,3},{3,2},{4,5},{5,4},{6,7},{7,6},{8,9},{9,8},{10,11... | collective-permute-start | bytes 688136 | tf_op jit(solution)/shard_map/ppermute | solution.py:566
  2.1 8.8 %collective-permute-start.1 = (f32[336,128]{1,0:T(8,128)S(1)}, f32[336,128]{1,0:T(8,128)S(1)}, u32[]{:S(2)}, u32[]{:S(2)}) collective-permute-start(f32[336,128]{1,0:T(8,128)S(1)} %get-tuple-element.24), channel_id=1, source_target_pairs={{0,2},{2,0},{1,3},{3,1},{4,6},{6,4},{5,7},{7,5},{8,10},{10,8},{9,1... | collective-permute-start | bytes 516104 | tf_op jit(solution)/shard_map/ppermute | solution.py:566
  4.8 7.3 %collective-permute-start.2 = (f32[176,128]{1,0:T(8,128)S(1)}, f32[176,128]{1,0:T(8,128)S(1)}, u32[]{:S(2)}, u32[]{:S(2)}) collective-permute-start(f32[176,128]{1,0:T(8,128)S(1)} %get-tuple-element.25), channel_id=1, source_target_pairs={{0,4},{1,13},{4,0},{5,9},{8,12},{9,5},{12,8},{13,1},{2,6},{3,15},{... | collective-permute-start | bytes 270344 | tf_op jit(solution)/shard_map/ppermute | solution.py:566
  6.4 5.6 %collective-permute-start.3 = (f32[128,128]{1,0:T(8,128)S(1)}, f32[128,128]{1,0:T(8,128)S(1)}, u32[]{:S(2)}, u32[]{:S(2)}) collective-permute-start(f32[128,128]{1,0:T(8,128)S(1)} %get-tuple-element.27), channel_id=1, source_target_pairs={{0,6},{1,15},{2,4},{3,13},{4,2},{5,11},{6,0},{7,9},{8,14},{9,7},{1... | collective-permute-start | bytes 196616 | tf_op jit(solution)/shard_map/ppermute | solution.py:566
  7.7 7.8 %copy-start = (f32[12,4,16,128]{3,2,1,0:T(8,128)S(1)}, f32[12,4,16,128]{3,2,1,0:T(8,128)}, u32[]{:S(2)}) copy-start(f32[12,4,16,128]{3,2,1,0:T(8,128)} %spectra_hbm.1) | copy-start | bytes 1179652
  12.1 3.4 %collective-permute-start.4 = (f32[640,128]{1,0:T(8,128)S(1)}, f32[640,128]{1,0:T(8,128)S(1)}, u32[]{:S(2)}, u32[]{:S(2)}) collective-permute-start(f32[640,128]{1,0:T(8,128)S(1)} %constant_dynamic-update-slice_fusion.halo_ref), channel_id=1, source_target_pairs={{0,1},{1,0},{2,3},{3,2},{4,5},{5,4},{6,7},{7,6},{8,9},{9,8},{10,11... | collective-permute-start | bytes 983048 | tf_op jit(solution)/shard_map/ppermute | solution.py:566
  15.5 16.2 %copy-start.1 = (f32[2048]{0:T(1024)S(1)}, f32[2048]{0:T(1024)}, u32[]{:S(2)}) copy-start(f32[2048]{0:T(1024)} %param.16) | copy-start | bytes 24580
  15.5 16.2 %copy-start.2 = (s32[2048]{0:T(1024)S(1)}, s32[2048]{0:T(1024)}, u32[]{:S(2)}) copy-start(s32[2048]{0:T(1024)} %param.17) | copy-start | bytes 24580
  19.0 1.3 %collective-permute-start.5 = (f32[64,128]{1,0:T(8,128)S(1)}, f32[64,128]{1,0:T(8,128)S(1)}, u32[]{:S(2)}, u32[]{:S(2)}) collective-permute-start(f32[64,128]{1,0:T(8,128)S(1)} %get-tuple-element.36), channel_id=1, source_target_pairs={{0,1},{1,0},{2,3},{3,2},{4,5},{5,4},{6,7},{7,6},{8,9},{9,8},{10,11... | collective-permute-start | bytes 98312 | tf_op jit(solution)/shard_map/ppermute | solution.py:566
  20.3 3.9 %collective-permute-start.6 = (f32[64,128]{1,0:T(8,128)S(1)}, f32[64,128]{1,0:T(8,128)S(1)}, u32[]{:S(2)}, u32[]{:S(2)}) collective-permute-start(f32[64,128]{1,0:T(8,128)S(1)} %add.18), channel_id=1, source_target_pairs={{0,2},{2,0},{1,3},{3,1},{4,6},{6,4},{5,7},{7,5},{8,10},{10,8},{9,1... | collective-permute-start | bytes 98312 | tf_op jit(solution)/shard_map/ppermute | solution.py:566
  24.3 6.0 %collective-permute-start.7 = (f32[80,128]{1,0:T(8,128)S(1)}, f32[80,128]{1,0:T(8,128)S(1)}, u32[]{:S(2)}, u32[]{:S(2)}) collective-permute-start(f32[80,128]{1,0:T(8,128)S(1)} %get-tuple-element.48), channel_id=1, source_target_pairs={{0,12},{4,8},{8,4},{12,0},{1,13},{5,9},{9,5},{13,1},{2,14},{6,10},... | collective-permute-start | bytes 122888 | tf_op jit(solution)/shard_map/ppermute | solution.py:566
  26.7 4.9 %collective-permute-start.8 = (f32[80,128]{1,0:T(8,128)S(1)}, f32[80,128]{1,0:T(8,128)S(1)}, u32[]{:S(2)}, u32[]{:S(2)}) collective-permute-start(f32[80,128]{1,0:T(8,128)S(1)} %get-tuple-element.47), channel_id=1, source_target_pairs={{0,8},{4,12},{8,0},{12,4},{1,9},{5,13},{9,1},{13,5},{2,10},{6,14},... | collective-permute-start | bytes 122888 | tf_op jit(solution)/shard_map/ppermute | solution.py:566
  26.7 4.9 %collective-permute-start.9 = (f32[80,128]{1,0:T(8,128)S(1)}, f32[80,128]{1,0:T(8,128)S(1)}, u32[]{:S(2)}, u32[]{:S(2)}) collective-permute-start(f32[80,128]{1,0:T(8,128)S(1)} %get-tuple-element.46), channel_id=1, source_target_pairs={{0,4},{4,0},{8,12},{12,8},{1,5},{5,1},{9,13},{13,9},{2,6},{6,2},{1... | collective-permute-start | bytes 122888 | tf_op jit(solution)/shard_map/ppermute | solution.py:566
